TPU v7x, 32 devices: a whole 2x2x4 slice. The times are simulated.
32 devices in a mesh: gx: 4 (over y, core), gy: 2 (over x), gz: 4 (over z).
Axes of the slice: x: 2, y: 2, z: 4, core: 2. Of those that a mesh axis runs over, the one named last changes fastest.
Arguments:
- charges: float32 [128, 64, 512], P('gx', 'gy', 'gz'), may hold values from -4 to 4
Outputs:
- potential: float32 [128, 64, 512], P('gx', 'gy', 'gz')
All inputs are finite; a program needn't handle non-finite values.
Results may differ from a plain program's by a relative error of at most 0.00014.
Values sent between devices are 32-bit elements; how exact they have to be, the bound alone decides.
No kernel may reach another device: no remote copies, remote signals or barrier semaphores. Data moves between devices by JAX's collectives and lax.ppermute only.
A program may use at most 64 MiB of HBM per device.

v0:
```python
import functools

import jax
import jax.numpy as jnp
import numpy as np
from jax import lax
from jax.experimental import pallas as pl
from jax.experimental.pallas import tpu as pltpu
from jax.sharding import PartitionSpec as P

REACH = 8
STENCIL_SIGMAS = (1.0, 2.0, 3.5)
STENCIL_WEIGHTS = (0.4, 0.1, 0.03)
TOP_SIGMAS = (1.5, 4.0)
TOP_WEIGHTS = (0.03, 0.006)
SPLINE_TAPS = np.array((-1.0, 0.0, 9.0, 16.0, 9.0, 0.0, -1.0)) / 16.0

LOW = (0, -1, -2, -2)
EXTRA = (0, 3, 5, 5)
FACE = 11
LANES = 128
BF = jnp.bfloat16
F32 = jnp.float32


def up(value, unit):
    return -(-value // unit) * unit


def band(rows, cols, sigma, reach):
    distance = cols[None, :] - rows[:, None]
    return np.where(abs(distance) <= reach, np.exp(-((distance / sigma) ** 2)), 0.0)


def restriction(size):
    position = np.arange(size)[None, :] - 2 * np.arange(size // 2)[:, None] + 3
    inside = (position >= 0) & (position <= 6)
    return np.where(inside, SPLINE_TAPS[np.clip(position, 0, 6)], 0.0)


class Axis:
    def __init__(self, count, length):
        self.count, self.length = count, length
        self.width = [(length >> level) + EXTRA[level] for level in range(4)]

    def window(self, level, brick):
        size = self.length >> level
        cells = brick * size + LOW[level] + np.arange(self.width[level])
        return cells, ((cells >= 0) & (cells < self.count * size)).astype(float)

    def partial(self, level, brick):
        matrix = np.eye(self.count * self.length)
        for _ in range(level):
            matrix = restriction(matrix.shape[0]) @ matrix
        cells, inside = self.window(level, brick)
        rows = matrix[np.clip(cells, 0, len(matrix) - 1)] * inside[:, None]
        return rows[:, brick * self.length : (brick + 1) * self.length]

    def prolong(self, level, brick):
        matrix = restriction((self.count * self.length) >> (level - 1)).T
        rows, row_inside = self.window(level - 1, brick)
        cols, col_inside = self.window(level, brick)
        taken = matrix[np.clip(rows, 0, len(matrix) - 1)][:, np.clip(cols, 0, matrix.shape[1] - 1)]
        return taken * row_inside[:, None] * col_inside[None, :]

    def mix(self, level, sigma, target, source):
        rows, row_inside = self.window(level, target)
        cols, col_inside = self.window(level, source)
        reach = REACH if level < 3 else self.count * self.length
        return band(rows, cols, sigma, reach) * row_inside[:, None] * col_inside[None, :]


def place(shape, *pieces):
    whole = np.zeros(shape)
    for row, col, block in pieces:
        whole[row : row + block.shape[0], col : col + block.shape[1]] += block
    return whole


def halves(matrix):
    high = matrix.astype(jnp.bfloat16)
    low = (matrix - high.astype(np.float64)).astype(jnp.bfloat16)
    return high, low


def left3(matrix):
    high, low = halves(matrix)
    return np.concatenate([high, low, high], axis=-1)


def left3t(matrix):
    high, low = halves(matrix)
    return np.concatenate([high, high, low], axis=-1)


def right3(matrix):
    high, low = halves(matrix)
    return np.concatenate([high, high, low], axis=-2)


def split(value):
    high = value.astype(BF)
    return high, (value - high.astype(F32)).astype(BF)


def dot(left, right, dims=((1,), (0,))):
    return lax.dot_general(left, right, (dims, ((), ())), preferred_element_type=F32)


class Plan:
    def __init__(self, counts, lengths):
        self.x, self.y, self.z = (Axis(n, length) for n, length in zip(counts, lengths))
        x, y, z = self.x, self.y, self.z
        assert x.count >= 3 and z.count >= 3
        self.lane = [0, 0, z.width[1], z.width[1] + z.width[2]]
        self.lane_end = self.lane[3] + z.width[3]
        assert self.lane_end <= LANES and z.length == LANES
        self.rows1, self.rows2, self.rows3 = up(y.width[1], 8), up(y.width[2], 16), up(y.width[3], 16)
        assert self.rows2 <= 16 and self.rows3 <= 16 and FACE <= 14 and self.rows1 == 24
        self.row = [0, 0, self.rows1, self.rows1 + self.rows2]
        self.row_face = self.rows1 + self.rows2 + self.rows3
        self.kinds = 1 if y.count == 2 else 2
        self.rows_restricted = self.row_face + 16 * self.kinds
        self.overlay = y.count == 2 and y.width[1] + 3 <= self.rows1
        self.coarse_rows = up(24 + 16 * (y.count - 1), 16) if not self.overlay else 32
        self.fine_halos = 1 if y.count == 2 else 2
        self.fine_rows = y.length + 8 * self.fine_halos
        self.planes = max(FACE, x.width[2], x.width[3])
        assert self.planes <= x.width[1]
        self.group = [0, 0, 3 * self.rows1, 3 * self.rows1 + 3 * self.rows2]
        self.rows_mixed = self.group[3] + 2 * self.rows3
        self.tall = [0, up(z.width[1], 8), up(z.width[2], 8), up(z.width[3], 8)]
        assert self.tall[1] - 16 == z.width[1] - FACE and self.tall[2] - 16 == z.width[2] - 13
        self.flat = [0, x.width[1] * self.rows1, x.width[2] * self.rows2, x.width[3] * self.rows3]
        assert self.flat[1] <= 512 and self.flat[2] <= 256 and self.flat[3] <= 256

    def face_kind(self, axis, offset, source):
        if axis.count == 2:
            return 1 - source
        return 1 if offset == 1 else 0

    def face_row(self, j):
        return j if j < 8 or not self.overlay else j + 3

    def restrict_z(self):
        z = self.z
        return np.stack(
            [
                right3(place((z.length, LANES), *[(0, self.lane[l], z.partial(l, b).T) for l in (1, 2, 3)]))
                for b in range(z.count)
            ]
        )

    def restrict_y(self):
        y, tables = self.y, []
        for b in range(y.count):
            pieces = [(self.row[l], 0, y.partial(l, b)) for l in (1, 2, 3)]
            first = y.partial(1, b)
            for k in range(self.kinds):
                kind = self.face_kind(y, 1, b) if self.kinds == 1 else 1 - k
                start = (y.width[1] - FACE) * kind
                for j in range(FACE):
                    pieces.append((self.row_face + 16 * k + self.face_row(j), 0, first[start + j][None]))
            tables.append(left3(place((self.rows_restricted, y.length), *pieces)))
        return np.stack(tables)

    def fine_y(self):
        y, tables = self.y, []
        for b in range(y.count):
            pieces = []
            for s, sigma in enumerate(STENCIL_SIGMAS):
                row = s * y.length
                pieces.append((row, 0, y.mix(0, sigma, b, b)))
                for h in range(self.fine_halos):
                    offset = 1 if h == 0 else y.count - 1
                    source = (b - offset) % y.count
                    start = (y.length - REACH) * self.face_kind(y, offset, source)
                    block = y.mix(0, sigma, b, source)[:, start : start + REACH]
                    pieces.append((row, y.length + 8 * h, block))
            tables.append(left3(place((3 * y.length, up(self.fine_rows, 16)), *pieces)))
        return np.stack(tables)

    def coarse_y(self):
        y, tables = self.y, []
        for b in range(y.count):
            whole = np.zeros((self.rows_mixed, self.coarse_rows))
            for level in (1, 2, 3):
                sigmas = STENCIL_SIGMAS if level < 3 else TOP_SIGMAS
                rows = (0, self.rows1, self.rows2, self.rows3)[level]
                for s, sigma in enumerate(sigmas):
                    top = self.group[level] + s * rows
                    for offset in range(y.count):
                        source = (b - offset) % y.count
                        block = y.mix(level, sigma, b, source)
                        if level == 1 and offset:
                            start = (y.width[1] - FACE) * self.face_kind(y, offset, source)
                            block = block[:, start : start + FACE]
                        for j in range(block.shape[1]):
                            slot = self.face_row(j) if level == 1 and offset else j
                            if self.overlay and offset:
                                slot = 24 + slot if slot < 8 else 8 + slot
                            elif offset:
                                slot = 24 + 16 * (offset - 1) + slot
                            whole[top : top + y.width[level], slot] += block[:, j]
            tables.append(left3(whole))
        return np.stack(tables)

    def top_x(self):
        x = self.x
        return np.stack(
            [
                np.stack(
                    [
                        np.stack([x.mix(3, sigma, b, (b - r) % x.count) for r in range(x.count)], axis=1)
                        for sigma in TOP_SIGMAS
                    ]
                ).reshape(-1)
                for b in range(x.count)
            ]
        ).astype(np.float32)

    def fine_z(self):
        z, own, pushed = self.z, [], []
        for b in range(z.count):
            mixes = lambda target: [
                w * z.mix(0, sigma, target, b) for sigma, w in zip(STENCIL_SIGMAS, STENCIL_WEIGHTS)
            ]
            own.append(right3(np.concatenate([m.T for m in mixes(b)], axis=0)))
            rows = [np.concatenate([m[:8] for m in mixes((b + 1) % z.count)], axis=1)]
            rows.append(np.concatenate([m[-8:] for m in mixes((b - 1) % z.count)], axis=1))
            pushed.append(left3t(np.concatenate(rows, axis=0)))
        return np.stack(own), np.stack(pushed)

    def coarse_z(self, level):
        z, tables = self.z, []
        sigmas, weights = (STENCIL_SIGMAS, STENCIL_WEIGHTS) if level < 3 else (TOP_SIGMAS, TOP_WEIGHTS)
        factor = 0.5**level if level < 3 else 1.0
        for b in range(z.count):

            def mixed(target):
                blocks = [
                    place((z.width[level], LANES), (0, self.lane[level], factor * w * z.mix(level, sigma, target, b)))
                    for sigma, w in zip(sigmas, weights)
                ]
                return np.concatenate(blocks, axis=1)

            cols = LANES * len(sigmas)
            tall = self.tall[level]
            pieces = [place((tall, cols), (0, 0, mixed(b)))]
            for offset in range(1, z.count):
                block = mixed((b + offset) % z.count)
                near = offset in (1, z.count - 1)
                if level < 3 and near:
                    layers = FACE if level == 1 else 13
                    block = block[:layers] if offset == 1 else block[-layers:]
                    pieces.append(place((16, cols), (0, 0, block)))
                elif level == 3 and near:
                    pieces.append(block[:16])
                    pieces.append(place((16, cols), (FACE, 0, block[16:])))
                elif level == 3:
                    pieces.append(place((tall, cols), (0, 0, block)))
            tables.append(left3t(np.concatenate(pieces, axis=0)))
        return np.stack(tables)

    def finish(self):
        x, y, z = self.x, self.y, self.z
        rows = (y.length, self.rows1, self.rows2, self.rows3)
        exact = lambda m: np.asarray(m, dtype=jnp.bfloat16)

        def free(axis, level):
            inner = Axis(5, axis.length)
            return inner.prolong(level, 2)

        flat = []
        for level in (3, 2, 1):
            q = place((rows[level], rows[level - 1]), (0, 0, free(y, level).T))
            flat.append(exact(np.kron(free(x, level).T, q))[None])
        masks = []
        for level in (2, 1):
            table = np.zeros((x.count * y.count, 1, self.flat[level]), np.float32)
            for bx in range(x.count):
                for by in range(y.count):
                    inside = np.zeros(rows[level])
                    inside[: y.width[level]] = y.window(level, by)[1]
                    table[bx * y.count + by, 0] = np.kron(x.window(level, bx)[1], inside)
            masks.append(table)
        tall = []
        for level in (3, 2):
            tall.append(
                np.stack(
                    [place((self.tall[level - 1], self.tall[level]), (0, 0, z.prolong(level, b))) for b in range(z.count)]
                )
            )
        pieces = [(0, 0, free(z, 1).T), (self.tall[1], 0, np.eye(8)), (self.tall[1] + 8, z.length - 8, np.eye(8))]
        last = place((up(self.tall[1] + 16, 16), z.length), *pieces)
        return flat, masks, [exact(m) for m in tall], exact(last)[None]


def restrict_kernel(plan, place_ref, q_ref, z_ref, y_ref, own_ref, *rest):
    faces, mixed = rest[: plan.kinds], rest[plan.kinds]
    nx, ny, nz = plan.x.length, plan.y.length, plan.z.length
    high, low = split(q_ref[...].reshape(nx * ny, nz))
    along_z = dot(jnp.concatenate([high, low, high], axis=1), z_ref[0])
    high, low = split(along_z)
    high, low = high.reshape(nx, ny, LANES), low.reshape(nx, ny, LANES)
    for i in range(0, nx, 2):
        pair = [jnp.concatenate([high[j], high[j], low[j]], axis=0) for j in (i, i + 1)]
        both = dot(y_ref[0], jnp.concatenate(pair, axis=1))
        mixed[i] = both[:, :LANES]
        mixed[i + 1] = both[:, LANES:]

    brick = place_ref[0]
    keep_low = jnp.where(brick > 0, 1.0, 0.0).astype(F32)
    keep_high = jnp.where(brick < plan.x.count - 1, 1.0, 0.0).astype(F32)

    def coarsen(planes, level):
        size = nx >> level
        result = {}
        for i in range(LOW[level], LOW[level] + plan.x.width[level]):
            get = lambda j: planes.get(2 * i + j)
            total = None
            for offsets, weight in (((-3, 3), -0.0625), ((-1, 1), 0.5625), ((0,), 1.0)):
                terms = [get(j) for j in offsets if get(j) is not None]
                if terms:
                    term = functools.reduce(jnp.add, terms)
                    term = term * weight if weight != 1.0 else term
                    total = term if total is None else total + term
            if i < 0:
                total = total * keep_low
            elif i >= size:
                total = total * keep_high
            result[i] = total
        return result

    lanes = lax.broadcasted_iota(jnp.int32, (8, LANES), 1)
    in1, in2 = lanes < plan.lane[2], lanes < plan.lane[3]

    def tile(planes, level, k, row):
        index = LOW[level] + k
        return planes[row][index] if k < plan.x.width[level] else None

    def rows_of(start, count, depth):
        levels = [{i: mixed[i, start : start + count, :] for i in range(nx)}]
        for level in range(1, depth + 1):
            levels.append(coarsen(levels[-1], level))
        return levels[-1]

    zero = jnp.zeros((8, LANES), F32)
    first = {r: rows_of(r, 8, 1) for r in range(0, plan.rows1, 8)}
    second = {r: rows_of(plan.row[2] + r, 8, 2) for r in (0, 8)}
    third = {r: rows_of(plan.row[3] + r, 8, 3) for r in (0, 8)}
    face = [{r: rows_of(plan.row_face + 16 * f + r, 8, 1) for r in (0, 8)} for f in range(plan.kinds)]
    for k in range(plan.x.width[1]):
        for r in range(0, plan.rows1, 8):
            one = first[r][LOW[1] + k]
            two = second[r][LOW[2] + k] if r < 16 and k < plan.x.width[2] else zero
            three = third[r][LOW[3] + k] if r < 16 and k < plan.x.width[3] else zero
            rest_ = jnp.where(in2, two, three)
            own_ref[k, r : r + 8, :] = jnp.where(in1, one, rest_)
            if r < 16:
                for f in range(plan.kinds):
                    faces[f][k, r : r + 8, :] = jnp.where(in1, face[f][r][LOW[1] + k], rest_)


def extend_kernel(plan, own_ref, *refs):
    count = plan.y.count - 1
    halos, (ext_ref, high_ref, low_ref) = refs[:count], refs[count:]
    lanes = lax.broadcasted_iota(jnp.int32, (1, 1, LANES), 2)
    own = own_ref[...]
    if plan.overlay:
        halo = halos[0][...]
        ext = jnp.concatenate([own[:, :16], own[:, 16:24] + halo[:, 8:], halo[:, :8]], axis=1)
    else:
        parts = [own] + [h[...] for h in halos]
        pad = plan.coarse_rows - 24 - 16 * count
        if pad:
            parts.append(jnp.zeros((own.shape[0], pad, LANES), F32))
        ext = jnp.concatenate(parts, axis=1)
    ext_ref[...] = ext
    low_ref[...] = ext[: plan.planes]
    start = plan.x.width[1] - FACE
    for p in range(plan.planes):
        first = ext[start + min(p, FACE - 1)]
        high_ref[p] = jnp.where(lanes[0] < plan.lane[2], first, ext[p])


def mix_planes(get, put, count, matrix, rows):
    for i in range(0, count, 2):
        pair = [i, min(i + 1, count - 1)]
        stacked = []
        for j in pair:
            high, low = split(get(j))
            stacked.append(jnp.concatenate([high, high, low], axis=0))
        both = dot(matrix, jnp.concatenate(stacked, axis=1))
        put(i, both[:, :LANES])
        if pair[1] != i:
            put(pair[1], both[:, LANES:])


def stencil(planes, start, count, sigma):
    weights = [float(np.exp(-((k / sigma) ** 2))) for k in range(REACH + 1)]
    result = []
    for i in range(start, start + count):
        total = planes[i]
        for k in range(1, REACH + 1):
            total = total + (planes[i - k] + planes[i + k]) * weights[k]
        result.append(total)
    return result


def mix_kernel(plan, place_ref, q_ref, *refs):
    x, y, z = plan.x, plan.y, plan.z
    refs = list(refs)
    take = lambda n: [refs.pop(0) for _ in range(n)]
    halos = take(plan.fine_halos)
    before_ref, after_ref, ext_ref = take(3)
    coarse = take(x.count - 1)
    fine_y, coarse_y, top_x, fine_own, fine_push, z1, z2, z3 = take(8)
    main_ref, near_next, near_prev = take(3)
    far = take(z.count - 3)
    e1_ref, e2_ref, e3_ref = take(3)
    fine_mixed, fine_ready, coarse_mixed, ready1, ready2, ready3 = take(6)

    brick = place_ref[0]
    mask = lambda condition: jnp.where(condition, 1.0, 0.0).astype(F32)
    keep_before, keep_after = mask(brick > 0), mask(brick < x.count - 1)

    pad = up(plan.fine_rows, 16) - plan.fine_rows
    padding = [jnp.zeros((pad, LANES), F32)] if pad else []

    def fine_plane(i):
        if i < REACH:
            return jnp.concatenate([before_ref[i] * keep_before] + padding, axis=0)
        if i < REACH + x.length:
            j = i - REACH
            return jnp.concatenate([q_ref[j]] + [h[j] for h in halos] + padding, axis=0)
        return jnp.concatenate([after_ref[i - REACH - x.length] * keep_after] + padding, axis=0)

    def fine_put(i, value):
        fine_mixed[i] = value

    mix_planes(fine_plane, fine_put, x.length + 2 * REACH, fine_y[0], None)

    def put_ready(ready, sigmas, s, row, value):
        high, low = split(value)
        rows = slice(row, row + value.shape[0])
        step = LANES * sigmas
        ready[rows, s * LANES : (s + 1) * LANES] = high
        ready[rows, step + s * LANES : step + (s + 1) * LANES] = low
        ready[rows, 2 * step + s * LANES : 2 * step + (s + 1) * LANES] = high

    for s, sigma in enumerate(STENCIL_SIGMAS):
        for r in range(0, y.length, 16):
            row = s * y.length + r
            planes = [fine_mixed[i, row : row + 16, :] for i in range(x.length + 2 * REACH)]
            for i, value in enumerate(stencil(planes, REACH, x.length, sigma)):
                put_ready(fine_ready, 3, s, i * y.length + r, value)

    own_planes = x.width[1]

    def coarse_plane(i):
        if i < own_planes:
            return ext_ref[i]
        return coarse[(i - own_planes) // plan.planes][(i - own_planes) % plan.planes]

    def coarse_put(i, value):
        coarse_mixed[i] = value

    mix_planes(coarse_plane, coarse_put, own_planes + plan.planes * (x.count - 1), coarse_y[0], None)

    for level, ready in ((1, ready1), (2, ready2)):
        size = x.length >> level
        rows = plan.rows1 if level == 1 else plan.rows2
        width = x.width[level]
        for s, sigma in enumerate(STENCIL_SIGMAS):
            for r in range(0, rows, 8):
                row = plan.group[level] + s * rows + r
                at = lambda i: coarse_mixed[i, row : row + 8, :]
                cells = {LOW[level] + k: at(k) for k in range(width)}
                for offset in range(1, x.count):
                    base = own_planes + plan.planes * (offset - 1)
                    for shift, here in ((-offset, brick >= offset), (x.count - offset, brick < offset)):
                        kind = plan.face_kind(x, offset, 0)
                        if abs(shift) > level:
                            continue
                        first = (width - FACE) * kind if level == 1 else 0
                        layers = FACE if level == 1 else width
                        keep = mask(here)
                        for k in range(layers):
                            cell = shift * size + LOW[level] + first + k
                            if LOW[level] - REACH <= cell < LOW[level] + width + REACH:
                                value = at(base + k) * keep
                                cells[cell] = cells[cell] + value if cell in cells else value
                planes = [cells[LOW[level] - REACH + k] for k in range(width + 2 * REACH)]
                for i, value in enumerate(stencil(planes, REACH, width, sigma)):
                    put_ready(ready, 3, s, i * rows + r, value)

    width = x.width[3]
    for s in range(len(TOP_SIGMAS)):
        row = plan.group[3] + s * plan.rows3
        totals = [None] * width
        for offset in range(x.count):
            base = 0 if offset == 0 else own_planes + plan.planes * (offset - 1)
            for k in range(width):
                value = coarse_mixed[base + k, row : row + plan.rows3, :]
                for i in range(width):
                    weight = top_x[brick, ((s * width + i) * x.count + offset) * width + k]
                    term = value * weight
                    totals[i] = term if totals[i] is None else totals[i] + term
        for i in range(width):
            put_ready(ready3, 2, s, i * plan.rows3, totals[i])

    pushed = dot(fine_push[0], fine_ready[...], ((1,), (1,)))
    near = (near_next, near_prev)
    for n, ref in enumerate(near):
        ref[8:24, :] = jnp.zeros((16, ref.shape[1]), F32)
        ref[:8, :] = pushed[8 * n : 8 * n + 8]
    one = dot(z1[0], ready1[...], ((1,), (1,)))
    two = dot(z2[0], ready2[...], ((1,), (1,)))
    three = dot(z3[0], ready3[...], ((1,), (1,)))
    e1_ref[...] = one[: plan.tall[1]]
    e2_ref[...] = two[: plan.tall[2]]
    e3_ref[...] = three[: plan.tall[3]]
    top = plan.tall[3]
    far_index = 0
    for offset in range(1, z.count):
        if offset in (1, z.count - 1):
            n = 0 if offset == 1 else 1
            ref = near[n]
            start = plan.tall[1] + 16 * n
            ref[8:24, : plan.flat[1]] = one[start : start + 16]
            ref[8:24, : plan.flat[3]] += three[top + 16 : top + 32]
            start = plan.tall[2] + 16 * n
            ref[8:24, 512 : 512 + plan.flat[2]] = two[start : start + 16]
            ref[8:24, 768 : 768 + plan.flat[3]] = three[top : top + 16]
            top += 32
        else:
            far[far_index][...] = three[top : top + plan.tall[3]]
            far_index += 1
            top += plan.tall[3]
    main_ref[...] = dot(fine_ready[...], fine_own[0])


def finish_kernel(plan, place_ref, main_ref, e1_ref, e2_ref, e3_ref, prev_ref, next_ref, *refs):
    z = plan.z
    refs = list(refs)
    far = [refs.pop(0) for _ in range(z.count - 3)]
    flat3, flat2, flat1, mask2, mask1, tall3, tall2, last, out_ref, e1, e2, e3 = refs
    e1[...], e2[...], e3[...] = e1_ref[...], e2_ref[...], e3_ref[...]
    for f in far:
        e3[...] += f[...]
    for n, ref in enumerate((prev_ref, next_ref)):
        e3[:16, :] += ref[8:24, 768 : 768 + plan.flat[3]]
        e3[16 : z.width[3], :] += ref[8 + FACE : 8 + FACE + z.width[3] - 16, : plan.flat[3]]
        start = 0 if n == 0 else plan.tall[2] - 16
        e2[start : start + 16, :] += ref[8:24, 512 : 512 + plan.flat[2]]
        start = 0 if n == 0 else z.width[1] - FACE
        e1[start : start + FACE, :] += ref[8 : 8 + FACE, : plan.flat[1]]

    def across(value, matrix):
        high, low = split(value)
        both = dot(jnp.concatenate([high, low], axis=0), matrix)
        return both[: value.shape[0]] + both[value.shape[0] :]

    def along(matrix, value):
        high, low = split(value)
        return dot(matrix, high) + dot(matrix, low)

    two = (e2[...] + along(tall3[0], across(e3[...], flat3[0]))) * mask2[0]
    one = (e1[...] + along(tall2[0], across(two, flat2[0]))) * mask1[0]
    spread = across(one, flat1[0])
    rows = jnp.concatenate([spread, prev_ref[:8, :], next_ref[:8, :]], axis=0)
    pad = last.shape[1] - rows.shape[0]
    if pad:
        rows = jnp.concatenate([rows, jnp.zeros((pad, rows.shape[1]), F32)], axis=0)
    high, low = split(rows)
    stacked = jnp.concatenate([high, low], axis=0)
    matrix = jnp.concatenate([last[0], last[0]], axis=0)
    out_ref[...] = main_ref[...] + dot(stacked, matrix, ((0,), (0,)))


def call(kernel, plan, place_at, operands, tables, outs, scratch=(), smem=()):
    whole = lambda a: pl.BlockSpec(a.shape, lambda i, at, n=a.ndim: (0,) * n)
    specs = [whole(a) for a in operands]
    arrays = list(operands)
    for table, index in tables:
        arrays.append(jnp.asarray(table))
        if index is None:
            specs.append(pl.BlockSpec(memory_space=pltpu.SMEM))
        elif index < 0:
            specs.append(whole(table))
        else:
            specs.append(
                pl.BlockSpec((1,) + table.shape[1:], lambda i, at, k=index, n=table.ndim: (at[k],) + (0,) * (n - 1))
            )
    return pl.pallas_call(
        functools.partial(kernel, plan),
        grid_spec=pltpu.PrefetchScalarGridSpec(
            num_scalar_prefetch=1,
            grid=(1,),
            in_specs=specs,
            out_specs=[whole(o) for o in outs],
            scratch_shapes=list(scratch),
        ),
        out_shape=list(outs),
        compiler_params=pltpu.CompilerParams(vmem_limit_bytes=48 * 2**20),
    )(place_at, *arrays)


def shift(value, axis, offset):
    count = lax.axis_size(axis)
    return lax.ppermute(value, axis, [(i, (i + offset) % count) for i in range(count)])


def shards(plan, charges):
    x, y, z = plan.x, plan.y, plan.z
    array = lambda *shape: jax.ShapeDtypeStruct(shape, F32)
    at = [lax.axis_index(name) for name in ("gx", "gy", "gz")]
    place_at = jnp.stack(at + [at[0] * y.count + at[1]]).astype(jnp.int32)

    faces = charges[:, : REACH], charges[:, y.length - REACH :]
    if y.count == 2:
        fine_y = [shift(jnp.where(at[1] == 0, faces[1], faces[0]), "gy", 1)]
    else:
        fine_y = [shift(faces[1], "gy", 1), shift(faces[0], "gy", y.count - 1)]
    own, *coarse_faces = call(
        restrict_kernel,
        plan,
        place_at,
        [charges],
        [(plan.restrict_z(), 2), (plan.restrict_y(), 1)],
        [array(x.width[1], plan.rows1, LANES)] + [array(x.width[1], 16, LANES)] * plan.kinds,
        [pltpu.VMEM((x.length, plan.rows_restricted, LANES), F32)],
    )
    coarse_halos = [shift(coarse_faces[0 if r == 1 else -1], "gy", r) for r in range(1, y.count)]

    fine_x = [
        shift(jnp.concatenate([charges[-REACH:]] + [f[-REACH:] for f in fine_y], axis=1), "gx", 1),
        shift(jnp.concatenate([charges[:REACH]] + [f[:REACH] for f in fine_y], axis=1), "gx", x.count - 1),
    ]
    extended = [array(n, plan.coarse_rows, LANES) for n in (x.width[1], plan.planes, plan.planes)]
    ext, high, low = pl.pallas_call(functools.partial(extend_kernel, plan), out_shape=extended)(own, *coarse_halos)
    coarse_x = [shift(high if r == 1 else low, "gx", r) for r in range(1, x.count)]

    fine_own, fine_push = plan.fine_z()
    zs = [plan.coarse_z(level) for level in (1, 2, 3)]
    cells = x.length * y.length
    ready = lambda rows, sigmas: pltpu.VMEM((rows, 3 * sigmas * LANES), BF)
    results = call(
        mix_kernel,
        plan,
        place_at,
        [charges] + fine_y + fine_x + [ext] + coarse_x,
        [
            (plan.fine_y(), 1),
            (plan.coarse_y(), 1),
            (plan.top_x(), None),
            (fine_own, 2),
            (fine_push, 2),
            (zs[0], 2),
            (zs[1], 2),
            (zs[2], 2),
        ],
        [array(cells, LANES), array(24, cells), array(24, cells)]
        + [array(plan.tall[3], plan.flat[3])] * (z.count - 3)
        + [array(plan.tall[l], plan.flat[l]) for l in (1, 2, 3)],
        [
            pltpu.VMEM((x.length + 2 * REACH, 3 * y.length, LANES), F32),
            ready(cells, 3),
            pltpu.VMEM((x.width[1] + plan.planes * (x.count - 1), plan.rows_mixed, LANES), F32),
            ready(plan.flat[1], 3),
            ready(plan.flat[2], 3),
            ready(plan.flat[3], 2),
        ],
    )
    main, near_next, near_prev = results[:3]
    far, windows = results[3 : z.count], results[z.count :]
    from_prev = shift(near_next, "gz", 1)
    from_next = shift(near_prev, "gz", z.count - 1)
    from_far = [shift(f, "gz", r) for f, r in zip(far, range(2, z.count - 1))]
    flat, masks, tall, last = plan.finish()
    (potential,) = call(
        finish_kernel,
        plan,
        place_at,
        [main, *windows, from_prev, from_next, *from_far],
        [(m, -1) for m in flat] + [(m, 3) for m in masks] + [(m, 2) for m in tall] + [(last, -1)],
        [array(cells, LANES)],
        [pltpu.VMEM((plan.tall[l], plan.flat[l]), F32) for l in (1, 2, 3)],
    )
    return potential.reshape(charges.shape)


def solution(mesh):
    counts = [mesh.shape[name] for name in ("gx", "gy", "gz")]

    def run(charges):
        plan = Plan(counts, [size // n for size, n in zip(charges.shape, counts)])
        placed = P("gx", "gy", "gz")
        return jax.shard_map(
            functools.partial(shards, plan), mesh=mesh, in_specs=(placed,), out_specs=placed, check_vma=False
        )(charges)

    return run
```

profile of v0, /device:TPU:0, one launch (start us, length us, event | category | flops | bytes accessed | tf_op | source)
XLA Modules:
  0.0 51.1 jit_solution(9843993557967657951)
XLA Ops:
  0.0 1.0 %slice_select_fusion = f32[32,8,128]{2,1,0:T(8,128)S(1)} fusion(f32[32,32,128]{2,1,0:T(8,128)} %q_ref.3, pred[]{:T(512)S(6)} %eq.3), kind=kLoop, calls=%fused_computation.2 | loop fusion | flops 32768 | bytes 393217 | tf_op jit(solution)/shard_map/jit(_where)/select_n | solution.py:623
  1.0 3.0 %collective-permute-start = (f32[32,8,128]{2,1,0:T(8,128)S(1)}, f32[32,8,128]{2,1,0:T(8,128)S(1)}, u32[]{:S(2)}, u32[]{:S(2)}) collective-permute-start(f32[32,8,128]{2,1,0:T(8,128)S(1)} %slice_select_fusion), channel_id=1, source_target_pairs={{0,4},{4,0},{1,5},{5,1},{2,6},{6,2},{3,7},{7,3},{8,12},{12,8},{9,1... | collective-permute-start | bytes 393224 | tf_op jit(solution)/shard_map/ppermute | solution.py:612
  4.1 1.0 %copy-done = f32[32,32,128]{2,1,0:T(8,128)S(1)} copy-done((f32[32,32,128]{2,1,0:T(8,128)S(1)}, f32[32,32,128]{2,1,0:T(8,128)}, u32[]{:S(2)}) %copy-start) | copy-done | bytes 524312
  5.1 1.0 %copy-done.6 = bf16[4,384,128]{2,1,0:T(8,128)(2,1)S(1)} copy-done((bf16[4,384,128]{2,1,0:T(8,128)(2,1)S(1)}, bf16[4,384,128]{2,1,0:T(8,128)(2,1)}, u32[]{:S(2)}) %copy-start.6) | copy-done | bytes 393240
  6.1 0.8 %copy-done.16 = bf16[2,72,96]{2,1,0:T(8,128)(2,1)S(1)} copy-done((bf16[2,72,96]{2,1,0:T(8,128)(2,1)S(1)}, bf16[2,72,96]{2,1,0:T(8,128)(2,1)}, u32[]{:S(2)}) %copy-start.16) | copy-done | bytes 27672
  6.9 1.2 %shard_map.181 = (f32[19,24,128]{2,1,0:T(8,128)S(1)}, f32[19,16,128]{2,1,0:T(8,128)S(1)}) custom-call(s32[4]{0:T(128)S(1)} %pad_add_fusion.place_ref, f32[32,32,128]{2,1,0:T(8,128)S(1)} %copy-done, bf16[4,384,128]{2,1,0:T(8,128)(2,1)S(1)} %copy-done.6, bf16[2,72,96]{2,1,0:T(8,128)(2,1)S(1)} %copy-done.16), custom_call_target="tpu_custom_call" | custom-call | tf_op jit(solution)/shard_map/pallas_call | solution.py:596
  8.1 0.1 collective-permute-start.3
  8.2 0.6 %copy-done.8 = f32[19,24,128]{2,1,0:T(8,128)} copy-done((f32[19,24,128]{2,1,0:T(8,128)}, f32[19,24,128]{2,1,0:T(8,128)S(1)}, u32[]{:S(2)}) %copy-start.8) | copy-done | bytes 233496
  8.9 4.8 %collective-permute-done.3.refs_0_ = f32[19,16,128]{2,1,0:T(8,128)S(1)} collective-permute-done((f32[19,16,128]{2,1,0:T(8,128)S(1)}, f32[19,16,128]{2,1,0:T(8,128)S(1)}, u32[]{:S(2)}, u32[]{:S(2)}) %collective-permute-start.3) | collective-permute-done | bytes 155680 | tf_op jit(solution)/shard_map/ppermute | solution.py:612
  13.6 0.7 %copy-done.21 = f32[19,16,128]{2,1,0:T(8,128)} copy-done((f32[19,16,128]{2,1,0:T(8,128)}, f32[19,16,128]{2,1,0:T(8,128)S(1)}, u32[]{:S(2)}) %copy-start.21) | copy-done | bytes 155672
  14.3 1.9 %shard_map.182 = (f32[19,32,128]{2,1,0:T(8,128)}, f32[13,32,128]{2,1,0:T(8,128)}, f32[13,32,128]{2,1,0:T(8,128)}) custom-call(f32[19,24,128]{2,1,0:T(8,128)} %copy-done.8, f32[19,16,128]{2,1,0:T(8,128)} %copy-done.21), custom_call_target="tpu_custom_call" | custom-call | tf_op jit(solution)/shard_map/pallas_call | solution.py:642
  16.2 1.5 %collective-permute-start.5 = (f32[13,32,128]{2,1,0:T(8,128)}, f32[13,32,128]{2,1,0:T(8,128)S(1)}, u32[]{:S(2)}, u32[]{:S(2)}) collective-permute-start(f32[13,32,128]{2,1,0:T(8,128)} %get-tuple-element.21), channel_id=1, source_target_pairs={{0,16},{8,24},{16,0},{24,8},{1,17},{9,25},{17,1},{25,9},{2,18},{10... | collective-permute-start | bytes 638984 | tf_op jit(solution)/shard_map/ppermute | solution.py:612
  17.8 0.2 collective-permute-start.4
  18.0 1.6 %collective-permute-start.2 = (f32[8,40,128]{2,1,0:T(8,128)S(1)}, f32[8,40,128]{2,1,0:T(8,128)S(1)}, u32[]{:S(2)}, u32[]{:S(2)}) collective-permute-start(f32[8,40,128]{2,1,0:T(8,128)S(1)} %pad_maximum_fusion.1), channel_id=1, source_target_pairs={{0,24},{8,0},{16,8},{24,16},{1,25},{9,1},{17,9},{25,17},{2,26},{10... | collective-permute-start | bytes 491528 | tf_op jit(solution)/shard_map/ppermute | solution.py:612
  19.6 8.8 %collective-permute-done.2.refs_2_ = f32[8,40,128]{2,1,0:T(8,128)S(1)} collective-permute-done((f32[8,40,128]{2,1,0:T(8,128)S(1)}, f32[8,40,128]{2,1,0:T(8,128)S(1)}, u32[]{:S(2)}, u32[]{:S(2)}) %collective-permute-start.2) | collective-permute-done | bytes 163872 | tf_op jit(solution)/shard_map/ppermute | solution.py:612
  28.4 0.3 collective-permute-done.4.refs_4_
  28.8 1.1 %copy-done.5 = bf16[4,72,1152]{2,1,0:T(8,128)(2,1)S(1)} copy-done((bf16[4,72,1152]{2,1,0:T(8,128)(2,1)S(1)}, bf16[4,72,1152]{2,1,0:T(8,128)(2,1)}, u32[]{:S(2)}) %copy-start.5) | copy-done | bytes 663576
  29.9 1.0 %copy-done.7 = f32[19,32,128]{2,1,0:T(8,128)S(1)} copy-done((f32[19,32,128]{2,1,0:T(8,128)S(1)}, f32[19,32,128]{2,1,0:T(8,128)}, u32[]{:S(2)}) %copy-start.7) | copy-done | bytes 311320
  30.9 6.9 %shard_map.183 = (f32[1024,128]{1,0:T(8,128)S(1)}, f32[24,1024]{1,0:T(8,128)S(1)}, f32[24,1024]{1,0:T(8,128)S(1)}, f32[24,144]{1,0:T(8,128)S(1)}, f32[72,456]{1,...) custom-call(s32[4]{0:T(128)S(1)} %pad_add_fusion.place_ref, f32[32,32,128]{2,1,0:T(8,128)S(1)} %copy-done.1, ...), custom_call_target="tpu_custom_call" | custom-call | tf_op jit(solution)/shard_map/pallas_call | solution.py:596
  37.7 1.6 %collective-permute-start.7 = (f32[24,1024]{1,0:T(8,128)S(1)}, f32[24,1024]{1,0:T(8,128)S(1)}, u32[]{:S(2)}, u32[]{:S(2)}) collective-permute-start(f32[24,1024]{1,0:T(8,128)S(1)} %get-tuple-element.26), channel_id=1, source_target_pairs={{0,1},{1,2},{2,3},{3,0},{4,5},{5,6},{6,7},{7,4},{8,9},{9,10},{10,1... | collective-permute-start | bytes 294920 | tf_op jit(solution)/shard_map/ppermute | solution.py:612
  39.4 2.3 %collective-permute-start.8 = (f32[24,1024]{1,0:T(8,128)S(1)}, f32[24,1024]{1,0:T(8,128)S(1)}, u32[]{:S(2)}, u32[]{:S(2)}) collective-permute-start(f32[24,1024]{1,0:T(8,128)S(1)} %get-tuple-element.27), channel_id=1, source_target_pairs={{0,3},{1,0},{2,1},{3,2},{4,7},{5,4},{6,5},{7,6},{8,11},{9,8},{10,9... | collective-permute-start | bytes 294920 | tf_op jit(solution)/shard_map/ppermute | solution.py:612
  41.6 0.8 %collective-permute-start.9 = (f32[24,144]{1,0:T(8,128)S(1)}, f32[24,144]{1,0:T(8,128)S(1)}, u32[]{:S(2)}, u32[]{:S(2)}) collective-permute-start(f32[24,144]{1,0:T(8,128)S(1)} %get-tuple-element.28), channel_id=1, source_target_pairs={{0,2},{1,3},{2,0},{3,1},{4,6},{5,7},{6,4},{7,5},{8,10},{9,11},{10,... | collective-permute-start | bytes 41480 | tf_op jit(solution)/shard_map/ppermute | solution.py:612
  42.4 6.0 %collective-permute-done.9.refs_0_ = f32[24,144]{1,0:T(8,128)S(1)} collective-permute-done((f32[24,144]{1,0:T(8,128)S(1)}, f32[24,144]{1,0:T(8,128)S(1)}, u32[]{:S(2)}, u32[]{:S(2)}) %collective-permute-start.9) | collective-permute-done | bytes 13856 | tf_op jit(solution)/shard_map/ppermute | solution.py:612
  48.5 2.6 %shard_map.184 = f32[1024,128]{1,0:T(8,128)} custom-call(s32[4]{0:T(128)S(1)} %pad_add_fusion.place_ref, f32[1024,128]{1,0:T(8,128)S(1)} %get-tuple-element.22.main_ref, f32[72,456]{1,0:T(8,128)S(1)} %get-tuple-element.23.e1_ref, f32[40,208]{1,0:T(8,128)S(1)} %get-tuple-element.24.e2_ref, f32[24,144]{1,0:T(8,128)S(1)} %get-tuple-element.25.e3_ref, ...), custom_call_target="tpu_custom_call" | custom-call | tf_op jit(solution)/shard_map/pallas_call | solution.py:596
  (50 shorter events, 0.3 us)
Async XLA Ops:
  1.0 7.2 %collective-permute-start = (f32[32,8,128]{2,1,0:T(8,128)S(1)}, f32[32,8,128]{2,1,0:T(8,128)S(1)}, u32[]{:S(2)}, u32[]{:S(2)}) collective-permute-start(f32[32,8,128]{2,1,0:T(8,128)S(1)} %slice_select_fusion), channel_id=1, source_target_pairs={{0,4},{4,0},{1,5},{5,1},{2,6},{6,2},{3,7},{7,3},{8,12},{12,8},{9,1... | collective-permute-start | bytes 393224 | tf_op jit(solution)/shard_map/ppermute | solution.py:612
  6.9 21.8 %copy-start.1 = (f32[32,32,128]{2,1,0:T(8,128)S(1)}, f32[32,32,128]{2,1,0:T(8,128)}, u32[]{:S(2)}) copy-start(f32[32,32,128]{2,1,0:T(8,128)} %q_ref.3) | copy-start | bytes 1572868
  6.9 21.8 %copy-start.2 = (bf16[4,104,1152]{2,1,0:T(8,128)(2,1)S(1)}, bf16[4,104,1152]{2,1,0:T(8,128)(2,1)}, u32[]{:S(2)}) copy-start(bf16[4,104,1152]{2,1,0:T(8,128)(2,1)} %constant.59.clone.refs_12_) | copy-start | bytes 2875396
  6.9 21.8 %copy-start.4 = (bf16[4,112,768]{2,1,0:T(8,128)(2,1)S(1)}, bf16[4,112,768]{2,1,0:T(8,128)(2,1)}, u32[]{:S(2)}) copy-start(bf16[4,112,768]{2,1,0:T(8,128)(2,1)} %constant.61.clone.refs_14_) | copy-start | bytes 2064388
  6.9 21.8 %copy-start.10 = (bf16[4,16,1152]{2,1,0:T(8,128)(2,1)S(1)}, bf16[4,16,1152]{2,1,0:T(8,128)(2,1)}, u32[]{:S(2)}) copy-start(bf16[4,16,1152]{2,1,0:T(8,128)(2,1)} %constant.58.clone.refs_11_) | copy-start | bytes 442372
  6.9 21.8 %copy-start.11 = (bf16[2,96,144]{2,1,0:T(8,128)(2,1)S(1)}, bf16[2,96,144]{2,1,0:T(8,128)(2,1)}, u32[]{:S(2)}) copy-start(bf16[2,96,144]{2,1,0:T(8,128)(2,1)} %constant.54.clone.refs_7_) | copy-start | bytes 165892
  6.9 21.8 %copy-start.12 = (bf16[2,152,96]{2,1,0:T(8,128)(2,1)S(1)}, bf16[2,152,96]{2,1,0:T(8,128)(2,1)}, u32[]{:S(2)}) copy-start(bf16[2,152,96]{2,1,0:T(8,128)(2,1)} %constant.55.clone.refs_8_) | copy-start | bytes 175108
  6.9 21.8 %copy-start.19 = (f32[4,648]{1,0:T(4,128)S(1)}, f32[4,648]{1,0:T(4,128)}, u32[]{:S(2)}) copy-start(f32[4,648]{1,0:T(4,128)} %constant.56.clone.refs_9_) | copy-start | bytes 31108
  8.1 5.5 %collective-permute-start.3 = (f32[19,16,128]{2,1,0:T(8,128)S(1)}, f32[19,16,128]{2,1,0:T(8,128)S(1)}, u32[]{:S(2)}, u32[]{:S(2)}) collective-permute-start(f32[19,16,128]{2,1,0:T(8,128)S(1)} %get-tuple-element.18), channel_id=1, source_target_pairs={{0,4},{4,0},{1,5},{5,1},{2,6},{6,2},{3,7},{7,3},{8,12},{12,8},{9,1... | collective-permute-start | bytes 466952 | tf_op jit(solution)/shard_map/ppermute | solution.py:612
  8.8 10.8 %collective-permute-start.1 = (f32[8,40,128]{2,1,0:T(8,128)S(1)}, f32[8,40,128]{2,1,0:T(8,128)S(1)}, u32[]{:S(2)}, u32[]{:S(2)}) collective-permute-start(f32[8,40,128]{2,1,0:T(8,128)S(1)} %pad_maximum_fusion), channel_id=1, source_target_pairs={{0,8},{8,16},{16,24},{24,0},{1,9},{9,17},{17,25},{25,1},{2,10},{10... | collective-permute-start | bytes 491528 | tf_op jit(solution)/shard_map/ppermute | solution.py:612
  16.2 12.4 %collective-permute-start.6 = (f32[13,32,128]{2,1,0:T(8,128)}, f32[13,32,128]{2,1,0:T(8,128)S(1)}, u32[]{:S(2)}, u32[]{:S(2)}) collective-permute-start(f32[13,32,128]{2,1,0:T(8,128)} %get-tuple-element.21), channel_id=1, source_target_pairs={{0,24},{8,0},{16,8},{24,16},{1,25},{9,1},{17,9},{25,17},{2,26},{10... | collective-permute-start | bytes 638984 | tf_op jit(solution)/shard_map/ppermute | solution.py:612
  16.2 12.4 %collective-permute-start.5 = (f32[13,32,128]{2,1,0:T(8,128)}, f32[13,32,128]{2,1,0:T(8,128)S(1)}, u32[]{:S(2)}, u32[]{:S(2)}) collective-permute-start(f32[13,32,128]{2,1,0:T(8,128)} %get-tuple-element.21), channel_id=1, source_target_pairs={{0,16},{8,24},{16,0},{24,8},{1,17},{9,25},{17,1},{25,9},{2,18},{10... | collective-permute-start | bytes 638984 | tf_op jit(solution)/shard_map/ppermute | solution.py:612
  17.8 10.9 %collective-permute-start.4 = (f32[13,32,128]{2,1,0:T(8,128)}, f32[13,32,128]{2,1,0:T(8,128)S(1)}, u32[]{:S(2)}, u32[]{:S(2)}) collective-permute-start(f32[13,32,128]{2,1,0:T(8,128)} %get-tuple-element.20), channel_id=1, source_target_pairs={{0,8},{8,16},{16,24},{24,0},{1,9},{9,17},{17,25},{25,1},{2,10},{10... | collective-permute-start | bytes 638984 | tf_op jit(solution)/shard_map/ppermute | solution.py:612
  18.0 10.4 %collective-permute-start.2 = (f32[8,40,128]{2,1,0:T(8,128)S(1)}, f32[8,40,128]{2,1,0:T(8,128)S(1)}, u32[]{:S(2)}, u32[]{:S(2)}) collective-permute-start(f32[8,40,128]{2,1,0:T(8,128)S(1)} %pad_maximum_fusion.1), channel_id=1, source_target_pairs={{0,24},{8,0},{16,8},{24,16},{1,25},{9,1},{17,9},{25,17},{2,26},{10... | collective-permute-start | bytes 491528 | tf_op jit(solution)/shard_map/ppermute | solution.py:612
  30.8 17.6 %copy-start.9 = (bf16[1,208,456]{2,1,0:T(8,128)(2,1)S(1)}, bf16[1,208,456]{2,1,0:T(8,128)(2,1)}, u32[]{:S(2)}) copy-start(bf16[1,208,456]{2,1,0:T(8,128)(2,1)} %constant.63.clone.refs_2_) | copy-start | bytes 569092
  30.8 17.6 %copy-start.13 = (bf16[4,72,40]{2,1,0:T(8,128)(2,1)S(1)}, bf16[4,72,40]{2,1,0:T(8,128)(2,1)}, u32[]{:S(2)}) copy-start(bf16[4,72,40]{2,1,0:T(8,128)(2,1)} %constant.68.clone.refs_7_) | copy-start | bytes 69124
  30.8 17.6 %copy-start.14 = (bf16[1,144,208]{2,1,0:T(8,128)(2,1)S(1)}, bf16[1,144,208]{2,1,0:T(8,128)(2,1)}, u32[]{:S(2)}) copy-start(bf16[1,144,208]{2,1,0:T(8,128)(2,1)} %constant.62.clone.refs_1_) | copy-start | bytes 179716
  30.8 17.6 %copy-start.15 = (bf16[4,40,24]{2,1,0:T(8,128)(2,1)S(1)}, bf16[4,40,24]{2,1,0:T(8,128)(2,1)}, u32[]{:S(2)}) copy-start(bf16[4,40,24]{2,1,0:T(8,128)(2,1)} %constant.67.clone.refs_6_) | copy-start | bytes 23044
  30.8 17.6 %copy-start.17 = (bf16[1,96,128]{2,1,0:T(8,128)(2,1)S(1)}, bf16[1,96,128]{2,1,0:T(8,128)(2,1)}, u32[]{:S(2)}) copy-start(bf16[1,96,128]{2,1,0:T(8,128)(2,1)} %constant.69.clone.refs_8_) | copy-start | bytes 73732
  30.9 17.6 %copy-start.18 = (f32[8,1,456]{2,1,0:T(1,128)S(1)}, f32[8,1,456]{2,1,0:T(1,128)}, u32[]{:S(2)}) copy-start(f32[8,1,456]{2,1,0:T(1,128)} %constant.66.clone.refs_5_) | copy-start | bytes 43780
  30.9 17.6 %copy-start.20 = (f32[8,1,208]{2,1,0:T(1,128)S(1)}, f32[8,1,208]{2,1,0:T(1,128)}, u32[]{:S(2)}) copy-start(f32[8,1,208]{2,1,0:T(1,128)} %constant.65.clone.refs_4_) | copy-start | bytes 19972
  37.7 10.6 %collective-permute-start.7 = (f32[24,1024]{1,0:T(8,128)S(1)}, f32[24,1024]{1,0:T(8,128)S(1)}, u32[]{:S(2)}, u32[]{:S(2)}) collective-permute-start(f32[24,1024]{1,0:T(8,128)S(1)} %get-tuple-element.26), channel_id=1, source_target_pairs={{0,1},{1,2},{2,3},{3,0},{4,5},{5,6},{6,7},{7,4},{8,9},{9,10},{10,1... | collective-permute-start | bytes 294920 | tf_op jit(solution)/shard_map/ppermute | solution.py:612
  39.4 9.0 %collective-permute-start.8 = (f32[24,1024]{1,0:T(8,128)S(1)}, f32[24,1024]{1,0:T(8,128)S(1)}, u32[]{:S(2)}, u32[]{:S(2)}) collective-permute-start(f32[24,1024]{1,0:T(8,128)S(1)} %get-tuple-element.27), channel_id=1, source_target_pairs={{0,3},{1,0},{2,1},{3,2},{4,7},{5,4},{6,5},{7,6},{8,11},{9,8},{10,9... | collective-permute-start | bytes 294920 | tf_op jit(solution)/shard_map/ppermute | solution.py:612
  41.6 6.8 %collective-permute-start.9 = (f32[24,144]{1,0:T(8,128)S(1)}, f32[24,144]{1,0:T(8,128)S(1)}, u32[]{:S(2)}, u32[]{:S(2)}) collective-permute-start(f32[24,144]{1,0:T(8,128)S(1)} %get-tuple-element.28), channel_id=1, source_target_pairs={{0,2},{1,3},{2,0},{3,1},{4,6},{5,7},{6,4},{7,5},{8,10},{9,11},{10,... | collective-permute-start | bytes 41480 | tf_op jit(solution)/shard_map/ppermute | solution.py:612
  (8 other events, 23.8 us)
where the time goes:
time: 51.5 us; the launch traced here: 51.1 us
  waiting for transfers between devices  19.9 us (39%)
  Pallas kernels  12.5 us (24%)
  starting transfers between devices  11.1 us (22%)
  local copies, waits for them, and re-layouts  6.18 us (12%)
  other arithmetic  1.09 us (2%)
    ppermute x10, waiting for transfers between devices, shift(): lax.ppermute(value, axis, [(i, (i + offset) % count) for i in range(count)])  19.9 us
    ppermute x10, starting transfers between devices, shift(): lax.ppermute(value, axis, [(i, (i + offset) % count) for i in range(count)])  11.1 us
    pallas_call x3, Pallas kernels, call(): pl.pallas_call(functools.partial(kernel, plan), grid_spec=pltpu.PrefetchS...  10.6 us
    unnamed x44, local copies, waits for them, and re-layouts  6.15 us
    pallas_call x1, Pallas kernels, shards(): pl.pallas_call(functools.partial(extend_kernel, plan), out_shape=extended)  1.93 us
  transfers between devices with their start and end apart: 10, of which 4 were waited for; matrix products, arithmetic and copies ran while one was open for 0% of the time, Pallas kernels for 6%

commit v1 on v0

--- a/solution.py
+++ b/solution.py
@@ -205,20 +205,6 @@
             tables.append(left3(whole))
         return np.stack(tables)
 
-    def top_x(self):
-        x = self.x
-        return np.stack(
-            [
-                np.stack(
-                    [
-                        np.stack([x.mix(3, sigma, b, (b - r) % x.count) for r in range(x.count)], axis=1)
-                        for sigma in TOP_SIGMAS
-                    ]
-                ).reshape(-1)
-                for b in range(x.count)
-            ]
-        ).astype(np.float32)
-
     def fine_z(self):
         z, own, pushed = self.z, [], []
         for b in range(z.count):
@@ -274,9 +260,9 @@
         flat = []
         for level in (3, 2, 1):
             q = place((rows[level], rows[level - 1]), (0, 0, free(y, level).T))
-            flat.append(exact(np.kron(free(x, level).T, q))[None])
+            flat.append(exact(np.kron(free(x, level).T, q)))
         masks = []
-        for level in (2, 1):
+        for level in (3, 2, 1):
             table = np.zeros((x.count * y.count, 1, self.flat[level]), np.float32)
             for bx in range(x.count):
                 for by in range(y.count):
@@ -293,23 +279,24 @@
             )
         pieces = [(0, 0, free(z, 1).T), (self.tall[1], 0, np.eye(8)), (self.tall[1] + 8, z.length - 8, np.eye(8))]
         last = place((up(self.tall[1] + 16, 16), z.length), *pieces)
-        return flat, masks, [exact(m) for m in tall], exact(last)[None]
-
-
-def restrict_kernel(plan, place_ref, q_ref, z_ref, y_ref, own_ref, *rest):
+        return flat, masks, [exact(m) for m in tall], exact(last)
+
+
+def restrict_kernel(plan, q_ref, z_ref, y_ref, own_ref, *rest):
     faces, mixed = rest[: plan.kinds], rest[plan.kinds]
     nx, ny, nz = plan.x.length, plan.y.length, plan.z.length
     high, low = split(q_ref[...].reshape(nx * ny, nz))
-    along_z = dot(jnp.concatenate([high, low, high], axis=1), z_ref[0])
+    along_z = dot(jnp.concatenate([high, low, high], axis=1), z_ref[lax.axis_index("gz")])
     high, low = split(along_z)
     high, low = high.reshape(nx, ny, LANES), low.reshape(nx, ny, LANES)
+    matrix_y = y_ref[lax.axis_index("gy")]
     for i in range(0, nx, 2):
         pair = [jnp.concatenate([high[j], high[j], low[j]], axis=0) for j in (i, i + 1)]
-        both = dot(y_ref[0], jnp.concatenate(pair, axis=1))
+        both = dot(matrix_y, jnp.concatenate(pair, axis=1))
         mixed[i] = both[:, :LANES]
         mixed[i + 1] = both[:, LANES:]
 
-    brick = place_ref[0]
+    brick = lax.axis_index("gx")
     keep_low = jnp.where(brick > 0, 1.0, 0.0).astype(F32)
     keep_high = jnp.where(brick < plan.x.count - 1, 1.0, 0.0).astype(F32)
 
@@ -384,7 +371,7 @@
         high_ref[p] = jnp.where(lanes[0] < plan.lane[2], first, ext[p])
 
 
-def mix_planes(get, put, count, matrix, rows):
+def mix_planes(get, put, count, matrix):
     for i in range(0, count, 2):
         pair = [i, min(i + 1, count - 1)]
         stacked = []
@@ -408,20 +395,21 @@
     return result
 
 
-def mix_kernel(plan, place_ref, q_ref, *refs):
+def mix_kernel(plan, q_ref, *refs):
     x, y, z = plan.x, plan.y, plan.z
     refs = list(refs)
     take = lambda n: [refs.pop(0) for _ in range(n)]
     halos = take(plan.fine_halos)
     before_ref, after_ref, ext_ref = take(3)
     coarse = take(x.count - 1)
-    fine_y, coarse_y, top_x, fine_own, fine_push, z1, z2, z3 = take(8)
+    fine_y, coarse_y, fine_own, fine_push, z1, z2, z3 = take(7)
     main_ref, near_next, near_prev = take(3)
     far = take(z.count - 3)
     e1_ref, e2_ref, e3_ref = take(3)
     fine_mixed, fine_ready, coarse_mixed, ready1, ready2, ready3 = take(6)
 
-    brick = place_ref[0]
+    brick = lax.axis_index("gx")
+    by, bz = lax.axis_index("gy"), lax.axis_index("gz")
     mask = lambda condition: jnp.where(condition, 1.0, 0.0).astype(F32)
     keep_before, keep_after = mask(brick > 0), mask(brick < x.count - 1)
 
@@ -439,7 +427,7 @@
     def fine_put(i, value):
         fine_mixed[i] = value
 
-    mix_planes(fine_plane, fine_put, x.length + 2 * REACH, fine_y[0], None)
+    mix_planes(fine_plane, fine_put, x.length + 2 * REACH, fine_y[by])
 
     def put_ready(ready, sigmas, s, row, value):
         high, low = split(value)
@@ -466,7 +454,7 @@
     def coarse_put(i, value):
         coarse_mixed[i] = value
 
-    mix_planes(coarse_plane, coarse_put, own_planes + plan.planes * (x.count - 1), coarse_y[0], None)
+    mix_planes(coarse_plane, coarse_put, own_planes + plan.planes * (x.count - 1), coarse_y[by])
 
     for level, ready in ((1, ready1), (2, ready2)):
         size = x.length >> level
@@ -495,29 +483,30 @@
                 for i, value in enumerate(stencil(planes, REACH, width, sigma)):
                     put_ready(ready, 3, s, i * rows + r, value)
 
-    width = x.width[3]
-    for s in range(len(TOP_SIGMAS)):
+    width, size = x.width[3], x.length >> 3
+    for s, sigma in enumerate(TOP_SIGMAS):
         row = plan.group[3] + s * plan.rows3
-        totals = [None] * width
-        for offset in range(x.count):
-            base = 0 if offset == 0 else own_planes + plan.planes * (offset - 1)
-            for k in range(width):
-                value = coarse_mixed[base + k, row : row + plan.rows3, :]
-                for i in range(width):
-                    weight = top_x[brick, ((s * width + i) * x.count + offset) * width + k]
-                    term = value * weight
-                    totals[i] = term if totals[i] is None else totals[i] + term
+        at = lambda i: coarse_mixed[i, row : row + plan.rows3, :]
+        cells = {LOW[3] + k: at(k) for k in range(width)}
+        for offset in range(1, x.count):
+            base = own_planes + plan.planes * (offset - 1)
+            for shift, here in ((-offset, brick >= offset), (x.count - offset, brick < offset)):
+                keep = mask(here)
+                for k in range(width):
+                    cell, value = shift * size + LOW[3] + k, at(base + k) * keep
+                    cells[cell] = cells[cell] + value if cell in cells else value
         for i in range(width):
-            put_ready(ready3, 2, s, i * plan.rows3, totals[i])
-
-    pushed = dot(fine_push[0], fine_ready[...], ((1,), (1,)))
+            terms = [v * float(np.exp(-(((c - LOW[3] - i) / sigma) ** 2))) for c, v in cells.items()]
+            put_ready(ready3, 2, s, i * plan.rows3, functools.reduce(jnp.add, terms))
+
+    pushed = dot(fine_push[bz], fine_ready[...], ((1,), (1,)))
     near = (near_next, near_prev)
     for n, ref in enumerate(near):
         ref[8:24, :] = jnp.zeros((16, ref.shape[1]), F32)
         ref[:8, :] = pushed[8 * n : 8 * n + 8]
-    one = dot(z1[0], ready1[...], ((1,), (1,)))
-    two = dot(z2[0], ready2[...], ((1,), (1,)))
-    three = dot(z3[0], ready3[...], ((1,), (1,)))
+    one = dot(z1[bz], ready1[...], ((1,), (1,)))
+    two = dot(z2[bz], ready2[...], ((1,), (1,)))
+    three = dot(z3[bz], ready3[...], ((1,), (1,)))
     e1_ref[...] = one[: plan.tall[1]]
     e2_ref[...] = two[: plan.tall[2]]
     e3_ref[...] = three[: plan.tall[3]]
@@ -538,14 +527,16 @@
             far[far_index][...] = three[top : top + plan.tall[3]]
             far_index += 1
             top += plan.tall[3]
-    main_ref[...] = dot(fine_ready[...], fine_own[0])
-
-
-def finish_kernel(plan, place_ref, main_ref, e1_ref, e2_ref, e3_ref, prev_ref, next_ref, *refs):
+    main_ref[...] = dot(fine_ready[...], fine_own[bz])
+
+
+def finish_kernel(plan, main_ref, e1_ref, e2_ref, e3_ref, prev_ref, next_ref, *refs):
     z = plan.z
     refs = list(refs)
     far = [refs.pop(0) for _ in range(z.count - 3)]
-    flat3, flat2, flat1, mask2, mask1, tall3, tall2, last, out_ref, e1, e2, e3 = refs
+    flat3, flat2, flat1, mask3, mask2, mask1, tall3, tall2, last, out_ref, e1, e2, e3 = refs
+    bz = lax.axis_index("gz")
+    column = lax.axis_index("gx") * plan.y.count + lax.axis_index("gy")
     e1[...], e2[...], e3[...] = e1_ref[...], e2_ref[...], e3_ref[...]
     for f in far:
         e3[...] += f[...]
@@ -566,45 +557,30 @@
         high, low = split(value)
         return dot(matrix, high) + dot(matrix, low)
 
-    two = (e2[...] + along(tall3[0], across(e3[...], flat3[0]))) * mask2[0]
-    one = (e1[...] + along(tall2[0], across(two, flat2[0]))) * mask1[0]
-    spread = across(one, flat1[0])
+    three = e3[...] * mask3[column]
+    two = (e2[...] + along(tall3[bz], across(three, flat3[...]))) * mask2[column]
+    one = (e1[...] + along(tall2[bz], across(two, flat2[...]))) * mask1[column]
+    spread = across(one, flat1[...])
     rows = jnp.concatenate([spread, prev_ref[:8, :], next_ref[:8, :]], axis=0)
-    pad = last.shape[1] - rows.shape[0]
+    pad = last.shape[0] - rows.shape[0]
     if pad:
         rows = jnp.concatenate([rows, jnp.zeros((pad, rows.shape[1]), F32)], axis=0)
     high, low = split(rows)
     stacked = jnp.concatenate([high, low], axis=0)
-    matrix = jnp.concatenate([last[0], last[0]], axis=0)
+    matrix = jnp.concatenate([last[...], last[...]], axis=0)
     out_ref[...] = main_ref[...] + dot(stacked, matrix, ((0,), (0,)))
 
 
-def call(kernel, plan, place_at, operands, tables, outs, scratch=(), smem=()):
-    whole = lambda a: pl.BlockSpec(a.shape, lambda i, at, n=a.ndim: (0,) * n)
-    specs = [whole(a) for a in operands]
-    arrays = list(operands)
-    for table, index in tables:
-        arrays.append(jnp.asarray(table))
-        if index is None:
-            specs.append(pl.BlockSpec(memory_space=pltpu.SMEM))
-        elif index < 0:
-            specs.append(whole(table))
-        else:
-            specs.append(
-                pl.BlockSpec((1,) + table.shape[1:], lambda i, at, k=index, n=table.ndim: (at[k],) + (0,) * (n - 1))
-            )
+def call(kernel, plan, operands, outs, scratch=()):
+    whole = pl.BlockSpec(memory_space=pltpu.VMEM)
     return pl.pallas_call(
         functools.partial(kernel, plan),
-        grid_spec=pltpu.PrefetchScalarGridSpec(
-            num_scalar_prefetch=1,
-            grid=(1,),
-            in_specs=specs,
-            out_specs=[whole(o) for o in outs],
-            scratch_shapes=list(scratch),
-        ),
+        in_specs=[whole] * len(operands),
+        out_specs=[whole] * len(outs),
+        scratch_shapes=list(scratch),
         out_shape=list(outs),
         compiler_params=pltpu.CompilerParams(vmem_limit_bytes=48 * 2**20),
-    )(place_at, *arrays)
+    )(*[jnp.asarray(o) for o in operands])
 
 
 def shift(value, axis, offset):
@@ -615,20 +591,17 @@
 def shards(plan, charges):
     x, y, z = plan.x, plan.y, plan.z
     array = lambda *shape: jax.ShapeDtypeStruct(shape, F32)
-    at = [lax.axis_index(name) for name in ("gx", "gy", "gz")]
-    place_at = jnp.stack(at + [at[0] * y.count + at[1]]).astype(jnp.int32)
+    at_y = lax.axis_index("gy")
 
     faces = charges[:, : REACH], charges[:, y.length - REACH :]
     if y.count == 2:
-        fine_y = [shift(jnp.where(at[1] == 0, faces[1], faces[0]), "gy", 1)]
+        fine_y = [shift(jnp.where(at_y == 0, faces[1], faces[0]), "gy", 1)]
     else:
         fine_y = [shift(faces[1], "gy", 1), shift(faces[0], "gy", y.count - 1)]
     own, *coarse_faces = call(
         restrict_kernel,
         plan,
-        place_at,
-        [charges],
-        [(plan.restrict_z(), 2), (plan.restrict_y(), 1)],
+        [charges, plan.restrict_z(), plan.restrict_y()],
         [array(x.width[1], plan.rows1, LANES)] + [array(x.width[1], 16, LANES)] * plan.kinds,
         [pltpu.VMEM((x.length, plan.rows_restricted, LANES), F32)],
     )
@@ -639,7 +612,7 @@
         shift(jnp.concatenate([charges[:REACH]] + [f[:REACH] for f in fine_y], axis=1), "gx", x.count - 1),
     ]
     extended = [array(n, plan.coarse_rows, LANES) for n in (x.width[1], plan.planes, plan.planes)]
-    ext, high, low = pl.pallas_call(functools.partial(extend_kernel, plan), out_shape=extended)(own, *coarse_halos)
+    ext, high, low = call(extend_kernel, plan, [own, *coarse_halos], extended)
     coarse_x = [shift(high if r == 1 else low, "gx", r) for r in range(1, x.count)]
 
     fine_own, fine_push = plan.fine_z()
@@ -649,18 +622,7 @@
     results = call(
         mix_kernel,
         plan,
-        place_at,
-        [charges] + fine_y + fine_x + [ext] + coarse_x,
-        [
-            (plan.fine_y(), 1),
-            (plan.coarse_y(), 1),
-            (plan.top_x(), None),
-            (fine_own, 2),
-            (fine_push, 2),
-            (zs[0], 2),
-            (zs[1], 2),
-            (zs[2], 2),
-        ],
+        [charges] + fine_y + fine_x + [ext] + coarse_x + [plan.fine_y(), plan.coarse_y(), fine_own, fine_push] + zs,
         [array(cells, LANES), array(24, cells), array(24, cells)]
         + [array(plan.tall[3], plan.flat[3])] * (z.count - 3)
         + [array(plan.tall[l], plan.flat[l]) for l in (1, 2, 3)],
@@ -682,9 +644,7 @@
     (potential,) = call(
         finish_kernel,
         plan,
-        place_at,
-        [main, *windows, from_prev, from_next, *from_far],
-        [(m, -1) for m in flat] + [(m, 3) for m in masks] + [(m, 2) for m in tall] + [(last, -1)],
+        [main, *windows, from_prev, from_next, *from_far, *flat, *masks, *tall, last],
         [array(cells, LANES)],
         [pltpu.VMEM((plan.tall[l], plan.flat[l]), F32) for l in (1, 2, 3)],
     )

time: 51.5 us -> 46 us (0.89)
  Pallas kernels: 12.5 us -> 9 us
  local copies, waits for them, and re-layouts: 6.18 us -> 3.99 us
    pallas_call x4, Pallas kernels: 12.5 us -> 9 us  [call(): pl.pallas_call(functools.partial(kernel, plan), in_specs=[whole] * len(op...]
    unnamed x44 -> x38, local copies, waits for them, and re-layouts: 6.15 us -> 3.97 us
  transfers between devices with their start and end apart: 10 -> 10, of which waited for: 4 -> 4; matrix products, arithmetic and copies ran while one was open for 0% -> 0% of each run, Pallas kernels for 6% -> 1%
where the time goes in v1:
time: 46 us; the launch traced here: 45.6 us
  waiting for transfers between devices  20.1 us (44%)
  starting transfers between devices  11.3 us (25%)
  Pallas kernels  9 us (20%)
  local copies, waits for them, and re-layouts  3.99 us (9%)
  other arithmetic  1.01 us (2%)
    ppermute x10, waiting for transfers between devices, shift(): lax.ppermute(value, axis, [(i, (i + offset) % count) for i in range(count)])  20.1 us
    ppermute x10, starting transfers between devices, shift(): lax.ppermute(value, axis, [(i, (i + offset) % count) for i in range(count)])  11.3 us
    pallas_call x4, Pallas kernels, call(): pl.pallas_call(functools.partial(kernel, plan), in_specs=[whole] * len(op...  9 us
    unnamed x38, local copies, waits for them, and re-layouts  3.97 us
    select_n x1, other arithmetic, shards(): fine_y = [shift(jnp.where(at_y == 0, faces[1], faces[0]), 'gy', 1)]  0.99 us
  transfers between devices with their start and end apart: 10, of which 4 were waited for; matrix products, arithmetic and copies ran while one was open for 0% of the time, Pallas kernels for 1%

profile of v1, /device:TPU:0, one launch (start us, length us, event | category | flops | bytes accessed | tf_op | source)
XLA Modules:
  0.0 45.6 jit_solution(358413069550462074)
XLA Ops:
  0.0 1.0 %slice_select_fusion = f32[32,8,128]{2,1,0:T(8,128)S(1)} fusion(f32[32,32,128]{2,1,0:T(8,128)} %q_ref.3, pred[]{:T(512)S(6)} %eq.3), kind=kLoop, calls=%fused_computation.2 | loop fusion | flops 32768 | bytes 393217 | tf_op jit(solution)/shard_map/jit(_where)/select_n | solution.py:598
  1.0 3.0 %collective-permute-start = (f32[32,8,128]{2,1,0:T(8,128)S(1)}, f32[32,8,128]{2,1,0:T(8,128)S(1)}, u32[]{:S(2)}, u32[]{:S(2)}) collective-permute-start(f32[32,8,128]{2,1,0:T(8,128)S(1)} %slice_select_fusion), channel_id=1, source_target_pairs={{0,4},{4,0},{1,5},{5,1},{2,6},{6,2},{3,7},{7,3},{8,12},{12,8},{9,1... | collective-permute-start | bytes 393224 | tf_op jit(solution)/shard_map/ppermute | solution.py:588
  4.0 1.0 %copy-done = f32[32,32,128]{2,1,0:T(8,128)S(1)} copy-done((f32[32,32,128]{2,1,0:T(8,128)S(1)}, f32[32,32,128]{2,1,0:T(8,128)}, u32[]{:S(2)}) %copy-start) | copy-done | bytes 524312
  5.0 1.0 %copy-done.6 = bf16[4,384,128]{2,1,0:T(8,128)(2,1)S(1)} copy-done((bf16[4,384,128]{2,1,0:T(8,128)(2,1)S(1)}, bf16[4,384,128]{2,1,0:T(8,128)(2,1)}, u32[]{:S(2)}) %copy-start.6) | copy-done | bytes 393240
  6.0 0.8 %copy-done.14 = bf16[2,72,96]{2,1,0:T(8,128)(2,1)S(1)} copy-done((bf16[2,72,96]{2,1,0:T(8,128)(2,1)S(1)}, bf16[2,72,96]{2,1,0:T(8,128)(2,1)}, u32[]{:S(2)}) %copy-start.14) | copy-done | bytes 27672
  6.8 0.0 copy-start.9
  6.8 0.6 %shard_map.181 = (f32[19,24,128]{2,1,0:T(8,128)S(1)}, f32[19,16,128]{2,1,0:T(8,128)S(1)}) custom-call(f32[32,32,128]{2,1,0:T(8,128)S(1)} %copy-done, bf16[4,384,128]{2,1,0:T(8,128)(2,1)S(1)} %copy-done.6, bf16[2,72,96]{2,1,0:T(8,128)(2,1)S(1)} %copy-done.14), custom_call_target="tpu_custom_call" | custom-call | tf_op jit(solution)/shard_map/pallas_call | solution.py:576
  7.5 0.1 collective-permute-start.3
  7.6 0.1 collective-permute-start.1
  7.7 5.3 %collective-permute-done.3.refs_0_ = f32[19,16,128]{2,1,0:T(8,128)S(1)} collective-permute-done((f32[19,16,128]{2,1,0:T(8,128)S(1)}, f32[19,16,128]{2,1,0:T(8,128)S(1)}, u32[]{:S(2)}, u32[]{:S(2)}) %collective-permute-start.3) | collective-permute-done | bytes 155680 | tf_op jit(solution)/shard_map/ppermute | solution.py:588
  13.1 0.1 collective-permute-start.6
  13.1 1.6 %collective-permute-start.5 = (f32[13,32,128]{2,1,0:T(8,128)S(1)}, f32[13,32,128]{2,1,0:T(8,128)S(1)}, u32[]{:S(2)}, u32[]{:S(2)}) collective-permute-start(f32[13,32,128]{2,1,0:T(8,128)S(1)} %get-tuple-element.21), channel_id=1, source_target_pairs={{0,16},{8,24},{16,0},{24,8},{1,17},{9,25},{17,1},{25,9},{2,18},{10... | collective-permute-start | bytes 638984 | tf_op jit(solution)/shard_map/ppermute | solution.py:588
  14.7 0.2 collective-permute-start.4
  14.9 1.6 %collective-permute-start.2 = (f32[8,40,128]{2,1,0:T(8,128)S(1)}, f32[8,40,128]{2,1,0:T(8,128)S(1)}, u32[]{:S(2)}, u32[]{:S(2)}) collective-permute-start(f32[8,40,128]{2,1,0:T(8,128)S(1)} %pad_maximum_fusion.1), channel_id=1, source_target_pairs={{0,24},{8,0},{16,8},{24,16},{1,25},{9,1},{17,9},{25,17},{2,26},{10... | collective-permute-start | bytes 491528 | tf_op jit(solution)/shard_map/ppermute | solution.py:588
  16.5 8.6 %collective-permute-done.2.refs_2_ = f32[8,40,128]{2,1,0:T(8,128)S(1)} collective-permute-done((f32[8,40,128]{2,1,0:T(8,128)S(1)}, f32[8,40,128]{2,1,0:T(8,128)S(1)}, u32[]{:S(2)}, u32[]{:S(2)}) %collective-permute-start.2) | collective-permute-done | bytes 163872 | tf_op jit(solution)/shard_map/ppermute | solution.py:588
  25.1 0.3 collective-permute-done.4.refs_4_
  25.4 0.0 copy-start.5
  25.4 1.1 %copy-done.5 = bf16[4,72,1152]{2,1,0:T(8,128)(2,1)S(1)} copy-done((bf16[4,72,1152]{2,1,0:T(8,128)(2,1)S(1)}, bf16[4,72,1152]{2,1,0:T(8,128)(2,1)}, u32[]{:S(2)}) %copy-start.5) | copy-done | bytes 663576
  26.6 6.3 %shard_map.183 = (f32[1024,128]{1,0:T(8,128)S(1)}, f32[24,1024]{1,0:T(8,128)S(1)}, f32[24,1024]{1,0:T(8,128)S(1)}, f32[24,144]{1,0:T(8,128)S(1)}, f32[72,456]{1,...) custom-call(f32[32,32,128]{2,1,0:T(8,128)S(1)} %copy-done.1, ...), custom_call_target="tpu_custom_call" | custom-call | tf_op jit(solution)/shard_map/pallas_call | solution.py:576
  32.9 1.6 %collective-permute-start.7 = (f32[24,1024]{1,0:T(8,128)S(1)}, f32[24,1024]{1,0:T(8,128)S(1)}, u32[]{:S(2)}, u32[]{:S(2)}) collective-permute-start(f32[24,1024]{1,0:T(8,128)S(1)} %get-tuple-element.26), channel_id=1, source_target_pairs={{0,1},{1,2},{2,3},{3,0},{4,5},{5,6},{6,7},{7,4},{8,9},{9,10},{10,1... | collective-permute-start | bytes 294920 | tf_op jit(solution)/shard_map/ppermute | solution.py:588
  34.5 2.2 %collective-permute-start.8 = (f32[24,1024]{1,0:T(8,128)S(1)}, f32[24,1024]{1,0:T(8,128)S(1)}, u32[]{:S(2)}, u32[]{:S(2)}) collective-permute-start(f32[24,1024]{1,0:T(8,128)S(1)} %get-tuple-element.27), channel_id=1, source_target_pairs={{0,3},{1,0},{2,1},{3,2},{4,7},{5,4},{6,5},{7,6},{8,11},{9,8},{10,9... | collective-permute-start | bytes 294920 | tf_op jit(solution)/shard_map/ppermute | solution.py:588
  36.8 0.8 %collective-permute-start.9 = (f32[24,144]{1,0:T(8,128)S(1)}, f32[24,144]{1,0:T(8,128)S(1)}, u32[]{:S(2)}, u32[]{:S(2)}) collective-permute-start(f32[24,144]{1,0:T(8,128)S(1)} %get-tuple-element.28), channel_id=1, source_target_pairs={{0,2},{1,3},{2,0},{3,1},{4,6},{5,7},{6,4},{7,5},{8,10},{9,11},{10,... | collective-permute-start | bytes 41480 | tf_op jit(solution)/shard_map/ppermute | solution.py:588
  37.5 6.0 %collective-permute-done.9.refs_0_ = f32[24,144]{1,0:T(8,128)S(1)} collective-permute-done((f32[24,144]{1,0:T(8,128)S(1)}, f32[24,144]{1,0:T(8,128)S(1)}, u32[]{:S(2)}, u32[]{:S(2)}) %collective-permute-start.9) | collective-permute-done | bytes 13856 | tf_op jit(solution)/shard_map/ppermute | solution.py:588
  43.6 2.1 %shard_map.184 = f32[1024,128]{1,0:T(8,128)} custom-call(f32[1024,128]{1,0:T(8,128)S(1)} %get-tuple-element.22.main_ref, f32[72,456]{1,0:T(8,128)S(1)} %get-tuple-element.23.e1_ref, f32[40,208]{1,0:T(8,128)S(1)} %get-tuple-element.24.e2_ref, f32[24,144]{1,0:T(8,128)S(1)} %get-tuple-element.25.e3_ref, f32[24,1024]{1,0:T(8,128)S(1)} %collective-permute-done.7.prev_ref, ...), custom_call_target="tpu_custom_call" | custom-call | tf_op jit(solution)/shard_map/pallas_call | solution.py:576
  (43 shorter events, 0.2 us)
Async XLA Ops:
  1.0 6.6 %collective-permute-start = (f32[32,8,128]{2,1,0:T(8,128)S(1)}, f32[32,8,128]{2,1,0:T(8,128)S(1)}, u32[]{:S(2)}, u32[]{:S(2)}) collective-permute-start(f32[32,8,128]{2,1,0:T(8,128)S(1)} %slice_select_fusion), channel_id=1, source_target_pairs={{0,4},{4,0},{1,5},{5,1},{2,6},{6,2},{3,7},{7,3},{8,12},{12,8},{9,1... | collective-permute-start | bytes 393224 | tf_op jit(solution)/shard_map/ppermute | solution.py:588
  6.8 18.6 %copy-start.1 = (f32[32,32,128]{2,1,0:T(8,128)S(1)}, f32[32,32,128]{2,1,0:T(8,128)}, u32[]{:S(2)}) copy-start(f32[32,32,128]{2,1,0:T(8,128)} %q_ref.3) | copy-start | bytes 1572868
  6.8 18.6 %copy-start.2 = (bf16[4,104,1152]{2,1,0:T(8,128)(2,1)S(1)}, bf16[4,104,1152]{2,1,0:T(8,128)(2,1)}, u32[]{:S(2)}) copy-start(bf16[4,104,1152]{2,1,0:T(8,128)(2,1)} %constant.50.clone.refs_11_) | copy-start | bytes 2875396
  6.8 18.6 %copy-start.4 = (bf16[4,112,768]{2,1,0:T(8,128)(2,1)S(1)}, bf16[4,112,768]{2,1,0:T(8,128)(2,1)}, u32[]{:S(2)}) copy-start(bf16[4,112,768]{2,1,0:T(8,128)(2,1)} %constant.52.clone.refs_13_) | copy-start | bytes 2064388
  6.8 18.6 %copy-start.8 = (bf16[4,16,1152]{2,1,0:T(8,128)(2,1)S(1)}, bf16[4,16,1152]{2,1,0:T(8,128)(2,1)}, u32[]{:S(2)}) copy-start(bf16[4,16,1152]{2,1,0:T(8,128)(2,1)} %constant.49.clone.refs_10_) | copy-start | bytes 442372
  6.8 18.6 %copy-start.9 = (bf16[2,96,144]{2,1,0:T(8,128)(2,1)S(1)}, bf16[2,96,144]{2,1,0:T(8,128)(2,1)}, u32[]{:S(2)}) copy-start(bf16[2,96,144]{2,1,0:T(8,128)(2,1)} %constant.46.clone.refs_7_) | copy-start | bytes 165892
  6.8 18.6 %copy-start.10 = (bf16[2,152,96]{2,1,0:T(8,128)(2,1)S(1)}, bf16[2,152,96]{2,1,0:T(8,128)(2,1)}, u32[]{:S(2)}) copy-start(bf16[2,152,96]{2,1,0:T(8,128)(2,1)} %constant.47.clone.refs_8_) | copy-start | bytes 175108
  7.5 5.5 %collective-permute-start.3 = (f32[19,16,128]{2,1,0:T(8,128)S(1)}, f32[19,16,128]{2,1,0:T(8,128)S(1)}, u32[]{:S(2)}, u32[]{:S(2)}) collective-permute-start(f32[19,16,128]{2,1,0:T(8,128)S(1)} %get-tuple-element.18), channel_id=1, source_target_pairs={{0,4},{4,0},{1,5},{5,1},{2,6},{6,2},{3,7},{7,3},{8,12},{12,8},{9,1... | collective-permute-start | bytes 466952 | tf_op jit(solution)/shard_map/ppermute | solution.py:588
  7.6 8.9 %collective-permute-start.1 = (f32[8,40,128]{2,1,0:T(8,128)S(1)}, f32[8,40,128]{2,1,0:T(8,128)S(1)}, u32[]{:S(2)}, u32[]{:S(2)}) collective-permute-start(f32[8,40,128]{2,1,0:T(8,128)S(1)} %pad_maximum_fusion), channel_id=1, source_target_pairs={{0,8},{8,16},{16,24},{24,0},{1,9},{9,17},{17,25},{25,1},{2,10},{10... | collective-permute-start | bytes 491528 | tf_op jit(solution)/shard_map/ppermute | solution.py:588
  13.1 12.3 %collective-permute-start.6 = (f32[13,32,128]{2,1,0:T(8,128)S(1)}, f32[13,32,128]{2,1,0:T(8,128)S(1)}, u32[]{:S(2)}, u32[]{:S(2)}) collective-permute-start(f32[13,32,128]{2,1,0:T(8,128)S(1)} %get-tuple-element.21), channel_id=1, source_target_pairs={{0,24},{8,0},{16,8},{24,16},{1,25},{9,1},{17,9},{25,17},{2,26},{10... | collective-permute-start | bytes 638984 | tf_op jit(solution)/shard_map/ppermute | solution.py:588
  13.1 12.2 %collective-permute-start.5 = (f32[13,32,128]{2,1,0:T(8,128)S(1)}, f32[13,32,128]{2,1,0:T(8,128)S(1)}, u32[]{:S(2)}, u32[]{:S(2)}) collective-permute-start(f32[13,32,128]{2,1,0:T(8,128)S(1)} %get-tuple-element.21), channel_id=1, source_target_pairs={{0,16},{8,24},{16,0},{24,8},{1,17},{9,25},{17,1},{25,9},{2,18},{10... | collective-permute-start | bytes 638984 | tf_op jit(solution)/shard_map/ppermute | solution.py:588
  14.7 10.6 %collective-permute-start.4 = (f32[13,32,128]{2,1,0:T(8,128)S(1)}, f32[13,32,128]{2,1,0:T(8,128)S(1)}, u32[]{:S(2)}, u32[]{:S(2)}) collective-permute-start(f32[13,32,128]{2,1,0:T(8,128)S(1)} %get-tuple-element.20), channel_id=1, source_target_pairs={{0,8},{8,16},{16,24},{24,0},{1,9},{9,17},{17,25},{25,1},{2,10},{10... | collective-permute-start | bytes 638984 | tf_op jit(solution)/shard_map/ppermute | solution.py:588
  14.9 10.2 %collective-permute-start.2 = (f32[8,40,128]{2,1,0:T(8,128)S(1)}, f32[8,40,128]{2,1,0:T(8,128)S(1)}, u32[]{:S(2)}, u32[]{:S(2)}) collective-permute-start(f32[8,40,128]{2,1,0:T(8,128)S(1)} %pad_maximum_fusion.1), channel_id=1, source_target_pairs={{0,24},{8,0},{16,8},{24,16},{1,25},{9,1},{17,9},{25,17},{2,26},{10... | collective-permute-start | bytes 491528 | tf_op jit(solution)/shard_map/ppermute | solution.py:588
  26.5 17.0 %copy-start.7 = (bf16[208,456]{1,0:T(8,128)(2,1)S(1)}, bf16[208,456]{1,0:T(8,128)(2,1)}, u32[]{:S(2)}) copy-start(bf16[208,456]{1,0:T(8,128)(2,1)} %constant.54.clone.refs_2_) | copy-start | bytes 569092
  26.5 17.0 %copy-start.11 = (bf16[4,72,40]{2,1,0:T(8,128)(2,1)S(1)}, bf16[4,72,40]{2,1,0:T(8,128)(2,1)}, u32[]{:S(2)}) copy-start(bf16[4,72,40]{2,1,0:T(8,128)(2,1)} %constant.60.clone.refs_8_) | copy-start | bytes 69124
  26.5 17.0 %copy-start.12 = (bf16[144,208]{1,0:T(8,128)(2,1)S(1)}, bf16[144,208]{1,0:T(8,128)(2,1)}, u32[]{:S(2)}) copy-start(bf16[144,208]{1,0:T(8,128)(2,1)} %constant.53.clone.refs_1_) | copy-start | bytes 179716
  26.5 17.0 %copy-start.13 = (bf16[4,40,24]{2,1,0:T(8,128)(2,1)S(1)}, bf16[4,40,24]{2,1,0:T(8,128)(2,1)}, u32[]{:S(2)}) copy-start(bf16[4,40,24]{2,1,0:T(8,128)(2,1)} %constant.59.clone.refs_7_) | copy-start | bytes 23044
  26.5 17.0 %copy-start.15 = (bf16[96,128]{1,0:T(8,128)(2,1)S(1)}, bf16[96,128]{1,0:T(8,128)(2,1)}, u32[]{:S(2)}) copy-start(bf16[96,128]{1,0:T(8,128)(2,1)} %constant.61.clone.refs_9_) | copy-start | bytes 73732
  26.5 17.0 %copy-start.16 = (f32[8,1,456]{2,1,0:T(1,128)S(1)}, f32[8,1,456]{2,1,0:T(1,128)}, u32[]{:S(2)}) copy-start(f32[8,1,456]{2,1,0:T(1,128)} %constant.58.clone.refs_6_) | copy-start | bytes 43780
  26.6 17.0 %copy-start.17 = (f32[8,1,208]{2,1,0:T(1,128)S(1)}, f32[8,1,208]{2,1,0:T(1,128)}, u32[]{:S(2)}) copy-start(f32[8,1,208]{2,1,0:T(1,128)} %constant.57.clone.refs_5_) | copy-start | bytes 19972
  26.6 17.0 %copy-start.18 = (f32[8,1,144]{2,1,0:T(1,128)S(1)}, f32[8,1,144]{2,1,0:T(1,128)}, u32[]{:S(2)}) copy-start(f32[8,1,144]{2,1,0:T(1,128)} %constant.56.clone.refs_4_) | copy-start | bytes 13828
  32.9 10.6 %collective-permute-start.7 = (f32[24,1024]{1,0:T(8,128)S(1)}, f32[24,1024]{1,0:T(8,128)S(1)}, u32[]{:S(2)}, u32[]{:S(2)}) collective-permute-start(f32[24,1024]{1,0:T(8,128)S(1)} %get-tuple-element.26), channel_id=1, source_target_pairs={{0,1},{1,2},{2,3},{3,0},{4,5},{5,6},{6,7},{7,4},{8,9},{9,10},{10,1... | collective-permute-start | bytes 294920 | tf_op jit(solution)/shard_map/ppermute | solution.py:588
  34.5 9.0 %collective-permute-start.8 = (f32[24,1024]{1,0:T(8,128)S(1)}, f32[24,1024]{1,0:T(8,128)S(1)}, u32[]{:S(2)}, u32[]{:S(2)}) collective-permute-start(f32[24,1024]{1,0:T(8,128)S(1)} %get-tuple-element.27), channel_id=1, source_target_pairs={{0,3},{1,0},{2,1},{3,2},{4,7},{5,4},{6,5},{7,6},{8,11},{9,8},{10,9... | collective-permute-start | bytes 294920 | tf_op jit(solution)/shard_map/ppermute | solution.py:588
  36.8 6.7 %collective-permute-start.9 = (f32[24,144]{1,0:T(8,128)S(1)}, f32[24,144]{1,0:T(8,128)S(1)}, u32[]{:S(2)}, u32[]{:S(2)}) collective-permute-start(f32[24,144]{1,0:T(8,128)S(1)} %get-tuple-element.28), channel_id=1, source_target_pairs={{0,2},{1,3},{2,0},{3,1},{4,6},{5,7},{6,4},{7,5},{8,10},{9,11},{10,... | collective-permute-start | bytes 41480 | tf_op jit(solution)/shard_map/ppermute | solution.py:588
  (5 other events, 20.9 us)

commit v2 on v1

v2 whole, which is shorter than its diff:
```python
import functools

import jax
import jax.numpy as jnp
import numpy as np
from jax import lax
from jax.experimental import pallas as pl
from jax.experimental.pallas import tpu as pltpu
from jax.sharding import PartitionSpec as P

REACH = 8
STENCIL_SIGMAS = (1.0, 2.0, 3.5)
STENCIL_WEIGHTS = (0.4, 0.1, 0.03)
TOP_SIGMAS = (1.5, 4.0)
TOP_WEIGHTS = (0.03, 0.006)
SPLINE_TAPS = np.array((-1.0, 0.0, 9.0, 16.0, 9.0, 0.0, -1.0)) / 16.0

LOW = (0, -1, -2, -2)
EXTRA = (0, 3, 5, 5)
FACE = 11
LANES = 128
BF = jnp.bfloat16
F32 = jnp.float32


def up(value, unit):
    return -(-value // unit) * unit


def band(rows, cols, sigma, reach):
    distance = cols[None, :] - rows[:, None]
    return np.where(abs(distance) <= reach, np.exp(-((distance / sigma) ** 2)), 0.0)


def restriction(size):
    position = np.arange(size)[None, :] - 2 * np.arange(size // 2)[:, None] + 3
    inside = (position >= 0) & (position <= 6)
    return np.where(inside, SPLINE_TAPS[np.clip(position, 0, 6)], 0.0)


class Axis:
    def __init__(self, count, length):
        self.count, self.length = count, length
        self.width = [(length >> level) + EXTRA[level] for level in range(4)]

    def window(self, level, brick):
        size = self.length >> level
        cells = brick * size + LOW[level] + np.arange(self.width[level])
        return cells, ((cells >= 0) & (cells < self.count * size)).astype(float)

    def partial(self, level, brick):
        matrix = np.eye(self.count * self.length)
        for _ in range(level):
            matrix = restriction(matrix.shape[0]) @ matrix
        cells, inside = self.window(level, brick)
        rows = matrix[np.clip(cells, 0, len(matrix) - 1)] * inside[:, None]
        return rows[:, brick * self.length : (brick + 1) * self.length]

    def prolong(self, level, brick):
        matrix = restriction((self.count * self.length) >> (level - 1)).T
        rows, row_inside = self.window(level - 1, brick)
        cols, col_inside = self.window(level, brick)
        taken = matrix[np.clip(rows, 0, len(matrix) - 1)][:, np.clip(cols, 0, matrix.shape[1] - 1)]
        return taken * row_inside[:, None] * col_inside[None, :]

    def mix(self, level, sigma, target, source):
        rows, row_inside = self.window(level, target)
        cols, col_inside = self.window(level, source)
        reach = REACH if level < 3 else self.count * self.length
        return band(rows, cols, sigma, reach) * row_inside[:, None] * col_inside[None, :]


def place(shape, *pieces):
    whole = np.zeros(shape)
    for row, col, block in pieces:
        whole[row : row + block.shape[0], col : col + block.shape[1]] += block
    return whole


def halves(matrix):
    high = matrix.astype(jnp.bfloat16)
    low = (matrix - high.astype(np.float64)).astype(jnp.bfloat16)
    return high, low


def left3(matrix):
    high, low = halves(matrix)
    return np.concatenate([high, low, high], axis=-1)


def left3t(matrix):
    high, low = halves(matrix)
    return np.concatenate([high, high, low], axis=-1)


def right3(matrix):
    high, low = halves(matrix)
    return np.concatenate([high, high, low], axis=-2)


def split(value):
    high = value.astype(BF)
    return high, (value - high.astype(F32)).astype(BF)


def dot(left, right, dims=((1,), (0,))):
    return lax.dot_general(left, right, (dims, ((), ())), preferred_element_type=F32)


class Plan:
    def __init__(self, counts, lengths):
        self.x, self.y, self.z = (Axis(n, length) for n, length in zip(counts, lengths))
        x, y, z = self.x, self.y, self.z
        assert x.count % 2 == 0 and x.count >= 4 and y.count % 2 == 0
        assert z.count >= 4 and z.count & (z.count - 1) == 0
        self.lane = [0, 0, z.width[1], z.width[1] + z.width[2]]
        self.lane_end = self.lane[3] + z.width[3]
        assert self.lane_end <= LANES and z.length == LANES
        self.rows1, self.rows2, self.rows3 = up(y.width[1], 8), up(y.width[2], 16), up(y.width[3], 16)
        assert self.rows2 <= 16 and self.rows3 <= 16 and FACE <= 14 and self.rows1 == 24
        self.row = [0, 0, self.rows1, self.rows1 + self.rows2]
        self.row_face = self.rows1 + self.rows2 + self.rows3
        self.kinds = 1 if y.count == 2 else 2
        self.rows_restricted = self.row_face + 16 * self.kinds
        self.overlay = y.count == 2 and y.width[1] + 3 <= self.rows1
        self.coarse_rows = up(24 + 16 * (y.count - 1), 16) if not self.overlay else 32
        self.fine_halos = 1 if y.count == 2 else 2
        self.fine_rows = y.length + 8 * self.fine_halos
        self.pair_width = [w + (x.length >> l) for l, w in enumerate(x.width)]
        self.planes = max(FACE, x.width[2], self.pair_width[3])
        assert self.planes <= x.width[1]
        self.group = [0, 0, 3 * self.rows1, 3 * self.rows1 + 3 * self.rows2]
        self.rows_mixed = up(self.group[3] + 2 * self.rows3, 16)
        self.tall = [0, up(z.width[1], 8), up(z.width[2], 8), up(z.width[3], 8)]
        assert self.tall[1] - 16 == z.width[1] - FACE and self.tall[2] - 16 == z.width[2] - 13
        self.flat = [0, x.width[1] * self.rows1, x.width[2] * self.rows2, x.width[3] * self.rows3]
        assert self.flat[1] <= 512 and self.flat[2] <= 256 and self.flat[3] <= 256

    def face_kind(self, axis, offset, source):
        if axis.count == 2:
            return 1 - source
        return 1 if offset == 1 else 0

    def near_y(self, halos):
        return [halos[0]] if self.y.count == 2 else [halos[0], halos[-1]]

    def pair_plane(self, ref, index):
        return plane(ref, self.fine_rows * REACH, self.coarse_rows, index)

    def face_row(self, j):
        return j if j < 8 or not self.overlay else j + 3

    def restrict_tables(self):
        rows = up(self.rows_restricted, 16)
        along_y = [place((rows, LANES), (0, 0, m)) for m in self.restrict_y().astype(np.float32)]
        along_z = list(self.restrict_z().astype(np.float32))
        return np.concatenate(along_z + along_y).astype(jnp.bfloat16).reshape(-1, 16, LANES)

    def y_tables(self):
        fine, coarse = self.fine_y(), self.coarse_y()
        cols = up(max(fine.shape[2], coarse.shape[2]), LANES)
        widen = lambda t: np.pad(t, ((0, 0), (0, 0), (0, cols - t.shape[2])))
        self.fine_cols, self.coarse_cols = fine.shape[2], coarse.shape[2]
        return np.concatenate([widen(fine), widen(coarse)], axis=1)

    def z_tables(self):
        tables = [*self.fine_z(), *[self.coarse_z(level) for level in (1, 2, 3)]]
        cols = 9 * LANES
        self.z_rows = np.cumsum([0] + [t.shape[1] for t in tables])
        return np.concatenate([np.pad(t, ((0, 0), (0, 0), (0, cols - t.shape[2]))) for t in tables], axis=1)

    def fine_matrix(self, ref):
        return ref[lax.axis_index("gy"), : 3 * self.y.length, :][:, : self.fine_cols]

    def coarse_matrix(self, ref):
        return ref[lax.axis_index("gy"), 3 * self.y.length :, :][:, : self.coarse_cols]

    def z_matrix(self, ref, number):
        cols = LANES * (6 if number == 4 else 9)
        return ref[lax.axis_index("gz"), int(self.z_rows[number]) : int(self.z_rows[number + 1]), :][:, :cols]

    def restrict_z(self):
        z = self.z
        return np.stack(
            [
                right3(place((z.length, LANES), *[(0, self.lane[l], z.partial(l, b).T) for l in (1, 2, 3)]))
                for b in range(z.count)
            ]
        )

    def restrict_y(self):
        y, tables = self.y, []
        for b in range(y.count):
            pieces = [(self.row[l], 0, y.partial(l, b)) for l in (1, 2, 3)]
            first = y.partial(1, b)
            for k in range(self.kinds):
                kind = self.face_kind(y, 1, b) if self.kinds == 1 else 1 - k
                start = (y.width[1] - FACE) * kind
                for j in range(FACE):
                    pieces.append((self.row_face + 16 * k + self.face_row(j), 0, first[start + j][None]))
            tables.append(left3(place((self.rows_restricted, y.length), *pieces)))
        return np.stack(tables)

    def fine_y(self):
        y, tables = self.y, []
        for b in range(y.count):
            pieces = []
            for s, sigma in enumerate(STENCIL_SIGMAS):
                row = s * y.length
                pieces.append((row, 0, y.mix(0, sigma, b, b)))
                for h in range(self.fine_halos):
                    offset = 1 if h == 0 else y.count - 1
                    source = (b - offset) % y.count
                    start = (y.length - REACH) * self.face_kind(y, offset, source)
                    block = y.mix(0, sigma, b, source)[:, start : start + REACH]
                    pieces.append((row, y.length + 8 * h, block))
            tables.append(left3(place((3 * y.length, up(self.fine_rows, 16)), *pieces)))
        return np.stack(tables)

    def coarse_y(self):
        y, tables = self.y, []
        for b in range(y.count):
            whole = np.zeros((self.rows_mixed, self.coarse_rows))
            for level in (1, 2, 3):
                sigmas = STENCIL_SIGMAS if level < 3 else TOP_SIGMAS
                rows = (0, self.rows1, self.rows2, self.rows3)[level]
                for s, sigma in enumerate(sigmas):
                    top = self.group[level] + s * rows
                    for offset in range(y.count):
                        source = (b - offset) % y.count
                        block = y.mix(level, sigma, b, source)
                        if level == 1 and offset:
                            start = (y.width[1] - FACE) * self.face_kind(y, offset, source)
                            block = block[:, start : start + FACE]
                        for j in range(block.shape[1]):
                            slot = self.face_row(j) if level == 1 and offset else j
                            if self.overlay and offset:
                                slot = 24 + slot if slot < 8 else 8 + slot
                            elif offset:
                                slot = 24 + 16 * (offset - 1) + slot
                            whole[top : top + y.width[level], slot] += block[:, j]
            tables.append(left3(whole))
        return np.stack(tables)

    def near_z(self, b, step):
        side = 1 if (b % 2 == 0) == (step == 0) else -1
        return side, b + side if 0 <= b + side < self.z.count else None

    def fine_z(self):
        z, own, pushed = self.z, [], []
        for b in range(z.count):
            mixes = lambda target: [
                w * z.mix(0, sigma, target, b) for sigma, w in zip(STENCIL_SIGMAS, STENCIL_WEIGHTS)
            ]
            own.append(left3t(np.concatenate(mixes(b), axis=1)))
            rows = []
            for step in (0, 1):
                side, target = self.near_z(b, step)
                if target is None:
                    rows.append(np.zeros((8, 3 * z.length)))
                else:
                    rows.append(np.concatenate([m[:8] if side > 0 else m[-8:] for m in mixes(target)], axis=1))
            pushed.append(left3t(np.concatenate(rows, axis=0)))
        return np.stack(own), np.stack(pushed)

    def coarse_z(self, level):
        z, tables = self.z, []
        sigmas, weights = (STENCIL_SIGMAS, STENCIL_WEIGHTS) if level < 3 else (TOP_SIGMAS, TOP_WEIGHTS)
        factor = 0.5**level if level < 3 else 1.0
        cols, tall = LANES * len(sigmas), self.tall[level]
        for b in range(z.count):

            def mixed(target):
                blocks = [
                    place((z.width[level], LANES), (0, self.lane[level], factor * w * z.mix(level, sigma, target, b)))
                    for sigma, w in zip(sigmas, weights)
                ]
                return np.concatenate(blocks, axis=1)

            pieces = [place((tall, cols), (0, 0, mixed(b)))]
            if level < 3:
                layers = FACE if level == 1 else 13
                for step in (0, 1):
                    side, target = self.near_z(b, step)
                    if target is None:
                        pieces.append(np.zeros((16, cols)))
                    else:
                        block = mixed(target)
                        pieces.append(place((16, cols), (0, 0, block[:layers] if side > 0 else block[-layers:])))
            else:
                block = mixed(b ^ 1)
                pieces.append(block[:16])
                pieces.append(place((16, cols), (FACE, 0, block[16:])))
                for m in range(2, z.count):
                    pieces.append(place((tall, cols), (0, 0, mixed(b ^ m))))
            whole = np.concatenate(pieces, axis=0)
            tables.append(left3t(place((up(len(whole), 16), cols), (0, 0, whole))))
        return np.stack(tables)

    def finish(self):
        x, y, z = self.x, self.y, self.z
        rows = (y.length, self.rows1, self.rows2, self.rows3)
        exact = lambda m: np.asarray(m, dtype=jnp.bfloat16)

        def free(axis, level):
            inner = Axis(5, axis.length)
            return inner.prolong(level, 2)

        flat = []
        for level in (3, 2, 1):
            q = place((rows[level], rows[level - 1]), (0, 0, free(y, level).T))
            flat.append(exact(np.kron(free(x, level).T, q)))
        joined = np.concatenate([np.pad(m, ((0, -len(m) % 16), (0, 1024 - m.shape[1]))) for m in flat])
        self.flat_rows = np.cumsum([0] + [up(len(m), 16) for m in flat])
        masks = np.zeros((x.count * y.count, 8, 512), np.float32)
        for level in (3, 2, 1):
            for bx in range(x.count):
                for by in range(y.count):
                    inside = np.zeros(rows[level])
                    inside[: y.width[level]] = y.window(level, by)[1]
                    line = np.kron(x.window(level, bx)[1], inside)
                    masks[bx * y.count + by, level, : len(line)] = line
        tall = []
        for b in range(z.count):
            ends = (0, z.length - 8) if b % 2 else (z.length - 8, 0)
            pieces = [(0, 0, free(z, 1).T)] + [(self.tall[1] + 8 * k, end, np.eye(8)) for k, end in enumerate(ends)]
            last = place((up(self.tall[1] + 16, 16), LANES), *pieces)
            parts = [place((up(self.tall[l - 1], 16), LANES), (0, 0, z.prolong(l, b))) for l in (3, 2)]
            tall.append(np.concatenate([last, *parts]))
        return joined, masks, exact(np.stack(tall))


def plane(ref, base, rows, index):
    return ref[pl.ds(base // 8 + rows // 8 * index, rows // 8)].reshape(rows, LANES)


def put_plane(ref, row, value):
    ref[row // 8 : (row + value.shape[0]) // 8] = value.reshape(value.shape[0] // 8, 8, LANES)


def restrict_kernel(plan, q_ref, table_ref, own_ref, *rest):
    targets, mixed = rest[: plan.kinds], rest[plan.kinds]
    nx, ny, nz = plan.x.length, plan.y.length, plan.z.length
    by, bz = lax.axis_index("gy"), lax.axis_index("gz")
    matrix_z = table_ref[pl.ds(3 * nz // 16 * bz, 3 * nz // 16)].reshape(3 * nz, LANES)
    rows = up(plan.rows_restricted, 16)
    matrix_y = table_ref[pl.ds(3 * nz // 16 * plan.z.count + rows // 16 * by, rows // 16)].reshape(rows, LANES)
    matrix_y = matrix_y[:, : 3 * ny]
    for i in range(nx):
        faces = [q_ref[i, ny - REACH :, :], q_ref[i, :REACH, :]]
        if plan.kinds == 1:
            faces = [jnp.where(by == 0, *faces)]
        for face, ref in zip(faces, targets):
            ref[i] = face
    high, low = split(q_ref[...].reshape(nx * ny, nz))
    along_z = dot(jnp.concatenate([high, low, high], axis=1), matrix_z)
    high, low = split(along_z)
    high, low = high.reshape(nx, ny, LANES), low.reshape(nx, ny, LANES)
    for i in range(0, nx, 2):
        pair = [jnp.concatenate([high[j], high[j], low[j]], axis=0) for j in (i, i + 1)]
        both = dot(matrix_y, jnp.concatenate(pair, axis=1))[: plan.rows_restricted]
        mixed[i] = both[:, :LANES]
        mixed[i + 1] = both[:, LANES:]

    brick = lax.axis_index("gx")
    keep_low = jnp.where(brick > 0, 1.0, 0.0).astype(F32)
    keep_high = jnp.where(brick < plan.x.count - 1, 1.0, 0.0).astype(F32)

    def coarsen(planes, level):
        size = nx >> level
        result = {}
        for i in range(LOW[level], LOW[level] + plan.x.width[level]):
            get = lambda j: planes.get(2 * i + j)
            total = None
            for offsets, weight in (((-3, 3), -0.0625), ((-1, 1), 0.5625), ((0,), 1.0)):
                terms = [get(j) for j in offsets if get(j) is not None]
                if terms:
                    term = functools.reduce(jnp.add, terms)
                    term = term * weight if weight != 1.0 else term
                    total = term if total is None else total + term
            if i < 0:
                total = total * keep_low
            elif i >= size:
                total = total * keep_high
            result[i] = total
        return result

    lanes = lax.broadcasted_iota(jnp.int32, (8, LANES), 1)
    in1, in2 = lanes < plan.lane[2], lanes < plan.lane[3]

    def tile(planes, level, k, row):
        index = LOW[level] + k
        return planes[row][index] if k < plan.x.width[level] else None

    def rows_of(start, count, depth):
        levels = [{i: mixed[i, start : start + count, :] for i in range(nx)}]
        for level in range(1, depth + 1):
            levels.append(coarsen(levels[-1], level))
        return levels[-1]

    zero = jnp.zeros((8, LANES), F32)
    first = {r: rows_of(r, 8, 1) for r in range(0, plan.rows1, 8)}
    second = {r: rows_of(plan.row[2] + r, 8, 2) for r in (0, 8)}
    third = {r: rows_of(plan.row[3] + r, 8, 3) for r in (0, 8)}
    face = [{r: rows_of(plan.row_face + 16 * f + r, 8, 1) for r in (0, 8)} for f in range(plan.kinds)]
    for k in range(plan.x.width[1]):
        for r in range(0, plan.rows1, 8):
            one = first[r][LOW[1] + k]
            two = second[r][LOW[2] + k] if r < 16 and k < plan.x.width[2] else zero
            three = third[r][LOW[3] + k] if r < 16 and k < plan.x.width[3] else zero
            rest_ = jnp.where(in2, two, three)
            own_ref[k, r : r + 8, :] = jnp.where(in1, one, rest_)
            if r < 16:
                for f in range(plan.kinds):
                    targets[f][nx + 2 * k + r // 8] = jnp.where(in1, face[f][r][LOW[1] + k], rest_)


def mask(condition):
    return jnp.where(condition, 1.0, 0.0).astype(F32)


def extend_kernel(plan, q_ref, own_ref, *refs):
    count = plan.y.count - 1
    halos, (ext_ref, partner_ref, side_ref) = refs[:count], refs[count:]
    x, y = plan.x, plan.y
    odd = lax.axis_index("gx") % 2
    end = x.length - REACH
    near = plan.near_y(halos)
    for start, ref in ((end * odd, side_ref), (end * (1 - odd), partner_ref)):
        for i in range(REACH):
            row = plan.fine_rows * i
            put_plane(ref, row, q_ref[start + i])
            for h, halo in enumerate(near):
                ref[(row + y.length) // 8 + h] = halo[start + i]

    base = [0 if halo.shape[0] == 2 * x.width[1] else 8 * x.length for halo in halos]
    for i in range(x.width[1]):
        own = own_ref[i]
        parts = [plane(halo, at, 16, i) for halo, at in zip(halos, base)]
        if plan.overlay:
            halo = parts[0]
            parts = [own[:16], own[16:] + halo[8:], halo[:8]]
        else:
            pad = plan.coarse_rows - 24 - 16 * count
            parts = [own] + parts + ([jnp.zeros((pad, LANES), F32)] if pad else [])
        ext_ref[i] = jnp.concatenate(parts, axis=0)
    lanes = lax.broadcasted_iota(jnp.int32, (1, LANES), 1)
    start = (x.width[1] - FACE) * (1 - odd)
    for p in range(plan.planes):
        row = plan.fine_rows * REACH + plan.coarse_rows * p
        value = jnp.where(lanes < plan.lane[2], ext_ref[start + min(p, FACE - 1)], ext_ref[p])
        put_plane(partner_ref, row, value)


def chip_kernel(plan, ext_ref, pair_ref, *targets):
    x, gx = plan.x, lax.axis_index("gx")
    odd, chip = gx % 2, gx // 2
    lanes = lax.broadcasted_iota(jnp.int32, (1, LANES), 1)
    in1, in2 = lanes < plan.lane[2], lanes < plan.lane[3]
    keep_even, keep_odd = mask(odd == 0), mask(odd == 1)

    def merged(level, cell):
        size, total = x.length >> level, None
        for where_own, where_partner, at in ((keep_even, keep_odd, cell), (keep_odd, keep_even, cell - size)):
            if 0 <= at < x.width[level]:
                value = ext_ref[at] * where_own + plan.pair_plane(pair_ref, at) * where_partner
                total = value if total is None else total + value
        return total

    second = [merged(2, c) for c in range(plan.pair_width[2])]
    third = [merged(3, c) for c in range(plan.pair_width[3])]
    start = (x.width[1] - FACE) * odd
    chips = x.count // 2
    for k, ref in zip(range(1, chips), targets):
        high = x.length >> 2
        for p in range(plan.planes):
            if chips == 2:
                two = jnp.where(chip == 0, second[high + p], second[p])
            else:
                two = second[high + p] if k == 1 else second[p]
            first = ext_ref[start + min(p, FACE - 1)]
            ref[p] = jnp.where(in1, first, jnp.where(in2, two, third[p]))


def mix_planes(get, put, count, matrix):
    for i in range(0, count, 2):
        pair = [i, min(i + 1, count - 1)]
        stacked = []
        for j in pair:
            high, low = split(get(j))
            stacked.append(jnp.concatenate([high, high, low], axis=0))
        both = dot(matrix, jnp.concatenate(stacked, axis=1))
        put(i, both[:, :LANES])
        if pair[1] != i:
            put(pair[1], both[:, LANES:])


def stencil(cells, wanted, sigma, reach=REACH):
    result = []
    for i in wanted:
        total = cells.get(i)
        for k in range(1, reach + 1):
            terms = [cells[j] for j in (i - k, i + k) if j in cells]
            if terms:
                term = functools.reduce(jnp.add, terms) * float(np.exp(-((k / sigma) ** 2)))
                total = term if total is None else total + term
        result.append(total)
    return result


def put_ready(ready, sigmas, s, row, value):
    high, low = split(value)
    rows = slice(row, row + value.shape[0])
    step = LANES * sigmas
    ready[rows, s * LANES : (s + 1) * LANES] = high
    ready[rows, step + s * LANES : step + (s + 1) * LANES] = low
    ready[rows, 2 * step + s * LANES : 2 * step + (s + 1) * LANES] = high


def fine_padding(plan):
    pad = up(plan.fine_rows, 16) - plan.fine_rows
    return [jnp.zeros((pad, LANES), F32)] if pad else []


def fine_inner_kernel(plan, q_ref, y_table, z_table, *refs):
    refs = list(refs)
    take = lambda n: [refs.pop(0) for _ in range(n)]
    halos = take(plan.y.count - 1)
    main_ref, push_ref, edge_ref = take(3)
    mixed, ready = refs
    x, y = plan.x, plan.y
    padding = fine_padding(plan)

    def get(i):
        return jnp.concatenate([q_ref[i]] + [plane(h, 0, 8, i) for h in plan.near_y(halos)] + padding, axis=0)

    def put(i, value):
        mixed[i] = value

    mix_planes(get, put, x.length, plan.fine_matrix(y_table))
    inner = range(REACH, x.length - REACH)
    edge = [*range(REACH), *range(x.length - REACH, x.length)]
    for s, sigma in enumerate(STENCIL_SIGMAS):
        for r in range(0, y.length, 16):
            row = s * y.length + r
            planes = {i: mixed[i, row : row + 16, :] for i in range(x.length)}
            for i, value in zip(inner, stencil(planes, inner, sigma)):
                put_ready(ready, 3, s, (i - REACH) * y.length + r, value)
            for i, value in enumerate(stencil(planes, edge, sigma)):
                edge_ref[i, row : row + 16, :] = value
    main_ref[...] = dot(ready[...], plan.z_matrix(z_table, 0), ((1,), (1,)))
    push_ref[...] = dot(plan.z_matrix(z_table, 1), ready[...], ((1,), (1,)))


def fine_edge_kernel(plan, partner_ref, side_ref, edge_ref, inner_ref, y_table, z_table, *refs):
    main_ref, push_ref, mixed, ready = refs
    x, y = plan.x, plan.y
    gx = lax.axis_index("gx")
    odd = gx % 2 == 1
    from_partner = mask(odd), mask(~odd)
    from_side = mask(~odd & (gx > 0)), mask(odd & (gx < x.count - 1))
    padding = fine_padding(plan)

    def get(i):
        blocks = []
        for k in range(plan.fine_rows // 8):
            at = plan.fine_rows // 8 * (i % REACH) + k
            blocks.append(partner_ref[at] * from_partner[i // REACH] + side_ref[at] * from_side[i // REACH])
        return jnp.concatenate(blocks + padding, axis=0)

    def put(i, value):
        mixed[i] = value

    mix_planes(get, put, 2 * REACH, plan.fine_matrix(y_table))
    for s, sigma in enumerate(STENCIL_SIGMAS):
        for r in range(0, y.length, 16):
            row = s * y.length + r
            at = lambda i: mixed[i, row : row + 16, :]
            before = {k - REACH: at(k) for k in range(REACH)}
            after = {x.length + k: at(REACH + k) for k in range(REACH)}
            added = stencil(before, range(REACH), sigma)
            added += stencil(after, range(x.length - REACH, x.length), sigma)
            for i, value in enumerate(added):
                put_ready(ready, 3, s, i * y.length + r, edge_ref[i, row : row + 16, :] + value)
    main_ref[...] = dot(ready[...], plan.z_matrix(z_table, 0), ((1,), (1,)))
    pushed = dot(plan.z_matrix(z_table, 1), ready[...], ((1,), (1,)))
    half = pushed.shape[1] // 2
    push_ref[...] = jnp.concatenate([pushed[:, :half], inner_ref[...], pushed[:, half:]], axis=1)


def coarse_inner_kernel(plan, ext_ref, pair_ref, y_table, mixed):
    own = plan.x.width[1]

    def put(i, value):
        mixed[i] = value

    mix_planes(lambda i: ext_ref[i] if i < own else plan.pair_plane(pair_ref, i - own), put, own + plan.planes, plan.coarse_matrix(y_table))


def collect(plan, level, inner, outer, row, rows):
    x, gx = plan.x, lax.axis_index("gx")
    odd, chip, chips = gx % 2, gx // 2, plan.x.count // 2
    size, width = x.length >> level, x.width[level]
    start = LOW[level]
    reach = REACH if level < 3 else x.count * x.length
    cells = {start + k: inner[k, row : row + rows, :] for k in range(width)}

    def add(cell, value, keep):
        if start - reach <= cell < start + width + reach:
            value = value * keep
            cells[cell] = cells[cell] + value if cell in cells else value

    own = x.width[1]
    layers = FACE if level == 1 else width
    for k in range(layers):
        value = inner[own + k, row : row + rows, :]
        add(size + start + k, value, mask(odd == 0))
        add(-size + start + width - layers + k, value, mask(odd == 1))
    for offset in range(1, chips):
        base = plan.planes * (offset - 1)
        at = lambda k: outer[base + k, row : row + rows, :]
        for shift, here in ((-offset, chip >= offset), (chips - offset, chip < offset)):
            if level < 3 and abs(shift) != 1:
                continue
            if level == 1:
                keep = mask(here & (odd == (0 if shift < 0 else 1)))
                first = -size + start + width - FACE if shift < 0 else size + start
                for k in range(FACE):
                    add(first + k, at(k), keep)
                continue
            for core in (0, 1):
                keep = mask(here & (odd == core))
                first = 2 * size * shift - size * core + start
                if level == 2 and shift < 0:
                    first += size
                for k in range(plan.planes if level == 2 else plan.pair_width[3]):
                    add(first + k, at(k), keep)
    return cells


def top_kernel(plan, inner, *refs):
    refs = list(refs)
    take = lambda n: [refs.pop(0) for _ in range(n)]
    chips, (y_table, z_table) = take(plan.x.count // 2 - 1), take(2)
    outer, own_ref, partner_ref = take(3)
    far, ready = take(plan.z.count - 2), refs[0]

    def put(i, value):
        outer[i] = value

    mix_planes(lambda i: chips[i // plan.planes][i % plan.planes], put, plan.planes * len(chips), plan.coarse_matrix(y_table))
    start, width, rows = LOW[3], plan.x.width[3], plan.rows3
    for s, sigma in enumerate(TOP_SIGMAS):
        for r in range(0, rows, 8):
            cells = collect(plan, 3, inner, outer, plan.group[3] + s * rows + r, 8)
            reach = max(cells) - min(cells)
            for i, value in enumerate(stencil(cells, range(start, start + width), sigma, reach)):
                put_ready(ready, 2, s, i * rows + r, value)
    three = dot(plan.z_matrix(z_table, 4), ready[...], ((1,), (1,)))
    tall = plan.tall[3]
    own_ref[...] = three[:tall]
    partner_ref[...] = three[tall : tall + 32]
    for m, ref in enumerate(far):
        ref[...] = three[tall * (m + 1) + 32 : tall * (m + 2) + 32]


def coarse_kernel(plan, inner, outer, top_ref, push_ref, z_table, *refs):
    partner_ref, side_ref, e1_ref, e2_ref, *ready = refs
    x = plan.x
    results = []
    for level in (1, 2):
        rows = plan.rows1 if level == 1 else plan.rows2
        wanted = range(LOW[level], LOW[level] + x.width[level])
        for s, sigma in enumerate(STENCIL_SIGMAS):
            for r in range(0, rows, 8):
                cells = collect(plan, level, inner, outer, plan.group[level] + s * rows + r, 8)
                for i, value in enumerate(stencil(cells, wanted, sigma)):
                    put_ready(ready[level - 1], 3, s, i * rows + r, value)
        results.append(dot(plan.z_matrix(z_table, level + 1), ready[level - 1][...], ((1,), (1,))))
    one, two = results
    e1_ref[...] = one[: plan.tall[1]]
    e2_ref[...] = two[: plan.tall[2]]
    for n, ref in enumerate((partner_ref, side_ref)):
        ref[:8, :] = push_ref[8 * n : 8 * n + 8, :]
        ref[8:, :] = jnp.zeros((16, ref.shape[1]), F32)
        start = plan.tall[1] + 16 * n
        ref[8:, : plan.flat[1]] = one[start : start + 16]
        start = plan.tall[2] + 16 * n
        ref[8:, 512 : 512 + plan.flat[2]] = two[start : start + 16]
    partner_ref[8:, : plan.flat[3]] += top_ref[16:]
    partner_ref[8:, 768 : 768 + plan.flat[3]] = top_ref[:16]


def finish_kernel(plan, inner_ref, edge_ref, e1_ref, e2_ref, e3_ref, *refs):
    z = plan.z
    refs = list(refs)
    partner_ref, side_ref, *far = [refs.pop(0) for _ in range(z.count)]
    flat, masks, tall, out_ref, e1, e2, e3 = refs
    bz = lax.axis_index("gz")
    column = lax.axis_index("gx") * plan.y.count + lax.axis_index("gy")
    odd = bz % 2
    spread_cols = plan.x.length * plan.y.length
    keep = lambda level: masks[column, level : level + 1, : plan.flat[level]]
    bounds = [int(r) for r in plan.flat_rows]
    flat3, flat2, flat1 = (
        flat[bounds[k] : bounds[k + 1], :][: plan.flat[3 - k], :cols]
        for k, cols in enumerate((plan.flat[2], plan.flat[1], spread_cols))
    )
    e1[...], e2[...], e3[...] = e1_ref[...], e2_ref[...], e3_ref[...]
    for f in far:
        e3[...] += f[...]
    e3[:16, :] += partner_ref[8:24, 768 : 768 + plan.flat[3]]
    e3[16 : z.width[3], :] += partner_ref[8 + FACE : 8 + FACE + z.width[3] - 16, : plan.flat[3]]
    kept = lax.broadcasted_iota(jnp.int32, (16, 1), 0) < FACE
    for ref, high in ((partner_ref, odd == 0), (side_ref, odd == 1)):
        one = jnp.where(kept, ref[8:, : plan.flat[1]], 0.0)
        two = ref[8:, 512 : 512 + plan.flat[2]]
        for window, value, tall_ in ((e1, one, plan.tall[1]), (e2, two, plan.tall[2])):
            window[:16, :] += value * mask(~high)
            window[tall_ - 16 :, :] += value * mask(high)

    def across(value, matrix):
        high, low = split(value)
        both = dot(jnp.concatenate([high, low], axis=0), matrix)
        return both[: value.shape[0]] + both[value.shape[0] :]

    def along(matrix, value):
        high, low = split(value)
        return dot(matrix, high) + dot(matrix, low)

    top = up(plan.tall[1] + 16, 16)
    middle = top + up(plan.tall[2], 16)
    tall3 = tall[bz, top:middle, :][: plan.tall[2], : plan.tall[3]]
    tall2 = tall[bz, middle:, :][: plan.tall[1], : plan.tall[2]]
    last = tall[bz, :top, :]
    three = e3[...] * keep(3)
    two = (e2[...] + along(tall3, across(three, flat3))) * keep(2)
    one = (e1[...] + along(tall2, across(two, flat2))) * keep(1)
    spread = across(one, flat1)
    rows = jnp.concatenate([spread, partner_ref[:8], side_ref[:8]], axis=0)
    pad = last.shape[0] - rows.shape[0]
    if pad:
        rows = jnp.concatenate([rows, jnp.zeros((pad, rows.shape[1]), F32)], axis=0)
    high, low = split(rows)
    stacked = jnp.concatenate([high, low], axis=0)
    matrix = jnp.concatenate([last, last], axis=0)
    coarse = dot(stacked, matrix, ((0,), (0,)))
    edge = REACH * plan.y.length
    end = coarse.shape[0] - edge
    out_ref[:edge] = coarse[:edge] + edge_ref[:edge]
    out_ref[edge:end] = coarse[edge:end] + inner_ref[...]
    out_ref[end:] = coarse[end:] + edge_ref[edge:]


def call(kernel, plan, operands, outs, scratch=()):
    whole = pl.BlockSpec(memory_space=pltpu.VMEM)
    return pl.pallas_call(
        functools.partial(kernel, plan),
        in_specs=[whole] * len(operands),
        out_specs=[whole] * len(outs),
        scratch_shapes=list(scratch),
        out_shape=list(outs),
        compiler_params=pltpu.CompilerParams(vmem_limit_bytes=32 * 2**20),
    )(*[jnp.asarray(o) for o in operands])


def shift(value, axis, offset):
    count = lax.axis_size(axis)
    return lax.ppermute(value, axis, [(i, (i + offset) % count) for i in range(count)])


def swap(value, axes, partner):
    first, second = (lax.axis_size(a) for a in axes)
    pairs = []
    for i in range(first):
        for j in range(second):
            k, m = partner(i, j)
            pairs.append((i * second + j, k * second + m))
    return lax.ppermute(value, axes, pairs)


def side_of(count):
    return lambda i: None if i in (0, count - 1) else i + (1 if i % 2 else -1)


def shards(plan, charges):
    x, y, z = plan.x, plan.y, plan.z
    array = lambda *shape: jax.ShapeDtypeStruct(shape, F32)
    vmem = lambda *shape: pltpu.VMEM(shape, F32)
    ready = lambda rows, sigmas: pltpu.VMEM((rows, 3 * sigmas * LANES), BF)
    side_x, side_z = side_of(x.count), side_of(z.count)
    partner_x = lambda v: swap(v, ("gx", "gy"), lambda i, j: (i ^ 1, j))
    across_x = lambda v: swap(v, ("gx", "gy"), lambda i, j: (i, j ^ 1) if side_x(i) is None else (side_x(i), j))
    partner_z = lambda v: swap(v, ("gx", "gz"), lambda i, j: (i, j ^ 1))
    across_z = lambda v: swap(v, ("gx", "gz"), lambda i, j: (i ^ 1, j) if side_z(j) is None else (i, side_z(j)))

    rows_y = 8 * x.length + 16 * x.width[1]
    own, *to_y = call(
        restrict_kernel,
        plan,
        [charges, plan.restrict_tables()],
        [array(x.width[1], plan.rows1, LANES)] + [array(rows_y // 8, 8, LANES)] * plan.kinds,
        [vmem(x.length, plan.rows_restricted, LANES)],
    )
    from_y = []
    for offset in range(1, y.count):
        value = to_y[0 if offset == 1 else -1]
        value = value if offset in (1, y.count - 1) else value[x.length :]
        from_y.append(shift(value, "gy", offset))

    ext, to_partner, to_side = call(
        extend_kernel,
        plan,
        [charges, own, *from_y],
        [
            array(x.width[1], plan.coarse_rows, LANES),
            array((REACH * plan.fine_rows + plan.planes * plan.coarse_rows) // 8, 8, LANES),
            array(REACH * plan.fine_rows // 8, 8, LANES),
        ],
    )
    from_side, pair = across_x(to_side), partner_x(to_partner)

    y_table, z_table = plan.y_tables(), plan.z_tables()
    inner_cells = (x.length - 2 * REACH) * y.length
    edge_cells = 2 * REACH * y.length
    main_inner, push_inner, edge = call(
        fine_inner_kernel,
        plan,
        [charges, y_table, z_table, *from_y],
        [array(inner_cells, z.length), array(16, inner_cells), array(2 * REACH, 3 * y.length, LANES)],
        [vmem(x.length, 3 * y.length, LANES), ready(inner_cells, 3)],
    )

    chips = x.count // 2
    to_chips = call(chip_kernel, plan, [ext, pair], [array(plan.planes, plan.coarse_rows, LANES)] * (chips - 1))
    from_chips = [
        swap(v, ("gx", "gy"), lambda i, j, k=k: ((i + 2 * k) % x.count ^ 1, j))
        for k, v in zip(range(1, chips), to_chips)
    ]
    planes_inner = x.width[1] + plan.planes
    (mixed_inner,) = call(
        coarse_inner_kernel, plan, [ext, pair, y_table], [array(planes_inner, plan.rows_mixed, LANES)]
    )

    main_edge, push = call(
        fine_edge_kernel,
        plan,
        [pair, from_side, edge, push_inner, y_table, z_table],
        [array(edge_cells, z.length), array(16, x.length * y.length)],
        [vmem(2 * REACH, 3 * y.length, LANES), ready(edge_cells, 3)],
    )
    planes_outer = plan.planes * (chips - 1)
    window = lambda level: array(plan.tall[level], plan.flat[level])
    mixed_outer, e3, top_partner, *far = call(
        top_kernel,
        plan,
        [mixed_inner, *from_chips, y_table, z_table],
        [array(planes_outer, plan.rows_mixed, LANES), window(3), array(32, plan.flat[3])]
        + [window(3)] * (z.count - 2),
        [ready(plan.flat[3], 2)],
    )
    from_far = [swap(f, ("gx", "gz"), lambda i, j, m=m: (i, j ^ m)) for m, f in zip(range(2, z.count), far)]
    to_partner, to_side, e1, e2 = call(
        coarse_kernel,
        plan,
        [mixed_inner, mixed_outer, top_partner, push, z_table],
        [array(24, 1024), array(24, 1024), window(1), window(2)],
        [ready(plan.flat[1], 3), ready(plan.flat[2], 3)],
    )
    from_near = [partner_z(to_partner), across_z(to_side)]

    (potential,) = call(
        finish_kernel,
        plan,
        [main_inner, main_edge, e1, e2, e3, *from_near, *from_far, *plan.finish()],
        [array(x.length * y.length, z.length)],
        [vmem(plan.tall[level], plan.flat[level]) for level in (1, 2, 3)],
    )
    return potential.reshape(charges.shape)


def solution(mesh):
    counts = [mesh.shape[name] for name in ("gx", "gy", "gz")]

    def run(charges):
        plan = Plan(counts, [size // n for size, n in zip(charges.shape, counts)])
        placed = P("gx", "gy", "gz")
        return jax.shard_map(
            functools.partial(shards, plan), mesh=mesh, in_specs=(placed,), out_specs=placed, check_vma=False
        )(charges)

    return run
```

time: 46 us -> 38.6 us (0.84)
  waiting for transfers between devices: 20.1 us -> 11.4 us
  starting transfers between devices: 11.3 us -> 13.3 us
  other arithmetic: 1.01 us -> 0 us
    ppermute x10 -> x1, waiting for transfers between devices: 20.1 us -> 6.83 us  [shift(): lax.ppermute(value, axis, [(i, (i + offset) % count) for i in range(count)])]
    ppermute x0 -> x7, starting transfers between devices: none -> 10.3 us  [swap(): return lax.ppermute(value, axes, pairs)]
    ppermute x10 -> x1, starting transfers between devices: 11.3 us -> 3 us  [shift(): lax.ppermute(value, axis, [(i, (i + offset) % count) for i in range(count)])]
    ppermute x0 -> x7, waiting for transfers between devices: none -> 4.62 us  [swap(): return lax.ppermute(value, axes, pairs)]
    select_n x1 -> x0, other arithmetic: 0.99 us -> none  [shards(): fine_y = [shift(jnp.where(at_y == 0, faces[1], faces[0]), 'gy', 1)]]
    unnamed x38 -> x18, local copies, waits for them, and re-layouts: 3.97 us -> 4.25 us
    pallas_call x4 -> x9, Pallas kernels: 9 us -> 9.17 us  [call(): pl.pallas_call(functools.partial(kernel, plan), in_specs=[whole] * len(op...]
  transfers between devices with their start and end apart: 10 -> 8, of which waited for: 4 -> 4; matrix products, arithmetic and copies ran while one was open for 0% -> 0% of each run, Pallas kernels for 1% -> 10%
where the time goes in v2:
time: 38.6 us; the launch traced here: 38.3 us
  starting transfers between devices  13.3 us (34%)
  waiting for transfers between devices  11.4 us (30%)
  Pallas kernels  9.17 us (24%)
  local copies, waits for them, and re-layouts  4.25 us (11%)
    ppermute x7, starting transfers between devices, swap(): return lax.ppermute(value, axes, pairs)  10.3 us
    pallas_call x9, Pallas kernels, call(): pl.pallas_call(functools.partial(kernel, plan), in_specs=[whole] * len(op...  9.17 us
    ppermute x1, waiting for transfers between devices, shift(): lax.ppermute(value, axis, [(i, (i + offset) % count) for i in range(count)])  6.83 us
    ppermute x7, waiting for transfers between devices, swap(): return lax.ppermute(value, axes, pairs)  4.62 us
    unnamed x18, local copies, waits for them, and re-layouts  4.25 us
    ppermute x1, starting transfers between devices, shift(): lax.ppermute(value, axis, [(i, (i + offset) % count) for i in range(count)])  3 us
  transfers between devices with their start and end apart: 8, of which 4 were waited for; matrix products, arithmetic and copies ran while one was open for 0% of the time, Pallas kernels for 10%

profile of v2, /device:TPU:0, one launch (start us, length us, event | category | flops | bytes accessed | tf_op | source)
XLA Modules:
  0.0 38.3 jit_solution(15057254982713080723)
XLA Ops:
  0.0 1.0 %copy-done.2 = f32[32,32,128]{2,1,0:T(8,128)S(1)} copy-done((f32[32,32,128]{2,1,0:T(8,128)S(1)}, f32[32,32,128]{2,1,0:T(8,128)}, u32[]{:S(2)}) %copy-start.2) | copy-done | bytes 524312
  1.0 1.0 %copy-done.6 = bf16[106,16,128]{2,1,0:T(8,128)(2,1)S(1)} copy-done((bf16[106,16,128]{2,1,0:T(8,128)(2,1)S(1)}, bf16[106,16,128]{2,1,0:T(8,128)(2,1)}, u32[]{:S(2)}) %copy-start.6) | copy-done | bytes 434200
  2.1 0.6 %shard_map.73 = (f32[19,24,128]{2,1,0:T(8,128)S(1)}, f32[70,8,128]{2,1,0:T(8,128)S(1)}) custom-call(f32[32,32,128]{2,1,0:T(8,128)S(1)} %copy-done.2, bf16[106,16,128]{2,1,0:T(8,128)(2,1)S(1)} %copy-done.6), custom_call_target="tpu_custom_call" | custom-call | tf_op jit(solution)/shard_map/pallas_call | solution.py:757
  2.7 3.0 %collective-permute-start = (f32[70,8,128]{2,1,0:T(8,128)S(1)}, f32[70,8,128]{2,1,0:T(8,128)S(1)}, u32[]{:S(2)}, u32[]{:S(2)}) collective-permute-start(f32[70,8,128]{2,1,0:T(8,128)S(1)} %get-tuple-element.24), channel_id=1, source_target_pairs={{0,4},{4,0},{1,5},{5,1},{2,6},{6,2},{3,7},{7,3},{8,12},{12,8},{9,1... | collective-permute-start | bytes 860168 | tf_op jit(solution)/shard_map/ppermute | solution.py:769
  5.7 6.8 %collective-permute-done.refs_0_ = f32[70,8,128]{2,1,0:T(8,128)S(1)} collective-permute-done((f32[70,8,128]{2,1,0:T(8,128)S(1)}, f32[70,8,128]{2,1,0:T(8,128)S(1)}, u32[]{:S(2)}, u32[]{:S(2)}) %collective-permute-start) | collective-permute-done | bytes 286752 | tf_op jit(solution)/shard_map/ppermute | solution.py:769
  12.5 0.1 shard_map.75
  12.6 0.1 collective-permute-start.1
  12.7 1.7 %collective-permute-done.1.partner_ref.pair_ref = f32[92,8,128]{2,1,0:T(8,128)S(1)} collective-permute-done((f32[92,8,128]{2,1,0:T(8,128)S(1)}, f32[92,8,128]{2,1,0:T(8,128)S(1)}, u32[]{:S(2)}, u32[]{:S(2)}) %collective-permute-start.1) | collective-permute-done | bytes 376864 | tf_op jit(solution)/shard_map/ppermute | solution.py:779
  14.3 0.1 shard_map.78
  14.4 1.6 %collective-permute-start.3 = (f32[13,32,128]{2,1,0:T(8,128)S(1)}, f32[13,32,128]{2,1,0:T(8,128)S(1)}, u32[]{:S(2)}, u32[]{:S(2)}) collective-permute-start(f32[13,32,128]{2,1,0:T(8,128)S(1)} %shard_map.78), channel_id=1, source_target_pairs={{0,24},{4,28},{8,16},{12,20},{16,8},{20,12},{24,0},{28,4},{1,25},{... | collective-permute-start | bytes 638984 | tf_op jit(solution)/shard_map/ppermute | solution.py:779
  16.0 1.5 %collective-permute-start.2 = (f32[40,8,128]{2,1,0:T(8,128)S(1)}, f32[40,8,128]{2,1,0:T(8,128)S(1)}, u32[]{:S(2)}, u32[]{:S(2)}) collective-permute-start(f32[40,8,128]{2,1,0:T(8,128)S(1)} %get-tuple-element.28), channel_id=1, source_target_pairs={{0,4},{4,0},{8,16},{12,20},{16,8},{20,12},{24,28},{28,24},{1,5},{5... | collective-permute-start | bytes 491528 | tf_op jit(solution)/shard_map/ppermute | solution.py:779
  17.5 2.2 %copy-done = bf16[4,448,1152]{2,1,0:T(8,128)(2,1)S(1)} copy-done((bf16[4,448,1152]{2,1,0:T(8,128)(2,1)S(1)}, bf16[4,448,1152]{2,1,0:T(8,128)(2,1)}, u32[]{:S(2)}) %copy-start) | copy-done | bytes 4128792
  19.7 2.1 %shard_map.74 = (f32[512,128]{1,0:T(8,128)S(1)}, f32[16,512]{1,0:T(8,128)S(1)}, f32[16,96,128]{2,1,0:T(8,128)S(1)}) custom-call(f32[32,32,128]{2,1,0:T(8,128)S(1)} %copy-done.3, bf16[2,256,256]{2,1,0:T(8,128)(2,1)S(1)} %copy-done.4, bf16[4,448,1152]{2,1,0:T(8,128)(2,1)S(1)} %copy-done, f32[70,8,128]{2,1,0:T(8,128)S(1)} %collective-permute-done.refs_0_), custom_call_target="tpu_custom_call" | custom-call | tf_op jit(solution)/shard_map/pallas_call | solution.py:757
  21.8 0.5 %shard_map.77.inner = f32[32,160,128]{2,1,0:T(8,128)S(1)} custom-call(f32[19,32,128]{2,1,0:T(8,128)S(1)} %get-tuple-element.32.ext_ref, f32[92,8,128]{2,1,0:T(8,128)S(1)} %collective-permute-done.1.partner_ref.pair_ref, bf16[2,256,256]{2,1,0:T(8,128)(2,1)S(1)} %copy-done.4), custom_call_target="tpu_custom_call" | custom-call | tf_op jit(solution)/shard_map/pallas_call | solution.py:757
  22.3 1.2 %shard_map.76 = (f32[512,128]{1,0:T(8,128)S(1)}, f32[16,1024]{1,0:T(8,128)S(1)}) custom-call(f32[92,8,128]{2,1,0:T(8,128)S(1)} %collective-permute-done.1.partner_ref.pair_ref, f32[40,8,128]{2,1,0:T(8,128)S(1)} %collective-permute-done.2.side_ref, f32[16,96,128]{2,1,0:T(8,128)S(1)} %get-tuple-element.29.edge_ref, f32[16,512]{1,0:T(8,128)S(1)} %get-tuple-element.30.inner_ref, ...), custom_call_target="tpu_custom_call" | custom-call | tf_op jit(solution)/shard_map/pallas_call | solution.py:757
  23.5 0.8 %shard_map.79 = (f32[13,160,128]{2,1,0:T(8,128)S(1)}, f32[24,144]{1,0:T(8,128)S(1)}, f32[32,144]{1,0:T(8,128)S(1)}, f32[24,144]{1,0:T(8,128)S(1)}, f32[24,144]{1,0:T(8,128)S(1)}) custom-call(f32[32,160,128]{2,1,0:T(8,128)S(1)} %shard_map.77.inner, f32[13,32,128]{2,1,0:T(8,128)S(1)} %collective-permute-done.3.refs_0_, bf16[2,256,256]{2,1,0:T(8,128)(2,1)S(1)} %copy-done.4, ...), custom_call_target="tpu_custom_call" | custom-call | tf_op jit(solution)/shard_map/pallas_call | solution.py:757
  24.4 1.7 %shard_map.80 = (f32[24,1024]{1,0:T(8,128)S(1)}, f32[24,1024]{1,0:T(8,128)S(1)}, f32[72,456]{1,0:T(8,128)S(1)}, f32[40,208]{1,0:T(8,128)S(1)}) custom-call(f32[32,160,128]{2,1,0:T(8,128)S(1)} %shard_map.77.inner, f32[13,160,128]{2,1,0:T(8,128)S(1)} %get-tuple-element.33.outer, f32[32,144]{1,0:T(8,128)S(1)} %get-tuple-element.34.top_ref, ...), custom_call_target="tpu_custom_call" | custom-call | tf_op jit(solution)/shard_map/pallas_call | solution.py:757
  26.1 1.6 %collective-permute-start.4 = (f32[24,1024]{1,0:T(8,128)S(1)}, f32[24,1024]{1,0:T(8,128)S(1)}, u32[]{:S(2)}, u32[]{:S(2)}) collective-permute-start(f32[24,1024]{1,0:T(8,128)S(1)} %get-tuple-element.39), channel_id=1, source_target_pairs={{0,1},{1,0},{2,3},{3,2},{8,9},{9,8},{10,11},{11,10},{16,17},{17,16... | collective-permute-start | bytes 294920 | tf_op jit(solution)/shard_map/ppermute | solution.py:779
  27.8 1.3 %collective-permute-start.5 = (f32[24,1024]{1,0:T(8,128)S(1)}, f32[24,1024]{1,0:T(8,128)S(1)}, u32[]{:S(2)}, u32[]{:S(2)}) collective-permute-start(f32[24,1024]{1,0:T(8,128)S(1)} %get-tuple-element.40), channel_id=1, source_target_pairs={{0,8},{1,2},{2,1},{3,11},{8,0},{9,10},{10,9},{11,3},{16,24},{17,18... | collective-permute-start | bytes 294920 | tf_op jit(solution)/shard_map/ppermute | solution.py:779
  29.1 1.3 %collective-permute-start.6 = (f32[24,144]{1,0:T(8,128)S(1)}, f32[24,144]{1,0:T(8,128)S(1)}, u32[]{:S(2)}, u32[]{:S(2)}) collective-permute-start(f32[24,144]{1,0:T(8,128)S(1)} %get-tuple-element.41), channel_id=1, source_target_pairs={{0,2},{1,3},{2,0},{3,1},{8,10},{9,11},{10,8},{11,9},{16,18},{17,19... | collective-permute-start | bytes 41480 | tf_op jit(solution)/shard_map/ppermute | solution.py:779
  30.4 2.9 %collective-permute-start.7 = (f32[24,144]{1,0:T(8,128)S(1)}, f32[24,144]{1,0:T(8,128)S(1)}, u32[]{:S(2)}, u32[]{:S(2)}) collective-permute-start(f32[24,144]{1,0:T(8,128)S(1)} %get-tuple-element.42), channel_id=1, source_target_pairs={{0,3},{1,2},{2,1},{3,0},{8,11},{9,10},{10,9},{11,8},{16,19},{17,18... | collective-permute-start | bytes 41480 | tf_op jit(solution)/shard_map/ppermute | solution.py:779
  33.3 0.8 %collective-permute-done.6.refs_2_ = f32[24,144]{1,0:T(8,128)S(1)} collective-permute-done((f32[24,144]{1,0:T(8,128)S(1)}, f32[24,144]{1,0:T(8,128)S(1)}, u32[]{:S(2)}, u32[]{:S(2)}) %collective-permute-start.6) | collective-permute-done | bytes 13856 | tf_op jit(solution)/shard_map/ppermute | solution.py:779
  34.0 2.2 %collective-permute-done.7.refs_3_ = f32[24,144]{1,0:T(8,128)S(1)} collective-permute-done((f32[24,144]{1,0:T(8,128)S(1)}, f32[24,144]{1,0:T(8,128)S(1)}, u32[]{:S(2)}, u32[]{:S(2)}) %collective-permute-start.7) | collective-permute-done | bytes 13856 | tf_op jit(solution)/shard_map/ppermute | solution.py:779
  36.2 2.0 %shard_map.81 = f32[1024,128]{1,0:T(8,128)} custom-call(f32[512,128]{1,0:T(8,128)S(1)} %get-tuple-element.25.inner_ref, f32[512,128]{1,0:T(8,128)S(1)} %get-tuple-element.31.edge_ref, f32[72,456]{1,0:T(8,128)S(1)} %get-tuple-element.36.e1_ref, f32[40,208]{1,0:T(8,128)S(1)} %get-tuple-element.37.e2_ref, f32[24,144]{1,0:T(8,128)S(1)} %get-tuple-element.38.e3_ref, ...), custom_call_target="tpu_custom_call" | custom-call | tf_op jit(solution)/shard_map/pallas_call | solution.py:757
  (19 shorter events, 0.0 us)
Async XLA Ops:
  0.0 1.0 %copy-start.2 = (f32[32,32,128]{2,1,0:T(8,128)S(1)}, f32[32,32,128]{2,1,0:T(8,128)}, u32[]{:S(2)}) copy-start(f32[32,32,128]{2,1,0:T(8,128)} %q_ref.5) | copy-start | bytes 1572868
  1.0 1.0 %copy-start.6 = (bf16[106,16,128]{2,1,0:T(8,128)(2,1)S(1)}, bf16[106,16,128]{2,1,0:T(8,128)(2,1)}, u32[]{:S(2)}) copy-start(bf16[106,16,128]{2,1,0:T(8,128)(2,1)} %constant.12.clone.table_ref) | copy-start | bytes 1302532
  2.1 15.4 %copy-start.3 = (f32[32,32,128]{2,1,0:T(8,128)S(1)}, f32[32,32,128]{2,1,0:T(8,128)}, u32[]{:S(2)}) copy-start(f32[32,32,128]{2,1,0:T(8,128)} %q_ref.5) | copy-start | bytes 1572868
  2.1 15.4 %copy-start.4 = (bf16[2,256,256]{2,1,0:T(8,128)(2,1)S(1)}, bf16[2,256,256]{2,1,0:T(8,128)(2,1)}, u32[]{:S(2)}) copy-start(bf16[2,256,256]{2,1,0:T(8,128)(2,1)} %constant.13.clone.y_table.refs_1_) | copy-start | bytes 786436
  2.7 9.8 %collective-permute-start = (f32[70,8,128]{2,1,0:T(8,128)S(1)}, f32[70,8,128]{2,1,0:T(8,128)S(1)}, u32[]{:S(2)}, u32[]{:S(2)}) collective-permute-start(f32[70,8,128]{2,1,0:T(8,128)S(1)} %get-tuple-element.24), channel_id=1, source_target_pairs={{0,4},{4,0},{1,5},{5,1},{2,6},{6,2},{3,7},{7,3},{8,12},{12,8},{9,1... | collective-permute-start | bytes 860168 | tf_op jit(solution)/shard_map/ppermute | solution.py:769
  12.6 1.8 %collective-permute-start.1 = (f32[92,8,128]{2,1,0:T(8,128)S(1)}, f32[92,8,128]{2,1,0:T(8,128)S(1)}, u32[]{:S(2)}, u32[]{:S(2)}) collective-permute-start(f32[92,8,128]{2,1,0:T(8,128)S(1)} %get-tuple-element.27), channel_id=1, source_target_pairs={{0,8},{4,12},{8,0},{12,4},{16,24},{20,28},{24,16},{28,20},{1,9},{5... | collective-permute-start | bytes 1130504 | tf_op jit(solution)/shard_map/ppermute | solution.py:779
  14.4 9.1 %collective-permute-start.3 = (f32[13,32,128]{2,1,0:T(8,128)S(1)}, f32[13,32,128]{2,1,0:T(8,128)S(1)}, u32[]{:S(2)}, u32[]{:S(2)}) collective-permute-start(f32[13,32,128]{2,1,0:T(8,128)S(1)} %shard_map.78), channel_id=1, source_target_pairs={{0,24},{4,28},{8,16},{12,20},{16,8},{20,12},{24,0},{28,4},{1,25},{... | collective-permute-start | bytes 638984 | tf_op jit(solution)/shard_map/ppermute | solution.py:779
  16.0 6.3 %collective-permute-start.2 = (f32[40,8,128]{2,1,0:T(8,128)S(1)}, f32[40,8,128]{2,1,0:T(8,128)S(1)}, u32[]{:S(2)}, u32[]{:S(2)}) collective-permute-start(f32[40,8,128]{2,1,0:T(8,128)S(1)} %get-tuple-element.28), channel_id=1, source_target_pairs={{0,4},{4,0},{8,16},{12,20},{16,8},{20,12},{24,28},{28,24},{1,5},{5... | collective-permute-start | bytes 491528 | tf_op jit(solution)/shard_map/ppermute | solution.py:779
  17.5 2.2 %copy-start = (bf16[4,448,1152]{2,1,0:T(8,128)(2,1)S(1)}, bf16[4,448,1152]{2,1,0:T(8,128)(2,1)}, u32[]{:S(2)}) copy-start(bf16[4,448,1152]{2,1,0:T(8,128)(2,1)} %constant.14.clone.z_table.refs_2_) | copy-start | bytes 12386308
  19.7 2.6 %copy-start.1 = (bf16[4,448,1152]{2,1,0:T(8,128)(2,1)S(1)}, bf16[4,448,1152]{2,1,0:T(8,128)(2,1)}, u32[]{:S(2)}) copy-start(bf16[4,448,1152]{2,1,0:T(8,128)(2,1)} %constant.14.clone.z_table.refs_2_) | copy-start | bytes 12386308
  24.3 11.9 %copy-start.5 = (bf16[816,1024]{1,0:T(8,128)(2,1)S(1)}, bf16[816,1024]{1,0:T(8,128)(2,1)}, u32[]{:S(2)}) copy-start(bf16[816,1024]{1,0:T(8,128)(2,1)} %constant.15.clone.refs_4_) | copy-start | bytes 5013508
  24.4 11.9 %copy-start.7 = (bf16[4,224,128]{2,1,0:T(8,128)(2,1)S(1)}, bf16[4,224,128]{2,1,0:T(8,128)(2,1)}, u32[]{:S(2)}) copy-start(bf16[4,224,128]{2,1,0:T(8,128)(2,1)} %constant.17.clone.refs_6_) | copy-start | bytes 688132
  24.4 11.9 %copy-start.8 = (f32[8,8,512]{2,1,0:T(8,128)S(1)}, f32[8,8,512]{2,1,0:T(8,128)}, u32[]{:S(2)}) copy-start(f32[8,8,512]{2,1,0:T(8,128)} %constant.16.clone.refs_5_) | copy-start | bytes 393220
  26.1 10.1 %collective-permute-start.4 = (f32[24,1024]{1,0:T(8,128)S(1)}, f32[24,1024]{1,0:T(8,128)S(1)}, u32[]{:S(2)}, u32[]{:S(2)}) collective-permute-start(f32[24,1024]{1,0:T(8,128)S(1)} %get-tuple-element.39), channel_id=1, source_target_pairs={{0,1},{1,0},{2,3},{3,2},{8,9},{9,8},{10,11},{11,10},{16,17},{17,16... | collective-permute-start | bytes 294920 | tf_op jit(solution)/shard_map/ppermute | solution.py:779
  27.8 8.5 %collective-permute-start.5 = (f32[24,1024]{1,0:T(8,128)S(1)}, f32[24,1024]{1,0:T(8,128)S(1)}, u32[]{:S(2)}, u32[]{:S(2)}) collective-permute-start(f32[24,1024]{1,0:T(8,128)S(1)} %get-tuple-element.40), channel_id=1, source_target_pairs={{0,8},{1,2},{2,1},{3,11},{8,0},{9,10},{10,9},{11,3},{16,24},{17,18... | collective-permute-start | bytes 294920 | tf_op jit(solution)/shard_map/ppermute | solution.py:779
  29.1 5.0 %collective-permute-start.6 = (f32[24,144]{1,0:T(8,128)S(1)}, f32[24,144]{1,0:T(8,128)S(1)}, u32[]{:S(2)}, u32[]{:S(2)}) collective-permute-start(f32[24,144]{1,0:T(8,128)S(1)} %get-tuple-element.41), channel_id=1, source_target_pairs={{0,2},{1,3},{2,0},{3,1},{8,10},{9,11},{10,8},{11,9},{16,18},{17,19... | collective-permute-start | bytes 41480 | tf_op jit(solution)/shard_map/ppermute | solution.py:779
  30.4 5.8 %collective-permute-start.7 = (f32[24,144]{1,0:T(8,128)S(1)}, f32[24,144]{1,0:T(8,128)S(1)}, u32[]{:S(2)}, u32[]{:S(2)}) collective-permute-start(f32[24,144]{1,0:T(8,128)S(1)} %get-tuple-element.42), channel_id=1, source_target_pairs={{0,3},{1,2},{2,1},{3,0},{8,11},{9,10},{10,9},{11,8},{16,19},{17,18... | collective-permute-start | bytes 41480 | tf_op jit(solution)/shard_map/ppermute | solution.py:779

commit v3 on v2

--- a/solution.py
+++ b/solution.py
@@ -116,10 +116,11 @@
         self.lane = [0, 0, z.width[1], z.width[1] + z.width[2]]
         self.lane_end = self.lane[3] + z.width[3]
         assert self.lane_end <= LANES and z.length == LANES
-        self.rows1, self.rows2, self.rows3 = up(y.width[1], 8), up(y.width[2], 16), up(y.width[3], 16)
+        self.rows1, self.rows2 = up(y.width[1], 8), up(y.width[2], 16)
+        self.rows3, self.whole3 = up(y.width[3], 16), up(y.count * y.length >> 3, 8)
         assert self.rows2 <= 16 and self.rows3 <= 16 and FACE <= 14 and self.rows1 == 24
         self.row = [0, 0, self.rows1, self.rows1 + self.rows2]
-        self.row_face = self.rows1 + self.rows2 + self.rows3
+        self.row_face = self.rows1 + self.rows2 + self.whole3
         self.kinds = 1 if y.count == 2 else 2
         self.rows_restricted = self.row_face + 16 * self.kinds
         self.overlay = y.count == 2 and y.width[1] + 3 <= self.rows1
@@ -127,10 +128,14 @@
         self.fine_halos = 1 if y.count == 2 else 2
         self.fine_rows = y.length + 8 * self.fine_halos
         self.pair_width = [w + (x.length >> l) for l, w in enumerate(x.width)]
-        self.planes = max(FACE, x.width[2], self.pair_width[3])
+        self.planes = max(FACE, x.width[2])
+        self.flat_top = up((x.count * x.length >> 3) * self.whole3, LANES)
+        self.top_shape = up(z.width[3], 8), self.flat_top
+        self.top_rows = self.top_shape[0] * self.flat_top // LANES
+        self.top_row = REACH * self.fine_rows + self.planes * self.coarse_rows
         assert self.planes <= x.width[1]
-        self.group = [0, 0, 3 * self.rows1, 3 * self.rows1 + 3 * self.rows2]
-        self.rows_mixed = up(self.group[3] + 2 * self.rows3, 16)
+        self.group = [0, 0, 3 * self.rows1]
+        self.rows_mixed = up(3 * self.rows1 + 3 * self.rows2, 16)
         self.tall = [0, up(z.width[1], 8), up(z.width[2], 8), up(z.width[3], 8)]
         assert self.tall[1] - 16 == z.width[1] - FACE and self.tall[2] - 16 == z.width[2] - 13
         self.flat = [0, x.width[1] * self.rows1, x.width[2] * self.rows2, x.width[3] * self.rows3]
@@ -144,6 +149,14 @@
     def near_y(self, halos):
         return [halos[0]] if self.y.count == 2 else [halos[0], halos[-1]]
 
+    def tiles(self):
+        nx, nt = self.x.length, self.y.length // 8
+        inner = range(REACH, nx - REACH)
+        edge = [*range(REACH), *range(nx - REACH, nx)]
+        order = [(x, t) for x in inner for t in range(1, nt - 1)]
+        order += [(x, t) for x in inner for t in (0, nt - 1)]
+        return order + [(x, t) for x in edge for t in range(nt)]
+
     def pair_plane(self, ref, index):
         return plane(ref, self.fine_rows * REACH, self.coarse_rows, index)
 
@@ -152,32 +165,45 @@
 
     def restrict_tables(self):
         rows = up(self.rows_restricted, 16)
-        along_y = [place((rows, LANES), (0, 0, m)) for m in self.restrict_y().astype(np.float32)]
-        along_z = list(self.restrict_z().astype(np.float32))
-        return np.concatenate(along_z + along_y).astype(jnp.bfloat16).reshape(-1, 16, LANES)
+        along_y = np.stack([place((rows, LANES), (0, 0, m)) for m in self.restrict_y().astype(np.float32)])
+        parts = [self.restrict_z(), along_y, self.y_tables(), self.top_z()]
+        parts = [p.astype(np.float32) for p in parts]
+        blocks = []
+        for p in parts:
+            columns = [p[:, :, c : c + LANES] for c in range(0, p.shape[2], LANES)]
+            blocks.append(np.concatenate(columns, axis=1).reshape(len(p), -1, 16, LANES))
+        self.blocks = [b.shape[1] for b in blocks]
+        table = np.concatenate([b.reshape(-1, 16, LANES) for b in blocks] + [self.top_select().reshape(-1, 2, LANES)
+            .transpose(1, 0, 2).reshape(-1, 16, LANES).astype(np.float32)])
+        return table.astype(jnp.bfloat16)
 
     def y_tables(self):
-        fine, coarse = self.fine_y(), self.coarse_y()
+        fine, halo, coarse = self.fine_y(), self.halo_y(), self.coarse_y()
         cols = up(max(fine.shape[2], coarse.shape[2]), LANES)
+        self.halo_rows, self.halo_cols = halo.shape[1:]
         widen = lambda t: np.pad(t, ((0, 0), (0, 0), (0, cols - t.shape[2])))
         self.fine_cols, self.coarse_cols = fine.shape[2], coarse.shape[2]
-        return np.concatenate([widen(fine), widen(coarse)], axis=1)
+        self.y_cols = cols
+        return np.concatenate([widen(fine), widen(coarse), widen(halo)], axis=1)
 
     def z_tables(self):
-        tables = [*self.fine_z(), *[self.coarse_z(level) for level in (1, 2, 3)]]
+        tables = [*self.fine_z(), *[self.coarse_z(level) for level in (1, 2)]]
         cols = 9 * LANES
         self.z_rows = np.cumsum([0] + [t.shape[1] for t in tables])
         return np.concatenate([np.pad(t, ((0, 0), (0, 0), (0, cols - t.shape[2]))) for t in tables], axis=1)
 
     def fine_matrix(self, ref):
-        return ref[lax.axis_index("gy"), : 3 * self.y.length, :][:, : self.fine_cols]
+        return ref[: 3 * self.y.length, :][:, : self.fine_cols]
 
     def coarse_matrix(self, ref):
-        return ref[lax.axis_index("gy"), 3 * self.y.length :, :][:, : self.coarse_cols]
+        start = 3 * self.y.length
+        return ref[start : start + self.rows_mixed, :][:, : self.coarse_cols]
+
+    def halo_matrix(self, ref):
+        return ref[3 * self.y.length + self.rows_mixed :, :][:, : self.halo_cols]
 
     def z_matrix(self, ref, number):
-        cols = LANES * (6 if number == 4 else 9)
-        return ref[lax.axis_index("gz"), int(self.z_rows[number]) : int(self.z_rows[number + 1]), :][:, :cols]
+        return ref[lax.axis_index("gz"), int(self.z_rows[number]) : int(self.z_rows[number + 1]), :]
 
     def restrict_z(self):
         z = self.z
@@ -191,7 +217,10 @@
     def restrict_y(self):
         y, tables = self.y, []
         for b in range(y.count):
-            pieces = [(self.row[l], 0, y.partial(l, b)) for l in (1, 2, 3)]
+            pieces = [(self.row[l], 0, y.partial(l, b)) for l in (1, 2)]
+            cells, inside = y.window(3, b)
+            for cell, line in zip(cells[inside > 0], y.partial(3, b)[inside > 0]):
+                pieces.append((self.row[3] + cell, 0, line[None]))
             first = y.partial(1, b)
             for k in range(self.kinds):
                 kind = self.face_kind(y, 1, b) if self.kinds == 1 else 1 - k
@@ -217,14 +246,19 @@
             tables.append(left3(place((3 * y.length, up(self.fine_rows, 16)), *pieces)))
         return np.stack(tables)
 
+    def halo_y(self):
+        n, cols = self.y.length, up(self.fine_rows, 16)
+        rows = [s * n + r for s in range(3) for r in (*range(8), *range(n - 8, n))]
+        columns = [c * cols + n + k for c in range(3) for k in range(cols - n)]
+        return self.fine_y()[:, rows][:, :, columns]
+
     def coarse_y(self):
         y, tables = self.y, []
         for b in range(y.count):
             whole = np.zeros((self.rows_mixed, self.coarse_rows))
-            for level in (1, 2, 3):
-                sigmas = STENCIL_SIGMAS if level < 3 else TOP_SIGMAS
-                rows = (0, self.rows1, self.rows2, self.rows3)[level]
-                for s, sigma in enumerate(sigmas):
+            for level in (1, 2):
+                rows = self.rows1 if level == 1 else self.rows2
+                for s, sigma in enumerate(STENCIL_SIGMAS):
                     top = self.group[level] + s * rows
                     for offset in range(y.count):
                         source = (b - offset) % y.count
@@ -265,37 +299,42 @@
 
     def coarse_z(self, level):
         z, tables = self.z, []
-        sigmas, weights = (STENCIL_SIGMAS, STENCIL_WEIGHTS) if level < 3 else (TOP_SIGMAS, TOP_WEIGHTS)
-        factor = 0.5**level if level < 3 else 1.0
-        cols, tall = LANES * len(sigmas), self.tall[level]
+        cols, tall = LANES * len(STENCIL_SIGMAS), self.tall[level]
         for b in range(z.count):
 
             def mixed(target):
-                blocks = [
-                    place((z.width[level], LANES), (0, self.lane[level], factor * w * z.mix(level, sigma, target, b)))
-                    for sigma, w in zip(sigmas, weights)
-                ]
+                blocks = [z.mix(level, sigma, target, b) * w * 0.5**level for sigma, w in zip(STENCIL_SIGMAS, STENCIL_WEIGHTS)]
+                blocks = [place((z.width[level], LANES), (0, self.lane[level], block)) for block in blocks]
                 return np.concatenate(blocks, axis=1)
 
             pieces = [place((tall, cols), (0, 0, mixed(b)))]
-            if level < 3:
-                layers = FACE if level == 1 else 13
-                for step in (0, 1):
-                    side, target = self.near_z(b, step)
-                    if target is None:
-                        pieces.append(np.zeros((16, cols)))
-                    else:
-                        block = mixed(target)
-                        pieces.append(place((16, cols), (0, 0, block[:layers] if side > 0 else block[-layers:])))
-            else:
-                block = mixed(b ^ 1)
-                pieces.append(block[:16])
-                pieces.append(place((16, cols), (FACE, 0, block[16:])))
-                for m in range(2, z.count):
-                    pieces.append(place((tall, cols), (0, 0, mixed(b ^ m))))
+            layers = FACE if level == 1 else 13
+            for step in (0, 1):
+                side, target = self.near_z(b, step)
+                if target is None:
+                    pieces.append(np.zeros((16, cols)))
+                else:
+                    block = mixed(target)
+                    pieces.append(place((16, cols), (0, 0, block[:layers] if side > 0 else block[-layers:])))
             whole = np.concatenate(pieces, axis=0)
             tables.append(left3t(place((up(len(whole), 16), cols), (0, 0, whole))))
         return np.stack(tables)
+
+    def top_z(self):
+        z, tall, tables = self.z, self.tall[3], []
+        for b in range(z.count):
+            pieces = []
+            for s, (sigma, w) in enumerate(zip(TOP_SIGMAS, TOP_WEIGHTS)):
+                for m in range(z.count):
+                    pieces.append((tall * s, tall * m, w * z.mix(3, sigma, b, b ^ m)))
+            tables.append(left3(place((2 * tall, z.count * tall), *pieces)))
+        self.top_cols = tables[0].shape[1]
+        widen = up(self.top_cols, LANES) - self.top_cols
+        return np.pad(np.stack(tables), ((0, 0), (0, 0), (0, widen)))
+
+    def top_select(self):
+        matrix = place((up(self.tall[3], 16), LANES), (0, self.lane[3], np.eye(self.z.width[3])))
+        return np.concatenate([matrix, matrix], axis=1).astype(jnp.bfloat16)
 
     def finish(self):
         x, y, z = self.x, self.y, self.z
@@ -309,7 +348,11 @@
         flat = []
         for level in (3, 2, 1):
             q = place((rows[level], rows[level - 1]), (0, 0, free(y, level).T))
-            flat.append(exact(np.kron(free(x, level).T, q)))
+            matrix = np.kron(free(x, level).T, q)
+            if level == 1:
+                cells = [x_ * y.length + 8 * t + k for x_, t in self.tiles() for k in range(8)]
+                matrix = matrix[:, cells]
+            flat.append(exact(matrix))
         joined = np.concatenate([np.pad(m, ((0, -len(m) % 16), (0, 1024 - m.shape[1]))) for m in flat])
         self.flat_rows = np.cumsum([0] + [up(len(m), 16) for m in flat])
         masks = np.zeros((x.count * y.count, 8, 512), np.float32)
@@ -338,14 +381,34 @@
     ref[row // 8 : (row + value.shape[0]) // 8] = value.reshape(value.shape[0] // 8, 8, LANES)
 
 
-def restrict_kernel(plan, q_ref, table_ref, own_ref, *rest):
-    targets, mixed = rest[: plan.kinds], rest[plan.kinds]
+def put_flat(ref, row, value):
+    for c in range(value.shape[1] // LANES):
+        put_plane(ref, row + c * value.shape[0], value[:, c * LANES : (c + 1) * LANES])
+
+
+def get_flat(ref, row, shape):
+    parts = [plane(ref, row, shape[0], c) for c in range(shape[1] // LANES)]
+    return jnp.concatenate(parts, axis=1)
+
+
+def restrict_kernel(plan, q_ref, table_ref, own_ref, top_ref, q_out, y_table_ref, z_table_ref, *rest):
+    targets, (mixed, top) = rest[: plan.kinds], rest[plan.kinds :]
     nx, ny, nz = plan.x.length, plan.y.length, plan.z.length
     by, bz = lax.axis_index("gy"), lax.axis_index("gz")
-    matrix_z = table_ref[pl.ds(3 * nz // 16 * bz, 3 * nz // 16)].reshape(3 * nz, LANES)
-    rows = up(plan.rows_restricted, 16)
-    matrix_y = table_ref[pl.ds(3 * nz // 16 * plan.z.count + rows // 16 * by, rows // 16)].reshape(rows, LANES)
+    blocks_z, blocks_y, blocks_table, blocks_top = plan.blocks
+    at_y = plan.z.count * blocks_z
+    at_table = at_y + plan.y.count * blocks_y
+    at_top = at_table + plan.y.count * blocks_table
+    at_select = at_top + plan.z.count * blocks_top
+    matrix_z = table_ref[pl.ds(blocks_z * bz, blocks_z)].reshape(3 * nz, LANES)
+    matrix_y = table_ref[pl.ds(at_y + blocks_y * by, blocks_y)].reshape(16 * blocks_y, LANES)
     matrix_y = matrix_y[:, : 3 * ny]
+    q_out[...] = q_ref[...]
+    for ref, at in ((y_table_ref, at_table + blocks_table * by), (z_table_ref, at_top + blocks_top * bz)):
+        rows = ref.shape[0]
+        for c in range(ref.shape[1] // LANES):
+            part = table_ref[pl.ds(at + rows // 16 * c, rows // 16)]
+            ref[:, c * LANES : (c + 1) * LANES] = part.reshape(rows, LANES)
     for i in range(nx):
         faces = [q_ref[i, ny - REACH :, :], q_ref[i, :REACH, :]]
         if plan.kinds == 1:
@@ -388,10 +451,6 @@
     lanes = lax.broadcasted_iota(jnp.int32, (8, LANES), 1)
     in1, in2 = lanes < plan.lane[2], lanes < plan.lane[3]
 
-    def tile(planes, level, k, row):
-        index = LOW[level] + k
-        return planes[row][index] if k < plan.x.width[level] else None
-
     def rows_of(start, count, depth):
         levels = [{i: mixed[i, start : start + count, :] for i in range(nx)}]
         for level in range(1, depth + 1):
@@ -401,14 +460,26 @@
     zero = jnp.zeros((8, LANES), F32)
     first = {r: rows_of(r, 8, 1) for r in range(0, plan.rows1, 8)}
     second = {r: rows_of(plan.row[2] + r, 8, 2) for r in (0, 8)}
-    third = {r: rows_of(plan.row[3] + r, 8, 3) for r in (0, 8)}
     face = [{r: rows_of(plan.row_face + 16 * f + r, 8, 1) for r in (0, 8)} for f in range(plan.kinds)]
+    for r in range(0, plan.whole3, 8):
+        third = rows_of(plan.row[3] + r, 8, 3)
+        for k in range(plan.x.width[3]):
+            top[k, r : r + 8, :] = third[LOW[3] + k]
+    high, low = split(top[...].reshape(plan.x.width[3] * plan.whole3, LANES))
+    select = table_ref[at_select:].reshape(2, -1, LANES)
+    select = jnp.concatenate([select[0], select[1]], axis=1)
+    flat = dot(select, jnp.concatenate([high, low], axis=1), ((1,), (1,)))[: plan.tall[3]]
+    flat = jnp.concatenate([flat, jnp.zeros((plan.tall[3], plan.flat_top - flat.shape[1]), F32)], axis=1)
+    start = ((plan.x.length >> 3) * brick + LOW[3]) * plan.whole3
+    flat = pltpu.roll(flat, lax.rem(start + plan.flat_top, plan.flat_top), 1)
+    top_ref[...] = flat
+    for ref in targets:
+        put_flat(ref, 8 * nx + 16 * plan.x.width[1], flat)
     for k in range(plan.x.width[1]):
         for r in range(0, plan.rows1, 8):
             one = first[r][LOW[1] + k]
             two = second[r][LOW[2] + k] if r < 16 and k < plan.x.width[2] else zero
-            three = third[r][LOW[3] + k] if r < 16 and k < plan.x.width[3] else zero
-            rest_ = jnp.where(in2, two, three)
+            rest_ = jnp.where(in2, two, 0.0)
             own_ref[k, r : r + 8, :] = jnp.where(in1, one, rest_)
             if r < 16:
                 for f in range(plan.kinds):
@@ -419,13 +490,26 @@
     return jnp.where(condition, 1.0, 0.0).astype(F32)
 
 
-def extend_kernel(plan, q_ref, own_ref, *refs):
+def top_z_kernel(plan, own_ref, *refs):
+    others, (table_ref, out_ref) = refs[: plan.z.count - 1], refs[plan.z.count - 1 :]
+    value = jnp.concatenate([ref[...] for ref in (own_ref, *others)], axis=0)
+    high, low = split(value)
+    stacked = jnp.concatenate([high, high, low], axis=0)
+    out_ref[...] = dot(table_ref[...][:, : plan.top_cols], stacked)
+
+
+def extend_kernel(plan, q_ref, own_ref, top_ref, *refs):
     count = plan.y.count - 1
-    halos, (ext_ref, partner_ref, side_ref) = refs[:count], refs[count:]
+    halos, (ext_ref, top_out, partner_ref, side_ref) = refs[:count], refs[count:]
     x, y = plan.x, plan.y
     odd = lax.axis_index("gx") % 2
     end = x.length - REACH
     near = plan.near_y(halos)
+    top = top_ref[...]
+    for halo in halos:
+        top = top + get_flat(halo, 8 * halo.shape[0] - plan.top_rows, plan.top_shape)
+    top_out[...] = top
+    put_flat(partner_ref, plan.top_row, top)
     for start, ref in ((end * odd, side_ref), (end * (1 - odd), partner_ref)):
         for i in range(REACH):
             row = plan.fine_rows * i
@@ -433,7 +517,7 @@
             for h, halo in enumerate(near):
                 ref[(row + y.length) // 8 + h] = halo[start + i]
 
-    base = [0 if halo.shape[0] == 2 * x.width[1] else 8 * x.length for halo in halos]
+    base = [8 * halo.shape[0] - plan.top_rows - 16 * x.width[1] for halo in halos]
     for i in range(x.width[1]):
         own = own_ref[i]
         parts = [plane(halo, at, 16, i) for halo, at in zip(halos, base)]
@@ -452,12 +536,14 @@
         put_plane(partner_ref, row, value)
 
 
-def chip_kernel(plan, ext_ref, pair_ref, *targets):
+def chip_kernel(plan, ext_ref, pair_ref, top_ref, top_out, *targets):
     x, gx = plan.x, lax.axis_index("gx")
     odd, chip = gx % 2, gx // 2
     lanes = lax.broadcasted_iota(jnp.int32, (1, LANES), 1)
-    in1, in2 = lanes < plan.lane[2], lanes < plan.lane[3]
+    in1 = lanes < plan.lane[2]
     keep_even, keep_odd = mask(odd == 0), mask(odd == 1)
+    top = top_ref[...] + get_flat(pair_ref, plan.top_row, plan.top_shape)
+    top_out[...] = top
 
     def merged(level, cell):
         size, total = x.length >> level, None
@@ -468,7 +554,6 @@
         return total
 
     second = [merged(2, c) for c in range(plan.pair_width[2])]
-    third = [merged(3, c) for c in range(plan.pair_width[3])]
     start = (x.width[1] - FACE) * odd
     chips = x.count // 2
     for k, ref in zip(range(1, chips), targets):
@@ -479,7 +564,7 @@
             else:
                 two = second[high + p] if k == 1 else second[p]
             first = ext_ref[start + min(p, FACE - 1)]
-            ref[p] = jnp.where(in1, first, jnp.where(in2, two, third[p]))
+            put_plane(ref, plan.coarse_rows * p, jnp.where(in1, first, two))
 
 
 def mix_planes(get, put, count, matrix):
@@ -522,37 +607,64 @@
     return [jnp.zeros((pad, LANES), F32)] if pad else []
 
 
-def fine_inner_kernel(plan, q_ref, y_table, z_table, *refs):
-    refs = list(refs)
-    take = lambda n: [refs.pop(0) for _ in range(n)]
-    halos = take(plan.y.count - 1)
-    main_ref, push_ref, edge_ref = take(3)
-    mixed, ready = refs
+def fine_inner_kernel(plan, q_ref, y_table, z_table, main_ref, push_ref, edge_ref, mixed, ready):
     x, y = plan.x, plan.y
-    padding = fine_padding(plan)
-
-    def get(i):
-        return jnp.concatenate([q_ref[i]] + [plane(h, 0, 8, i) for h in plan.near_y(halos)] + padding, axis=0)
+    halo = jnp.zeros((up(plan.fine_rows, 16) - y.length, LANES), F32)
 
     def put(i, value):
         mixed[i] = value
 
-    mix_planes(get, put, x.length, plan.fine_matrix(y_table))
+    mix_planes(lambda i: jnp.concatenate([q_ref[i], halo], axis=0), put, x.length, plan.fine_matrix(y_table))
     inner = range(REACH, x.length - REACH)
     edge = [*range(REACH), *range(x.length - REACH, x.length)]
+    half = len(inner) * (y.length - 16)
     for s, sigma in enumerate(STENCIL_SIGMAS):
-        for r in range(0, y.length, 16):
-            row = s * y.length + r
-            planes = {i: mixed[i, row : row + 16, :] for i in range(x.length)}
-            for i, value in zip(inner, stencil(planes, inner, sigma)):
-                put_ready(ready, 3, s, (i - REACH) * y.length + r, value)
-            for i, value in enumerate(stencil(planes, edge, sigma)):
-                edge_ref[i, row : row + 16, :] = value
+        row, end = s * y.length, (s + 1) * y.length
+        planes = {i: mixed[i, row + 8 : end - 8, :] for i in range(x.length)}
+        for i, value in enumerate(stencil(planes, inner, sigma)):
+            put_ready(ready, 3, s, i * (y.length - 16), value)
+        for i, value in enumerate(stencil(planes, edge, sigma)):
+            edge_ref[i, row + 8 : end - 8, :] = value
+        ends = lambda i: jnp.concatenate([mixed[i, row : row + 8, :], mixed[i, end - 8 : end, :]], axis=0)
+        planes = {i: ends(i) for i in range(x.length)}
+        for i, value in enumerate(stencil(planes, inner, sigma)):
+            put_ready(ready, 3, s, half + i * 16, value)
+        for i, value in enumerate(stencil(planes, edge, sigma)):
+            edge_ref[i, row : row + 8, :] = value[:8]
+            edge_ref[i, end - 8 : end, :] = value[8:]
     main_ref[...] = dot(ready[...], plan.z_matrix(z_table, 0), ((1,), (1,)))
     push_ref[...] = dot(plan.z_matrix(z_table, 1), ready[...], ((1,), (1,)))
 
 
-def fine_edge_kernel(plan, partner_ref, side_ref, edge_ref, inner_ref, y_table, z_table, *refs):
+def fine_halo_kernel(plan, edge_ref, y_table, z_table, *refs):
+    halos, (main_ref, push_ref, out_ref, mixed, ready) = refs[: plan.y.count - 1], refs[plan.y.count - 1 :]
+    x, y = plan.x, plan.y
+    near = plan.near_y(halos)
+    padding = [jnp.zeros((8, LANES), F32)] * (plan.halo_cols // 24 - len(near))
+
+    def get(i):
+        return jnp.concatenate([plane(h, 0, 8, i) for h in near] + padding, axis=0)
+
+    def put(i, value):
+        mixed[i] = value
+
+    mix_planes(get, put, x.length, plan.halo_matrix(y_table))
+    inner = range(REACH, x.length - REACH)
+    edge = [*range(REACH), *range(x.length - REACH, x.length)]
+    out_ref[...] = edge_ref[...]
+    for s, sigma in enumerate(STENCIL_SIGMAS):
+        row, end = s * y.length, (s + 1) * y.length
+        planes = {i: mixed[i, 16 * s : 16 * s + 16, :] for i in range(x.length)}
+        for i, value in enumerate(stencil(planes, inner, sigma)):
+            put_ready(ready, 3, s, i * 16, value)
+        for i, value in enumerate(stencil(planes, edge, sigma)):
+            out_ref[i, row : row + 8, :] += value[:8]
+            out_ref[i, end - 8 : end, :] += value[8:]
+    main_ref[...] = dot(ready[...], plan.z_matrix(z_table, 0), ((1,), (1,)))
+    push_ref[...] = dot(plan.z_matrix(z_table, 1), ready[...], ((1,), (1,)))
+
+
+def fine_edge_kernel(plan, partner_ref, side_ref, edge_ref, inner_ref, halo_ref, y_table, z_table, *refs):
     main_ref, push_ref, mixed, ready = refs
     x, y = plan.x, plan.y
     gx = lax.axis_index("gx")
@@ -584,8 +696,9 @@
                 put_ready(ready, 3, s, i * y.length + r, edge_ref[i, row : row + 16, :] + value)
     main_ref[...] = dot(ready[...], plan.z_matrix(z_table, 0), ((1,), (1,)))
     pushed = dot(plan.z_matrix(z_table, 1), ready[...], ((1,), (1,)))
-    half = pushed.shape[1] // 2
-    push_ref[...] = jnp.concatenate([pushed[:, :half], inner_ref[...], pushed[:, half:]], axis=1)
+    inner = inner_ref[...]
+    half = inner.shape[1] - halo_ref.shape[1]
+    push_ref[...] = jnp.concatenate([inner[:, :half], inner[:, half:] + halo_ref[...], pushed], axis=1)
 
 
 def coarse_inner_kernel(plan, ext_ref, pair_ref, y_table, mixed):
@@ -602,7 +715,7 @@
     odd, chip, chips = gx % 2, gx // 2, plan.x.count // 2
     size, width = x.length >> level, x.width[level]
     start = LOW[level]
-    reach = REACH if level < 3 else x.count * x.length
+    reach = REACH
     cells = {start + k: inner[k, row : row + rows, :] for k in range(width)}
 
     def add(cell, value, keep):
@@ -620,7 +733,7 @@
         base = plan.planes * (offset - 1)
         at = lambda k: outer[base + k, row : row + rows, :]
         for shift, here in ((-offset, chip >= offset), (chips - offset, chip < offset)):
-            if level < 3 and abs(shift) != 1:
+            if abs(shift) != 1:
                 continue
             if level == 1:
                 keep = mask(here & (odd == (0 if shift < 0 else 1)))
@@ -633,39 +746,22 @@
                 first = 2 * size * shift - size * core + start
                 if level == 2 and shift < 0:
                     first += size
-                for k in range(plan.planes if level == 2 else plan.pair_width[3]):
+                for k in range(plan.planes):
                     add(first + k, at(k), keep)
     return cells
 
 
-def top_kernel(plan, inner, *refs):
-    refs = list(refs)
-    take = lambda n: [refs.pop(0) for _ in range(n)]
-    chips, (y_table, z_table) = take(plan.x.count // 2 - 1), take(2)
-    outer, own_ref, partner_ref = take(3)
-    far, ready = take(plan.z.count - 2), refs[0]
+def coarse_kernel(plan, inner, *refs):
+    chips = plan.x.count // 2 - 1
+    others, refs = refs[:chips], refs[chips:]
+    push_ref, y_table, z_table, partner_ref, side_ref, e1_ref, e2_ref, outer, *ready = refs
 
     def put(i, value):
         outer[i] = value
 
-    mix_planes(lambda i: chips[i // plan.planes][i % plan.planes], put, plan.planes * len(chips), plan.coarse_matrix(y_table))
-    start, width, rows = LOW[3], plan.x.width[3], plan.rows3
-    for s, sigma in enumerate(TOP_SIGMAS):
-        for r in range(0, rows, 8):
-            cells = collect(plan, 3, inner, outer, plan.group[3] + s * rows + r, 8)
-            reach = max(cells) - min(cells)
-            for i, value in enumerate(stencil(cells, range(start, start + width), sigma, reach)):
-                put_ready(ready, 2, s, i * rows + r, value)
-    three = dot(plan.z_matrix(z_table, 4), ready[...], ((1,), (1,)))
-    tall = plan.tall[3]
-    own_ref[...] = three[:tall]
-    partner_ref[...] = three[tall : tall + 32]
-    for m, ref in enumerate(far):
-        ref[...] = three[tall * (m + 1) + 32 : tall * (m + 2) + 32]
-
-
-def coarse_kernel(plan, inner, outer, top_ref, push_ref, z_table, *refs):
-    partner_ref, side_ref, e1_ref, e2_ref, *ready = refs
+    count = plan.planes * chips
+    get = lambda i: plane(others[i // plan.planes], 0, plan.coarse_rows, i % plan.planes)
+    mix_planes(get, put, count, plan.coarse_matrix(y_table))
     x = plan.x
     results = []
     for level in (1, 2):
@@ -687,15 +783,33 @@
         ref[8:, : plan.flat[1]] = one[start : start + 16]
         start = plan.tall[2] + 16 * n
         ref[8:, 512 : 512 + plan.flat[2]] = two[start : start + 16]
-    partner_ref[8:, : plan.flat[3]] += top_ref[16:]
-    partner_ref[8:, 768 : 768 + plan.flat[3]] = top_ref[:16]
-
-
-def finish_kernel(plan, inner_ref, edge_ref, e1_ref, e2_ref, e3_ref, *refs):
+
+
+def top_kernel(plan, *refs):
+    *values, out_ref = refs
+    total = functools.reduce(jnp.add, [v[...] for v in values])
+    shape = (plan.flat_top, plan.flat[3])
+    source, target = (lax.broadcasted_iota(jnp.int32, shape, d) for d in (0, 1))
+    first_x = (plan.x.length >> 3) * lax.axis_index("gx") + LOW[3]
+    first_y = (plan.y.length >> 3) * lax.axis_index("gy") + LOW[3]
+    apart_x = source // plan.whole3 - target // plan.rows3 - first_x
+    apart_y = source % plan.whole3 - target % plan.rows3 - first_y
+    square = (apart_x * apart_x + apart_y * apart_y).astype(F32)
+    result, tall = None, plan.tall[3]
+    for s, sigma in enumerate(TOP_SIGMAS):
+        matrix = jnp.exp(square * (-1.0 / sigma**2))
+        matrix_high, matrix_low = split(matrix)
+        high, low = split(total[s * tall : (s + 1) * tall])
+        left = jnp.concatenate([high, low, high], axis=1)
+        term = dot(left, jnp.concatenate([matrix_high, matrix_high, matrix_low], axis=0))
+        result = term if result is None else result + term
+    out_ref[...] = result
+
+
+def finish_kernel(plan, inner_ref, halo_ref, edge_ref, e1_ref, e2_ref, *refs):
     z = plan.z
     refs = list(refs)
-    partner_ref, side_ref, *far = [refs.pop(0) for _ in range(z.count)]
-    flat, masks, tall, out_ref, e1, e2, e3 = refs
+    partner_ref, side_ref, e3_ref, flat, masks, tall, out_ref, e1, e2 = refs
     bz = lax.axis_index("gz")
     column = lax.axis_index("gx") * plan.y.count + lax.axis_index("gy")
     odd = bz % 2
@@ -706,11 +820,7 @@
         flat[bounds[k] : bounds[k + 1], :][: plan.flat[3 - k], :cols]
         for k, cols in enumerate((plan.flat[2], plan.flat[1], spread_cols))
     )
-    e1[...], e2[...], e3[...] = e1_ref[...], e2_ref[...], e3_ref[...]
-    for f in far:
-        e3[...] += f[...]
-    e3[:16, :] += partner_ref[8:24, 768 : 768 + plan.flat[3]]
-    e3[16 : z.width[3], :] += partner_ref[8 + FACE : 8 + FACE + z.width[3] - 16, : plan.flat[3]]
+    e1[...], e2[...] = e1_ref[...], e2_ref[...]
     kept = lax.broadcasted_iota(jnp.int32, (16, 1), 0) < FACE
     for ref, high in ((partner_ref, odd == 0), (side_ref, odd == 1)):
         one = jnp.where(kept, ref[8:, : plan.flat[1]], 0.0)
@@ -728,12 +838,12 @@
         high, low = split(value)
         return dot(matrix, high) + dot(matrix, low)
 
-    top = up(plan.tall[1] + 16, 16)
-    middle = top + up(plan.tall[2], 16)
-    tall3 = tall[bz, top:middle, :][: plan.tall[2], : plan.tall[3]]
+    start = up(plan.tall[1] + 16, 16)
+    middle = start + up(plan.tall[2], 16)
+    tall3 = tall[bz, start:middle, :][: plan.tall[2], : plan.tall[3]]
     tall2 = tall[bz, middle:, :][: plan.tall[1], : plan.tall[2]]
-    last = tall[bz, :top, :]
-    three = e3[...] * keep(3)
+    last = tall[bz, :start, :]
+    three = e3_ref[...] * keep(3)
     two = (e2[...] + along(tall3, across(three, flat3))) * keep(2)
     one = (e1[...] + along(tall2, across(two, flat2))) * keep(1)
     spread = across(one, flat1)
@@ -745,11 +855,19 @@
     stacked = jnp.concatenate([high, low], axis=0)
     matrix = jnp.concatenate([last, last], axis=0)
     coarse = dot(stacked, matrix, ((0,), (0,)))
-    edge = REACH * plan.y.length
-    end = coarse.shape[0] - edge
-    out_ref[:edge] = coarse[:edge] + edge_ref[:edge]
-    out_ref[edge:end] = coarse[edge:end] + inner_ref[...]
-    out_ref[end:] = coarse[end:] + edge_ref[edge:]
+    inner = inner_ref.shape[0]
+    half = inner - halo_ref.shape[0]
+    tiles = plan.y.length // 8
+    for k, (x, t) in enumerate(plan.tiles()):
+        row = 8 * k
+        value = coarse[row : row + 8]
+        if row < inner:
+            value = value + inner_ref[row : row + 8]
+            if row >= half:
+                value = value + halo_ref[row - half : row - half + 8]
+        else:
+            value = value + edge_ref[row - inner : row - inner + 8]
+        out_ref[8 * (tiles * x + t) : 8 * (tiles * x + t) + 8] = value
 
 
 def call(kernel, plan, operands, outs, scratch=()):
@@ -794,13 +912,21 @@
     partner_z = lambda v: swap(v, ("gx", "gz"), lambda i, j: (i, j ^ 1))
     across_z = lambda v: swap(v, ("gx", "gz"), lambda i, j: (i ^ 1, j) if side_z(j) is None else (i, side_z(j)))
 
-    rows_y = 8 * x.length + 16 * x.width[1]
-    own, *to_y = call(
+    rows_y = 8 * x.length + 16 * x.width[1] + plan.top_rows
+    table = plan.restrict_tables()
+    own, top, charges, y_table, top_table, *to_y = call(
         restrict_kernel,
         plan,
-        [charges, plan.restrict_tables()],
-        [array(x.width[1], plan.rows1, LANES)] + [array(rows_y // 8, 8, LANES)] * plan.kinds,
-        [vmem(x.length, plan.rows_restricted, LANES)],
+        [charges, table],
+        [
+            array(x.width[1], plan.rows1, LANES),
+            array(plan.tall[3], plan.flat_top),
+            array(*charges.shape),
+            jax.ShapeDtypeStruct((3 * y.length + plan.rows_mixed + plan.halo_rows, plan.y_cols), BF),
+            jax.ShapeDtypeStruct((2 * plan.tall[3], up(plan.top_cols, LANES)), BF),
+        ]
+        + [array(rows_y // 8, 8, LANES)] * plan.kinds,
+        [vmem(x.length, plan.rows_restricted, LANES), vmem(x.width[3], plan.whole3, LANES)],
     )
     from_y = []
     for offset in range(1, y.count):
@@ -808,31 +934,48 @@
         value = value if offset in (1, y.count - 1) else value[x.length :]
         from_y.append(shift(value, "gy", offset))
 
-    ext, to_partner, to_side = call(
-        extend_kernel,
-        plan,
-        [charges, own, *from_y],
-        [
-            array(x.width[1], plan.coarse_rows, LANES),
-            array((REACH * plan.fine_rows + plan.planes * plan.coarse_rows) // 8, 8, LANES),
-            array(REACH * plan.fine_rows // 8, 8, LANES),
-        ],
-    )
-    from_side, pair = across_x(to_side), partner_x(to_partner)
-
-    y_table, z_table = plan.y_tables(), plan.z_tables()
+    z_table = plan.z_tables()
     inner_cells = (x.length - 2 * REACH) * y.length
     edge_cells = 2 * REACH * y.length
     main_inner, push_inner, edge = call(
         fine_inner_kernel,
         plan,
-        [charges, y_table, z_table, *from_y],
+        [charges, y_table, z_table],
         [array(inner_cells, z.length), array(16, inner_cells), array(2 * REACH, 3 * y.length, LANES)],
         [vmem(x.length, 3 * y.length, LANES), ready(inner_cells, 3)],
     )
+    edge, *from_y = lax.optimization_barrier((edge, *from_y))
+
+    ext, top, to_partner, to_side = call(
+        extend_kernel,
+        plan,
+        [charges, own, top, *from_y],
+        [
+            array(x.width[1], plan.coarse_rows, LANES),
+            array(*plan.top_shape),
+            array((plan.top_row + plan.top_rows) // 8, 8, LANES),
+            array(REACH * plan.fine_rows // 8, 8, LANES),
+        ],
+    )
+    from_side, pair = across_x(to_side), partner_x(to_partner)
+
+    halo_cells = (x.length - 2 * REACH) * 16
+    main_halo, push_halo, edge = call(
+        fine_halo_kernel,
+        plan,
+        [edge, y_table, z_table, *from_y],
+        [array(halo_cells, z.length), array(16, halo_cells), array(2 * REACH, 3 * y.length, LANES)],
+        [vmem(x.length, plan.halo_rows, LANES), ready(halo_cells, 3)],
+    )
 
     chips = x.count // 2
-    to_chips = call(chip_kernel, plan, [ext, pair], [array(plan.planes, plan.coarse_rows, LANES)] * (chips - 1))
+    rows_x = plan.planes * plan.coarse_rows
+    top, *to_chips = call(
+        chip_kernel,
+        plan,
+        [ext, pair, top],
+        [array(*plan.top_shape)] + [array(rows_x // 8, 8, LANES)] * (chips - 1),
+    )
     from_chips = [
         swap(v, ("gx", "gy"), lambda i, j, k=k: ((i + 2 * k) % x.count ^ 1, j))
         for k, v in zip(range(1, chips), to_chips)
@@ -842,39 +985,37 @@
         coarse_inner_kernel, plan, [ext, pair, y_table], [array(planes_inner, plan.rows_mixed, LANES)]
     )
 
+    tops = [swap(top, ("gx", "gz"), lambda i, j, m=m: (i, j ^ m)) for m in range(1, z.count)]
+    (top,) = call(top_z_kernel, plan, [top, *tops, top_table], [array(2 * plan.tall[3], plan.flat_top)])
+
     main_edge, push = call(
         fine_edge_kernel,
         plan,
-        [pair, from_side, edge, push_inner, y_table, z_table],
+        [pair, from_side, edge, push_inner, push_halo, y_table, z_table],
         [array(edge_cells, z.length), array(16, x.length * y.length)],
         [vmem(2 * REACH, 3 * y.length, LANES), ready(edge_cells, 3)],
     )
-    planes_outer = plan.planes * (chips - 1)
+    push, top = lax.optimization_barrier((push, top))
     window = lambda level: array(plan.tall[level], plan.flat[level])
-    mixed_outer, e3, top_partner, *far = call(
-        top_kernel,
-        plan,
-        [mixed_inner, *from_chips, y_table, z_table],
-        [array(planes_outer, plan.rows_mixed, LANES), window(3), array(32, plan.flat[3])]
-        + [window(3)] * (z.count - 2),
-        [ready(plan.flat[3], 2)],
-    )
-    from_far = [swap(f, ("gx", "gz"), lambda i, j, m=m: (i, j ^ m)) for m, f in zip(range(2, z.count), far)]
     to_partner, to_side, e1, e2 = call(
         coarse_kernel,
         plan,
-        [mixed_inner, mixed_outer, top_partner, push, z_table],
+        [mixed_inner, *from_chips, push, y_table, z_table],
         [array(24, 1024), array(24, 1024), window(1), window(2)],
-        [ready(plan.flat[1], 3), ready(plan.flat[2], 3)],
+        [vmem(plan.planes * (chips - 1), plan.rows_mixed, LANES), ready(plan.flat[1], 3), ready(plan.flat[2], 3)],
     )
     from_near = [partner_z(to_partner), across_z(to_side)]
+
+    chip_swap = lambda k: lambda i, j: ((i + 2 * k) % x.count ^ 1, j)
+    tops = [top] + [swap(top, ("gx", "gy"), chip_swap(k)) for k in range(1, chips)]
+    (e3,) = call(top_kernel, plan, tops, [window(3)])
 
     (potential,) = call(
         finish_kernel,
         plan,
-        [main_inner, main_edge, e1, e2, e3, *from_near, *from_far, *plan.finish()],
+        [main_inner, main_halo, main_edge, e1, e2, *from_near, e3, *plan.finish()],
         [array(x.length * y.length, z.length)],
-        [vmem(plan.tall[level], plan.flat[level]) for level in (1, 2, 3)],
+        [vmem(plan.tall[level], plan.flat[level]) for level in (1, 2)],
     )
     return potential.reshape(charges.shape)
 

time: 38.6 us -> 35.6 us (0.922)
  waiting for transfers between devices: 11.4 us -> 7.36 us
  Pallas kernels: 9.17 us -> 10.2 us
    ppermute x1, waiting for transfers between devices: 6.83 us -> 3.11 us  [shift(): lax.ppermute(value, axis, [(i, (i + offset) % count) for i in range(count)])]
    pallas_call x9 -> x11, Pallas kernels: 9.17 us -> 10.2 us  [call(): pl.pallas_call(functools.partial(kernel, plan), in_specs=[whole] * len(op...]
    ppermute x7 -> x9, waiting for transfers between devices: 4.62 us -> 4.25 us  [swap(): return lax.ppermute(value, axes, pairs)]
    unnamed x18 -> x14, local copies, waits for them, and re-layouts: 4.25 us -> 4.1 us
    ppermute x7 -> x9, starting transfers between devices: 10.3 us -> 10.4 us  [swap(): return lax.ppermute(value, axes, pairs)]
  transfers between devices with their start and end apart: 8 -> 10, of which waited for: 4 -> 4; matrix products, arithmetic and copies ran while one was open for 0% -> 0% of each run, Pallas kernels for 10% -> 15%
where the time goes in v3:
time: 35.6 us; the launch traced here: 35.2 us
  starting transfers between devices  13.4 us (38%)
  Pallas kernels  10.2 us (29%)
  waiting for transfers between devices  7.36 us (21%)
  local copies, waits for them, and re-layouts  4.1 us (12%)
    ppermute x9, starting transfers between devices, swap(): return lax.ppermute(value, axes, pairs)  10.4 us
    pallas_call x11, Pallas kernels, call(): pl.pallas_call(functools.partial(kernel, plan), in_specs=[whole] * len(op...  10.2 us
    ppermute x9, waiting for transfers between devices, swap(): return lax.ppermute(value, axes, pairs)  4.25 us
    unnamed x14, local copies, waits for them, and re-layouts  4.1 us
    ppermute x1, waiting for transfers between devices, shift(): lax.ppermute(value, axis, [(i, (i + offset) % count) for i in range(count)])  3.11 us
    ppermute x1, starting transfers between devices, shift(): lax.ppermute(value, axis, [(i, (i + offset) % count) for i in range(count)])  2.95 us
  transfers between devices with their start and end apart: 10, of which 4 were waited for; matrix products, arithmetic and copies ran while one was open for 0% of the time, Pallas kernels for 15%

profile of v3, /device:TPU:0, one launch (start us, length us, event | category | flops | bytes accessed | tf_op | source)
XLA Modules:
  0.0 35.2 jit_solution(17652870654491419117)
XLA Ops:
  0.0 1.2 %copy-done.3 = bf16[212,16,128]{2,1,0:T(8,128)(2,1)S(1)} copy-done((bf16[212,16,128]{2,1,0:T(8,128)(2,1)S(1)}, bf16[212,16,128]{2,1,0:T(8,128)(2,1)}, u32[]{:S(2)}) %copy-start.3) | copy-done | bytes 868376
  1.2 1.0 %copy-done.4 = f32[32,32,128]{2,1,0:T(8,128)S(1)} copy-done((f32[32,32,128]{2,1,0:T(8,128)S(1)}, f32[32,32,128]{2,1,0:T(8,128)}, u32[]{:S(2)}) %copy-start.4) | copy-done | bytes 524312
  2.2 0.8 %shard_map.64 = (f32[19,24,128]{2,1,0:T(8,128)S(1)}, f32[24,128]{1,0:T(8,128)S(1)}, f32[32,32,128]{2,1,0:T(8,128)S(1)}, bf16[272,256]{1,0:T(8,128)(2,1)S(1)}, bf...) custom-call(f32[32,32,128]{2,1,0:T(8,128)S(1)} %copy-done.4, bf16[212,16,128]{2,1,0:T(8,128)(2,1)S(1)} %copy-done.3), custom_call_target="tpu_custom_call" | custom-call | tf_op jit(solution)/shard_map/pallas_call | solution.py:875
  3.0 3.0 %collective-permute-start = (f32[73,8,128]{2,1,0:T(8,128)S(1)}, f32[73,8,128]{2,1,0:T(8,128)S(1)}, u32[]{:S(2)}, u32[]{:S(2)}) collective-permute-start(f32[73,8,128]{2,1,0:T(8,128)S(1)} %get-tuple-element.37), channel_id=1, source_target_pairs={{0,4},{4,0},{1,5},{5,1},{2,6},{6,2},{3,7},{7,3},{8,12},{12,8},{9,1... | collective-permute-start | bytes 897032 | tf_op jit(solution)/shard_map/ppermute | solution.py:887
  6.0 1.9 %copy-done = bf16[4,336,1152]{2,1,0:T(8,128)(2,1)S(1)} copy-done((bf16[4,336,1152]{2,1,0:T(8,128)(2,1)S(1)}, bf16[4,336,1152]{2,1,0:T(8,128)(2,1)}, u32[]{:S(2)}) %copy-start) | copy-done | bytes 3096600
  7.8 2.1 %shard_map.65 = (f32[512,128]{1,0:T(8,128)S(1)}, f32[16,512]{1,0:T(8,128)S(1)}, f32[16,96,128]{2,1,0:T(8,128)S(1)}) custom-call(f32[32,32,128]{2,1,0:T(8,128)S(1)} %get-tuple-element.33.q_ref, bf16[272,256]{1,0:T(8,128)(2,1)S(1)} %get-tuple-element.34.y_table.refs_2_, bf16[4,336,1152]{2,1,0:T(8,128)(2,1)S(1)} %copy-done), custom_call_target="tpu_custom_call" | custom-call | tf_op jit(solution)/shard_map/pallas_call | solution.py:875
  9.9 3.1 %collective-permute-done.refs_0_ = f32[73,8,128]{2,1,0:T(8,128)S(1)} collective-permute-done((f32[73,8,128]{2,1,0:T(8,128)S(1)}, f32[73,8,128]{2,1,0:T(8,128)S(1)}, u32[]{:S(2)}, u32[]{:S(2)}) %collective-permute-start) | collective-permute-done | bytes 299040 | tf_op jit(solution)/shard_map/ppermute | solution.py:887
  13.2 1.7 %collective-permute-done.1.partner_ref.pair_ref = f32[95,8,128]{2,1,0:T(8,128)S(1)} collective-permute-done((f32[95,8,128]{2,1,0:T(8,128)S(1)}, f32[95,8,128]{2,1,0:T(8,128)S(1)}, u32[]{:S(2)}, u32[]{:S(2)}) %collective-permute-start.1) | collective-permute-done | bytes 389152 | tf_op jit(solution)/shard_map/ppermute | solution.py:897
  15.0 1.6 %collective-permute-start.3 = (f32[52,8,128]{2,1,0:T(8,128)S(1)}, f32[52,8,128]{2,1,0:T(8,128)S(1)}, u32[]{:S(2)}, u32[]{:S(2)}) collective-permute-start(f32[52,8,128]{2,1,0:T(8,128)S(1)} %get-tuple-element.51), channel_id=1, source_target_pairs={{0,24},{4,28},{8,16},{12,20},{16,8},{20,12},{24,0},{28,4},{1,25},{... | collective-permute-start | bytes 638984 | tf_op jit(solution)/shard_map/ppermute | solution.py:897
  16.6 1.5 %collective-permute-start.2 = (f32[40,8,128]{2,1,0:T(8,128)S(1)}, f32[40,8,128]{2,1,0:T(8,128)S(1)}, u32[]{:S(2)}, u32[]{:S(2)}) collective-permute-start(f32[40,8,128]{2,1,0:T(8,128)S(1)} %get-tuple-element.44), channel_id=1, source_target_pairs={{0,4},{4,0},{8,16},{12,20},{16,8},{20,12},{24,28},{28,24},{1,5},{5... | collective-permute-start | bytes 491528 | tf_op jit(solution)/shard_map/ppermute | solution.py:897
  18.1 3.6 %collective-permute-start.6 = (f32[24,128]{1,0:T(8,128)S(1)}, f32[24,128]{1,0:T(8,128)S(1)}, u32[]{:S(2)}, u32[]{:S(2)}) collective-permute-start(f32[24,128]{1,0:T(8,128)S(1)} %get-tuple-element.53.own_ref), channel_id=1, source_target_pairs={{0,3},{1,2},{2,1},{3,0},{8,11},{9,10},{10,9},{11,8},{16,19},{17,18... | collective-permute-start | bytes 36872 | tf_op jit(solution)/shard_map/ppermute | solution.py:897
  21.7 0.8 %collective-permute-start.4 = (f32[24,128]{1,0:T(8,128)S(1)}, f32[24,128]{1,0:T(8,128)S(1)}, u32[]{:S(2)}, u32[]{:S(2)}) collective-permute-start(f32[24,128]{1,0:T(8,128)S(1)} %get-tuple-element.53.own_ref), channel_id=1, source_target_pairs={{0,1},{1,0},{2,3},{3,2},{8,9},{9,8},{10,11},{11,10},{16,17},{17,16... | collective-permute-start | bytes 36872 | tf_op jit(solution)/shard_map/ppermute | solution.py:897
  22.5 1.2 %shard_map.66 = (f32[256,128]{1,0:T(8,128)S(1)}, f32[16,256]{1,0:T(8,128)S(1)}, f32[16,96,128]{2,1,0:T(8,128)S(1)}) custom-call(f32[16,96,128]{2,1,0:T(8,128)S(1)} %get-tuple-element.38.edge_ref, bf16[272,256]{1,0:T(8,128)(2,1)S(1)} %get-tuple-element.34.y_table.refs_2_, bf16[4,336,1152]{2,1,0:T(8,128)(2,1)S(1)} %copy-done.1, ...), custom_call_target="tpu_custom_call" | custom-call | tf_op jit(solution)/shard_map/pallas_call | solution.py:875
  23.7 0.4 %shard_map.69.inner = f32[32,128,128]{2,1,0:T(8,128)S(1)} custom-call(f32[19,32,128]{2,1,0:T(8,128)S(1)} %get-tuple-element.49.ext_ref, f32[95,8,128]{2,1,0:T(8,128)S(1)} %collective-permute-done.1.partner_ref.pair_ref, bf16[272,256]{1,0:T(8,128)(2,1)S(1)} %get-tuple-element.34.y_table.refs_2_), custom_call_target="tpu_custom_call" | custom-call | tf_op jit(solution)/shard_map/pallas_call | solution.py:875
  24.1 1.2 %shard_map.68 = (f32[512,128]{1,0:T(8,128)S(1)}, f32[16,1024]{1,0:T(8,128)S(1)}) custom-call(f32[95,8,128]{2,1,0:T(8,128)S(1)} %collective-permute-done.1.partner_ref.pair_ref, f32[40,8,128]{2,1,0:T(8,128)S(1)} %collective-permute-done.2.side_ref, f32[16,96,128]{2,1,0:T(8,128)S(1)} %get-tuple-element.45.edge_ref, f32[16,512]{1,0:T(8,128)S(1)} %get-tuple-element.46.inner_ref, ...), custom_call_target="tpu_custom_call" | custom-call | tf_op jit(solution)/shard_map/pallas_call | solution.py:875
  25.3 0.9 %collective-permute-done.5.refs_1_ = f32[24,128]{1,0:T(8,128)S(1)} collective-permute-done((f32[24,128]{1,0:T(8,128)S(1)}, f32[24,128]{1,0:T(8,128)S(1)}, u32[]{:S(2)}, u32[]{:S(2)}) %collective-permute-start.5) | collective-permute-done | bytes 12320 | tf_op jit(solution)/shard_map/ppermute | solution.py:897
  26.3 0.1 shard_map.71.refs_0_
  26.5 1.9 %shard_map.72 = (f32[24,1024]{1,0:T(8,128)S(1)}, f32[24,1024]{1,0:T(8,128)S(1)}, f32[72,456]{1,0:T(8,128)S(1)}, f32[40,208]{1,0:T(8,128)S(1)}) custom-call(f32[32,128,128]{2,1,0:T(8,128)S(1)} %shard_map.69.inner, f32[52,8,128]{2,1,0:T(8,128)S(1)} %collective-permute-done.3.refs_0_, f32[16,1024]{1,0:T(8,128)S(1)} %get-tuple-element.55.refs_1_, ...), custom_call_target="tpu_custom_call" | custom-call | tf_op jit(solution)/shard_map/pallas_call | solution.py:875
  28.4 0.4 %collective-permute-start.7 = (f32[24,1024]{1,0:T(8,128)S(1)}, f32[24,1024]{1,0:T(8,128)S(1)}, u32[]{:S(2)}, u32[]{:S(2)}) collective-permute-start(f32[24,1024]{1,0:T(8,128)S(1)} %get-tuple-element.58), channel_id=1, source_target_pairs={{0,1},{1,0},{2,3},{3,2},{8,9},{9,8},{10,11},{11,10},{16,17},{17,16... | collective-permute-start | bytes 294920 | tf_op jit(solution)/shard_map/ppermute | solution.py:897
  28.8 0.6 %collective-permute-start.8 = (f32[24,1024]{1,0:T(8,128)S(1)}, f32[24,1024]{1,0:T(8,128)S(1)}, u32[]{:S(2)}, u32[]{:S(2)}) collective-permute-start(f32[24,1024]{1,0:T(8,128)S(1)} %get-tuple-element.59), channel_id=1, source_target_pairs={{0,8},{1,2},{2,1},{3,11},{8,0},{9,10},{10,9},{11,3},{16,24},{17,18... | collective-permute-start | bytes 294920 | tf_op jit(solution)/shard_map/ppermute | solution.py:897
  29.4 1.8 %collective-permute-start.9 = (f32[48,128]{1,0:T(8,128)S(1)}, f32[48,128]{1,0:T(8,128)S(1)}, u32[]{:S(2)}, u32[]{:S(2)}) collective-permute-start(f32[48,128]{1,0:T(8,128)S(1)} %shard_map.71.refs_0_), channel_id=1, source_target_pairs={{0,24},{4,28},{8,16},{12,20},{16,8},{20,12},{24,0},{28,4},{1,25},{... | collective-permute-start | bytes 73736 | tf_op jit(solution)/shard_map/ppermute | solution.py:897
  31.3 1.6 %collective-permute-done.9.refs_1_ = f32[48,128]{1,0:T(8,128)S(1)} collective-permute-done((f32[48,128]{1,0:T(8,128)S(1)}, f32[48,128]{1,0:T(8,128)S(1)}, u32[]{:S(2)}, u32[]{:S(2)}) %collective-permute-start.9) | collective-permute-done | bytes 24608 | tf_op jit(solution)/shard_map/ppermute | solution.py:897
  32.9 0.2 shard_map.73.refs_2_
  33.1 2.0 %shard_map.74 = f32[1024,128]{1,0:T(8,128)} custom-call(f32[512,128]{1,0:T(8,128)S(1)} %get-tuple-element.35.inner_ref, f32[256,128]{1,0:T(8,128)S(1)} %get-tuple-element.40.halo_ref, f32[512,128]{1,0:T(8,128)S(1)} %get-tuple-element.48.edge_ref, f32[72,456]{1,0:T(8,128)S(1)} %get-tuple-element.56.e1_ref, f32[40,208]{1,0:T(8,128)S(1)} %get-tuple-element.57.e2_ref, ...), custom_call_target="tpu_custom_call" | custom-call | tf_op jit(solution)/shard_map/pallas_call | solution.py:875
  (21 shorter events, 0.3 us)
Async XLA Ops:
  0.0 1.2 %copy-start.3 = (bf16[212,16,128]{2,1,0:T(8,128)(2,1)S(1)}, bf16[212,16,128]{2,1,0:T(8,128)(2,1)}, u32[]{:S(2)}) copy-start(bf16[212,16,128]{2,1,0:T(8,128)(2,1)} %constant.10.clone.table_ref) | copy-start | bytes 2605060
  1.2 1.0 %copy-start.4 = (f32[32,32,128]{2,1,0:T(8,128)S(1)}, f32[32,32,128]{2,1,0:T(8,128)}, u32[]{:S(2)}) copy-start(f32[32,32,128]{2,1,0:T(8,128)} %q_ref.1) | copy-start | bytes 1572868
  3.0 10.0 %collective-permute-start = (f32[73,8,128]{2,1,0:T(8,128)S(1)}, f32[73,8,128]{2,1,0:T(8,128)S(1)}, u32[]{:S(2)}, u32[]{:S(2)}) collective-permute-start(f32[73,8,128]{2,1,0:T(8,128)S(1)} %get-tuple-element.37), channel_id=1, source_target_pairs={{0,4},{4,0},{1,5},{5,1},{2,6},{6,2},{3,7},{7,3},{8,12},{12,8},{9,1... | collective-permute-start | bytes 897032 | tf_op jit(solution)/shard_map/ppermute | solution.py:887
  6.0 1.9 %copy-start = (bf16[4,336,1152]{2,1,0:T(8,128)(2,1)S(1)}, bf16[4,336,1152]{2,1,0:T(8,128)(2,1)}, u32[]{:S(2)}) copy-start(bf16[4,336,1152]{2,1,0:T(8,128)(2,1)} %constant.11.clone.z_table.refs_3_) | copy-start | bytes 9289732
  7.8 14.6 %copy-start.1 = (bf16[4,336,1152]{2,1,0:T(8,128)(2,1)S(1)}, bf16[4,336,1152]{2,1,0:T(8,128)(2,1)}, u32[]{:S(2)}) copy-start(bf16[4,336,1152]{2,1,0:T(8,128)(2,1)} %constant.11.clone.z_table.refs_3_) | copy-start | bytes 9289732
  13.1 1.8 %collective-permute-start.1 = (f32[95,8,128]{2,1,0:T(8,128)S(1)}, f32[95,8,128]{2,1,0:T(8,128)S(1)}, u32[]{:S(2)}, u32[]{:S(2)}) collective-permute-start(f32[95,8,128]{2,1,0:T(8,128)S(1)} %get-tuple-element.43), channel_id=1, source_target_pairs={{0,8},{4,12},{8,0},{12,4},{16,24},{20,28},{24,16},{28,20},{1,9},{5... | collective-permute-start | bytes 1167368 | tf_op jit(solution)/shard_map/ppermute | solution.py:897
  15.0 11.5 %collective-permute-start.3 = (f32[52,8,128]{2,1,0:T(8,128)S(1)}, f32[52,8,128]{2,1,0:T(8,128)S(1)}, u32[]{:S(2)}, u32[]{:S(2)}) collective-permute-start(f32[52,8,128]{2,1,0:T(8,128)S(1)} %get-tuple-element.51), channel_id=1, source_target_pairs={{0,24},{4,28},{8,16},{12,20},{16,8},{20,12},{24,0},{28,4},{1,25},{... | collective-permute-start | bytes 638984 | tf_op jit(solution)/shard_map/ppermute | solution.py:897
  16.6 7.5 %collective-permute-start.2 = (f32[40,8,128]{2,1,0:T(8,128)S(1)}, f32[40,8,128]{2,1,0:T(8,128)S(1)}, u32[]{:S(2)}, u32[]{:S(2)}) collective-permute-start(f32[40,8,128]{2,1,0:T(8,128)S(1)} %get-tuple-element.44), channel_id=1, source_target_pairs={{0,4},{4,0},{8,16},{12,20},{16,8},{20,12},{24,28},{28,24},{1,5},{5... | collective-permute-start | bytes 491528 | tf_op jit(solution)/shard_map/ppermute | solution.py:897
  18.1 7.3 %collective-permute-start.6 = (f32[24,128]{1,0:T(8,128)S(1)}, f32[24,128]{1,0:T(8,128)S(1)}, u32[]{:S(2)}, u32[]{:S(2)}) collective-permute-start(f32[24,128]{1,0:T(8,128)S(1)} %get-tuple-element.53.own_ref), channel_id=1, source_target_pairs={{0,3},{1,2},{2,1},{3,0},{8,11},{9,10},{10,9},{11,8},{16,19},{17,18... | collective-permute-start | bytes 36872 | tf_op jit(solution)/shard_map/ppermute | solution.py:897
  21.7 4.6 %collective-permute-start.5 = (f32[24,128]{1,0:T(8,128)S(1)}, f32[24,128]{1,0:T(8,128)S(1)}, u32[]{:S(2)}, u32[]{:S(2)}) collective-permute-start(f32[24,128]{1,0:T(8,128)S(1)} %get-tuple-element.53.own_ref), channel_id=1, source_target_pairs={{0,2},{1,3},{2,0},{3,1},{8,10},{9,11},{10,8},{11,9},{16,18},{17,19... | collective-permute-start | bytes 36872 | tf_op jit(solution)/shard_map/ppermute | solution.py:897
  21.7 4.6 %collective-permute-start.4 = (f32[24,128]{1,0:T(8,128)S(1)}, f32[24,128]{1,0:T(8,128)S(1)}, u32[]{:S(2)}, u32[]{:S(2)}) collective-permute-start(f32[24,128]{1,0:T(8,128)S(1)} %get-tuple-element.53.own_ref), channel_id=1, source_target_pairs={{0,1},{1,0},{2,3},{3,2},{8,9},{9,8},{10,11},{11,10},{16,17},{17,16... | collective-permute-start | bytes 36872 | tf_op jit(solution)/shard_map/ppermute | solution.py:897
  26.4 6.7 %copy-start.2 = (bf16[816,1024]{1,0:T(8,128)(2,1)S(1)}, bf16[816,1024]{1,0:T(8,128)(2,1)}, u32[]{:S(2)}) copy-start(bf16[816,1024]{1,0:T(8,128)(2,1)} %constant.12.clone.refs_3_) | copy-start | bytes 5013508
  26.4 6.7 %copy-start.5 = (bf16[4,224,128]{2,1,0:T(8,128)(2,1)S(1)}, bf16[4,224,128]{2,1,0:T(8,128)(2,1)}, u32[]{:S(2)}) copy-start(bf16[4,224,128]{2,1,0:T(8,128)(2,1)} %constant.14.clone.refs_5_) | copy-start | bytes 688132
  26.4 6.7 %copy-start.6 = (f32[8,8,512]{2,1,0:T(8,128)S(1)}, f32[8,8,512]{2,1,0:T(8,128)}, u32[]{:S(2)}) copy-start(f32[8,8,512]{2,1,0:T(8,128)} %constant.13.clone.refs_4_) | copy-start | bytes 393220
  28.4 4.7 %collective-permute-start.7 = (f32[24,1024]{1,0:T(8,128)S(1)}, f32[24,1024]{1,0:T(8,128)S(1)}, u32[]{:S(2)}, u32[]{:S(2)}) collective-permute-start(f32[24,1024]{1,0:T(8,128)S(1)} %get-tuple-element.58), channel_id=1, source_target_pairs={{0,1},{1,0},{2,3},{3,2},{8,9},{9,8},{10,11},{11,10},{16,17},{17,16... | collective-permute-start | bytes 294920 | tf_op jit(solution)/shard_map/ppermute | solution.py:897
  28.8 4.3 %collective-permute-start.8 = (f32[24,1024]{1,0:T(8,128)S(1)}, f32[24,1024]{1,0:T(8,128)S(1)}, u32[]{:S(2)}, u32[]{:S(2)}) collective-permute-start(f32[24,1024]{1,0:T(8,128)S(1)} %get-tuple-element.59), channel_id=1, source_target_pairs={{0,8},{1,2},{2,1},{3,11},{8,0},{9,10},{10,9},{11,3},{16,24},{17,18... | collective-permute-start | bytes 294920 | tf_op jit(solution)/shard_map/ppermute | solution.py:897
  29.4 3.4 %collective-permute-start.9 = (f32[48,128]{1,0:T(8,128)S(1)}, f32[48,128]{1,0:T(8,128)S(1)}, u32[]{:S(2)}, u32[]{:S(2)}) collective-permute-start(f32[48,128]{1,0:T(8,128)S(1)} %shard_map.71.refs_0_), channel_id=1, source_target_pairs={{0,24},{4,28},{8,16},{12,20},{16,8},{20,12},{24,0},{28,4},{1,25},{... | collective-permute-start | bytes 73736 | tf_op jit(solution)/shard_map/ppermute | solution.py:897

commit v4 on v3

--- a/solution.py
+++ b/solution.py
@@ -17,6 +17,7 @@
 
 LOW = (0, -1, -2, -2)
 EXTRA = (0, 3, 5, 5)
+SLOT = 40
 FACE = 11
 LANES = 128
 BF = jnp.bfloat16
@@ -129,8 +130,15 @@
         self.fine_rows = y.length + 8 * self.fine_halos
         self.pair_width = [w + (x.length >> l) for l, w in enumerate(x.width)]
         self.planes = max(FACE, x.width[2])
+        self.half, self.left = LANES // 2, z.width[1] - LANES // 2
+        self.face_groups = up(FACE, 2) // 2
+        assert 0 < self.left and self.left * FACE <= LANES and z.width[2] <= SLOT
+        chips = x.count // 2
+        self.near_chips = [1] if chips == 2 else [1, chips - 1]
+        self.pair_groups = up(self.planes, 3) // 3
+        self.side_rows = REACH * self.fine_rows + (self.face_groups + 1) * self.coarse_rows
         self.flat_top = up((x.count * x.length >> 3) * self.whole3, LANES)
-        self.top_shape = up(z.width[3], 8), self.flat_top
+        self.top_shape = 2 * up(z.width[3], 8), self.flat_top
         self.top_rows = self.top_shape[0] * self.flat_top // LANES
         self.top_row = REACH * self.fine_rows + self.planes * self.coarse_rows
         assert self.planes <= x.width[1]
@@ -471,10 +479,7 @@
     flat = dot(select, jnp.concatenate([high, low], axis=1), ((1,), (1,)))[: plan.tall[3]]
     flat = jnp.concatenate([flat, jnp.zeros((plan.tall[3], plan.flat_top - flat.shape[1]), F32)], axis=1)
     start = ((plan.x.length >> 3) * brick + LOW[3]) * plan.whole3
-    flat = pltpu.roll(flat, lax.rem(start + plan.flat_top, plan.flat_top), 1)
-    top_ref[...] = flat
-    for ref in targets:
-        put_flat(ref, 8 * nx + 16 * plan.x.width[1], flat)
+    top_ref[...] = pltpu.roll(flat, lax.rem(start + plan.flat_top, plan.flat_top), 1)
     for k in range(plan.x.width[1]):
         for r in range(0, plan.rows1, 8):
             one = first[r][LOW[1] + k]
@@ -498,18 +503,40 @@
     out_ref[...] = dot(table_ref[...][:, : plan.top_cols], stacked)
 
 
+def roll_lanes(value, amount):
+    return pltpu.roll(value, amount % LANES, 1)
+
+
+def pack_faces(plan, faces):
+    lanes = lax.broadcasted_iota(jnp.int32, (1, LANES), 1)
+    groups = []
+    for g in range(plan.face_groups):
+        value = faces[g]
+        if g + plan.face_groups < FACE:
+            value = jnp.where(lanes < plan.half, value, roll_lanes(faces[g + plan.face_groups], plan.half))
+        groups.append(value)
+    rest = jnp.zeros(faces[0].shape, F32)
+    for p, face in enumerate(faces):
+        start = plan.left * p
+        inside = (lanes >= start) & (lanes < start + plan.left)
+        rest = jnp.where(inside, roll_lanes(face, start - plan.half), rest)
+    return groups + [rest]
+
+
+def unpack_face(plan, groups, p):
+    lanes = lax.broadcasted_iota(jnp.int32, (1, LANES), 1)
+    value = groups[p] if p < plan.face_groups else roll_lanes(groups[p - plan.face_groups], plan.half)
+    return jnp.where(lanes < plan.half, value, roll_lanes(groups[-1], plan.half - plan.left * p))
+
+
 def extend_kernel(plan, q_ref, own_ref, top_ref, *refs):
     count = plan.y.count - 1
-    halos, (ext_ref, top_out, partner_ref, side_ref) = refs[:count], refs[count:]
+    halos, (ext_ref, partner_ref, side_ref) = refs[:count], refs[count:]
     x, y = plan.x, plan.y
     odd = lax.axis_index("gx") % 2
     end = x.length - REACH
     near = plan.near_y(halos)
-    top = top_ref[...]
-    for halo in halos:
-        top = top + get_flat(halo, 8 * halo.shape[0] - plan.top_rows, plan.top_shape)
-    top_out[...] = top
-    put_flat(partner_ref, plan.top_row, top)
+    put_flat(partner_ref, plan.top_row, top_ref[...])
     for start, ref in ((end * odd, side_ref), (end * (1 - odd), partner_ref)):
         for i in range(REACH):
             row = plan.fine_rows * i
@@ -517,7 +544,7 @@
             for h, halo in enumerate(near):
                 ref[(row + y.length) // 8 + h] = halo[start + i]
 
-    base = [8 * halo.shape[0] - plan.top_rows - 16 * x.width[1] for halo in halos]
+    base = [8 * halo.shape[0] - 16 * x.width[1] for halo in halos]
     for i in range(x.width[1]):
         own = own_ref[i]
         parts = [plane(halo, at, 16, i) for halo, at in zip(halos, base)]
@@ -534,13 +561,15 @@
         row = plan.fine_rows * REACH + plan.coarse_rows * p
         value = jnp.where(lanes < plan.lane[2], ext_ref[start + min(p, FACE - 1)], ext_ref[p])
         put_plane(partner_ref, row, value)
+    start = (x.width[1] - FACE) * odd
+    for g, value in enumerate(pack_faces(plan, [ext_ref[start + p] for p in range(FACE)])):
+        put_plane(side_ref, plan.fine_rows * REACH + plan.coarse_rows * g, value)
 
 
 def chip_kernel(plan, ext_ref, pair_ref, top_ref, top_out, *targets):
     x, gx = plan.x, lax.axis_index("gx")
     odd, chip = gx % 2, gx // 2
     lanes = lax.broadcasted_iota(jnp.int32, (1, LANES), 1)
-    in1 = lanes < plan.lane[2]
     keep_even, keep_odd = mask(odd == 0), mask(odd == 1)
     top = top_ref[...] + get_flat(pair_ref, plan.top_row, plan.top_shape)
     top_out[...] = top
@@ -554,17 +583,20 @@
         return total
 
     second = [merged(2, c) for c in range(plan.pair_width[2])]
-    start = (x.width[1] - FACE) * odd
     chips = x.count // 2
+    high = x.length >> 2
     for k, ref in zip(range(1, chips), targets):
-        high = x.length >> 2
-        for p in range(plan.planes):
-            if chips == 2:
-                two = jnp.where(chip == 0, second[high + p], second[p])
-            else:
-                two = second[high + p] if k == 1 else second[p]
-            first = ext_ref[start + min(p, FACE - 1)]
-            put_plane(ref, plan.coarse_rows * p, jnp.where(in1, first, two))
+        for g in range(plan.pair_groups):
+            total = None
+            for slot, p in enumerate(range(3 * g, min(3 * g + 3, plan.planes))):
+                if chips == 2:
+                    two = jnp.where(chip == 0, second[high + p], second[p])
+                else:
+                    two = second[high + p] if k == 1 else second[p]
+                two = roll_lanes(two, SLOT * slot - plan.lane[2])
+                total = two if slot == 0 else jnp.where(lanes < SLOT * slot, total, two)
+            put_plane(ref, plan.coarse_rows * g, total)
+        put_flat(ref, plan.coarse_rows * plan.pair_groups, top)
 
 
 def mix_planes(get, put, count, matrix):
@@ -607,7 +639,7 @@
     return [jnp.zeros((pad, LANES), F32)] if pad else []
 
 
-def fine_inner_kernel(plan, q_ref, y_table, z_table, main_ref, push_ref, edge_ref, mixed, ready):
+def fine_inner_kernel(plan, q_ref, y_table, inner_ref, edge_ref, mixed):
     x, y = plan.x, plan.y
     halo = jnp.zeros((up(plan.fine_rows, 16) - y.length, LANES), F32)
 
@@ -621,22 +653,21 @@
     for s, sigma in enumerate(STENCIL_SIGMAS):
         row, end = s * y.length, (s + 1) * y.length
         planes = {i: mixed[i, row + 8 : end - 8, :] for i in range(x.length)}
+        step = y.length - 16
         for i, value in enumerate(stencil(planes, inner, sigma)):
-            put_ready(ready, 3, s, i * (y.length - 16), value)
+            inner_ref[s, i * step : (i + 1) * step, :] = value
         for i, value in enumerate(stencil(planes, edge, sigma)):
             edge_ref[i, row + 8 : end - 8, :] = value
         ends = lambda i: jnp.concatenate([mixed[i, row : row + 8, :], mixed[i, end - 8 : end, :]], axis=0)
         planes = {i: ends(i) for i in range(x.length)}
         for i, value in enumerate(stencil(planes, inner, sigma)):
-            put_ready(ready, 3, s, half + i * 16, value)
+            inner_ref[s, half + i * 16 : half + i * 16 + 16, :] = value
         for i, value in enumerate(stencil(planes, edge, sigma)):
             edge_ref[i, row : row + 8, :] = value[:8]
             edge_ref[i, end - 8 : end, :] = value[8:]
-    main_ref[...] = dot(ready[...], plan.z_matrix(z_table, 0), ((1,), (1,)))
-    push_ref[...] = dot(plan.z_matrix(z_table, 1), ready[...], ((1,), (1,)))
-
-
-def fine_halo_kernel(plan, edge_ref, y_table, z_table, *refs):
+
+
+def fine_halo_kernel(plan, inner_ref, edge_ref, y_table, z_table, *refs):
     halos, (main_ref, push_ref, out_ref, mixed, ready) = refs[: plan.y.count - 1], refs[plan.y.count - 1 :]
     x, y = plan.x, plan.y
     near = plan.near_y(halos)
@@ -652,11 +683,15 @@
     inner = range(REACH, x.length - REACH)
     edge = [*range(REACH), *range(x.length - REACH, x.length)]
     out_ref[...] = edge_ref[...]
+    half = len(inner) * (y.length - 16)
     for s, sigma in enumerate(STENCIL_SIGMAS):
         row, end = s * y.length, (s + 1) * y.length
         planes = {i: mixed[i, 16 * s : 16 * s + 16, :] for i in range(x.length)}
+        for start in range(0, half, 64):
+            put_ready(ready, 3, s, start, inner_ref[s, start : start + 64, :])
         for i, value in enumerate(stencil(planes, inner, sigma)):
-            put_ready(ready, 3, s, i * 16, value)
+            start = half + 16 * i
+            put_ready(ready, 3, s, start, inner_ref[s, start : start + 16, :] + value)
         for i, value in enumerate(stencil(planes, edge, sigma)):
             out_ref[i, row : row + 8, :] += value[:8]
             out_ref[i, end - 8 : end, :] += value[8:]
@@ -664,7 +699,7 @@
     push_ref[...] = dot(plan.z_matrix(z_table, 1), ready[...], ((1,), (1,)))
 
 
-def fine_edge_kernel(plan, partner_ref, side_ref, edge_ref, inner_ref, halo_ref, y_table, z_table, *refs):
+def fine_edge_kernel(plan, partner_ref, side_ref, edge_ref, inner_ref, y_table, z_table, *refs):
     main_ref, push_ref, mixed, ready = refs
     x, y = plan.x, plan.y
     gx = lax.axis_index("gx")
@@ -696,9 +731,7 @@
                 put_ready(ready, 3, s, i * y.length + r, edge_ref[i, row : row + 16, :] + value)
     main_ref[...] = dot(ready[...], plan.z_matrix(z_table, 0), ((1,), (1,)))
     pushed = dot(plan.z_matrix(z_table, 1), ready[...], ((1,), (1,)))
-    inner = inner_ref[...]
-    half = inner.shape[1] - halo_ref.shape[1]
-    push_ref[...] = jnp.concatenate([inner[:, :half], inner[:, half:] + halo_ref[...], pushed], axis=1)
+    push_ref[...] = jnp.concatenate([inner_ref[...], pushed], axis=1)
 
 
 def coarse_inner_kernel(plan, ext_ref, pair_ref, y_table, mixed):
@@ -729,39 +762,44 @@
         value = inner[own + k, row : row + rows, :]
         add(size + start + k, value, mask(odd == 0))
         add(-size + start + width - layers + k, value, mask(odd == 1))
-    for offset in range(1, chips):
-        base = plan.planes * (offset - 1)
-        at = lambda k: outer[base + k, row : row + rows, :]
+    if level == 1:
+        for k in range(FACE):
+            value = outer[k, row : row + rows, :]
+            add(-size + start + width - FACE + k, value, mask((chip > 0) & (odd == 0)))
+            add(size + start + k, value, mask((chip < chips - 1) & (odd == 1)))
+        return cells
+    for n, offset in enumerate(plan.near_chips):
         for shift, here in ((-offset, chip >= offset), (chips - offset, chip < offset)):
             if abs(shift) != 1:
                 continue
-            if level == 1:
-                keep = mask(here & (odd == (0 if shift < 0 else 1)))
-                first = -size + start + width - FACE if shift < 0 else size + start
-                for k in range(FACE):
-                    add(first + k, at(k), keep)
-                continue
             for core in (0, 1):
                 keep = mask(here & (odd == core))
-                first = 2 * size * shift - size * core + start
-                if level == 2 and shift < 0:
-                    first += size
+                first = 2 * size * shift - size * core + start + (size if shift < 0 else 0)
                 for k in range(plan.planes):
-                    add(first + k, at(k), keep)
+                    add(first + k, outer[plan.planes * n + k, row : row + rows, :], keep)
     return cells
 
 
 def coarse_kernel(plan, inner, *refs):
     chips = plan.x.count // 2 - 1
     others, refs = refs[:chips], refs[chips:]
-    push_ref, y_table, z_table, partner_ref, side_ref, e1_ref, e2_ref, outer, *ready = refs
+    side_in, push_ref, y_table, z_table, partner_ref, side_ref, e1_ref, e2_ref, outer, *ready = refs
 
     def put(i, value):
         outer[i] = value
 
-    count = plan.planes * chips
-    get = lambda i: plane(others[i // plan.planes], 0, plan.coarse_rows, i % plan.planes)
-    mix_planes(get, put, count, plan.coarse_matrix(y_table))
+    lanes = lax.broadcasted_iota(jnp.int32, (1, LANES), 1)
+    groups = [plane(side_in, plan.fine_rows * REACH, plan.coarse_rows, g) for g in range(plan.face_groups + 1)]
+
+    def get(i):
+        n, p = i // plan.planes, i % plan.planes
+        two = plane(others[plan.near_chips[n] - 1], 0, plan.coarse_rows, p // 3)
+        value = roll_lanes(two, plan.lane[2] - SLOT * (p % 3))
+        if n == 0 and p < FACE:
+            value = jnp.where(lanes < plan.lane[2], unpack_face(plan, groups, p), value)
+        return value
+
+    mix_planes(get, put, plan.planes * len(plan.near_chips), plan.coarse_matrix(y_table))
     x = plan.x
     results = []
     for level in (1, 2):
@@ -785,6 +823,14 @@
         ref[8:, 512 : 512 + plan.flat[2]] = two[start : start + 16]
 
 
+def top_chips_kernel(plan, top_ref, *refs):
+    *others, out_ref = refs
+    total = top_ref[...]
+    for ref in others:
+        total = total + get_flat(ref, plan.coarse_rows * plan.pair_groups, plan.top_shape)
+    out_ref[...] = total
+
+
 def top_kernel(plan, *refs):
     *values, out_ref = refs
     total = functools.reduce(jnp.add, [v[...] for v in values])
@@ -806,7 +852,7 @@
     out_ref[...] = result
 
 
-def finish_kernel(plan, inner_ref, halo_ref, edge_ref, e1_ref, e2_ref, *refs):
+def finish_kernel(plan, inner_ref, edge_ref, e1_ref, e2_ref, *refs):
     z = plan.z
     refs = list(refs)
     partner_ref, side_ref, e3_ref, flat, masks, tall, out_ref, e1, e2 = refs
@@ -856,15 +902,12 @@
     matrix = jnp.concatenate([last, last], axis=0)
     coarse = dot(stacked, matrix, ((0,), (0,)))
     inner = inner_ref.shape[0]
-    half = inner - halo_ref.shape[0]
     tiles = plan.y.length // 8
     for k, (x, t) in enumerate(plan.tiles()):
         row = 8 * k
         value = coarse[row : row + 8]
         if row < inner:
             value = value + inner_ref[row : row + 8]
-            if row >= half:
-                value = value + halo_ref[row - half : row - half + 8]
         else:
             value = value + edge_ref[row - inner : row - inner + 8]
         out_ref[8 * (tiles * x + t) : 8 * (tiles * x + t) + 8] = value
@@ -912,7 +955,7 @@
     partner_z = lambda v: swap(v, ("gx", "gz"), lambda i, j: (i, j ^ 1))
     across_z = lambda v: swap(v, ("gx", "gz"), lambda i, j: (i ^ 1, j) if side_z(j) is None else (i, side_z(j)))
 
-    rows_y = 8 * x.length + 16 * x.width[1] + plan.top_rows
+    rows_y = 8 * x.length + 16 * x.width[1]
     table = plan.restrict_tables()
     own, top, charges, y_table, top_table, *to_y = call(
         restrict_kernel,
@@ -934,42 +977,43 @@
         value = value if offset in (1, y.count - 1) else value[x.length :]
         from_y.append(shift(value, "gy", offset))
 
+    tops = [swap(top, ("gx", "gz"), lambda i, j, m=m: (i, j ^ m)) for m in range(1, z.count)]
+    (top,) = call(top_z_kernel, plan, [top, *tops, top_table], [array(*plan.top_shape)])
+
     z_table = plan.z_tables()
     inner_cells = (x.length - 2 * REACH) * y.length
     edge_cells = 2 * REACH * y.length
-    main_inner, push_inner, edge = call(
+    inner, edge = call(
         fine_inner_kernel,
         plan,
-        [charges, y_table, z_table],
-        [array(inner_cells, z.length), array(16, inner_cells), array(2 * REACH, 3 * y.length, LANES)],
-        [vmem(x.length, 3 * y.length, LANES), ready(inner_cells, 3)],
+        [charges, y_table],
+        [array(3, inner_cells, LANES), array(2 * REACH, 3 * y.length, LANES)],
+        [vmem(x.length, 3 * y.length, LANES)],
     )
     edge, *from_y = lax.optimization_barrier((edge, *from_y))
 
-    ext, top, to_partner, to_side = call(
+    ext, to_partner, to_side = call(
         extend_kernel,
         plan,
         [charges, own, top, *from_y],
         [
             array(x.width[1], plan.coarse_rows, LANES),
-            array(*plan.top_shape),
             array((plan.top_row + plan.top_rows) // 8, 8, LANES),
-            array(REACH * plan.fine_rows // 8, 8, LANES),
+            array(plan.side_rows // 8, 8, LANES),
         ],
     )
     from_side, pair = across_x(to_side), partner_x(to_partner)
 
-    halo_cells = (x.length - 2 * REACH) * 16
-    main_halo, push_halo, edge = call(
+    main_inner, push_inner, edge = call(
         fine_halo_kernel,
         plan,
-        [edge, y_table, z_table, *from_y],
-        [array(halo_cells, z.length), array(16, halo_cells), array(2 * REACH, 3 * y.length, LANES)],
-        [vmem(x.length, plan.halo_rows, LANES), ready(halo_cells, 3)],
+        [inner, edge, y_table, z_table, *from_y],
+        [array(inner_cells, z.length), array(16, inner_cells), array(2 * REACH, 3 * y.length, LANES)],
+        [vmem(x.length, plan.halo_rows, LANES), ready(inner_cells, 3)],
     )
 
     chips = x.count // 2
-    rows_x = plan.planes * plan.coarse_rows
+    rows_x = plan.pair_groups * plan.coarse_rows + plan.top_rows
     top, *to_chips = call(
         chip_kernel,
         plan,
@@ -985,35 +1029,31 @@
         coarse_inner_kernel, plan, [ext, pair, y_table], [array(planes_inner, plan.rows_mixed, LANES)]
     )
 
-    tops = [swap(top, ("gx", "gz"), lambda i, j, m=m: (i, j ^ m)) for m in range(1, z.count)]
-    (top,) = call(top_z_kernel, plan, [top, *tops, top_table], [array(2 * plan.tall[3], plan.flat_top)])
-
     main_edge, push = call(
         fine_edge_kernel,
         plan,
-        [pair, from_side, edge, push_inner, push_halo, y_table, z_table],
+        [pair, from_side, edge, push_inner, y_table, z_table],
         [array(edge_cells, z.length), array(16, x.length * y.length)],
         [vmem(2 * REACH, 3 * y.length, LANES), ready(edge_cells, 3)],
     )
-    push, top = lax.optimization_barrier((push, top))
     window = lambda level: array(plan.tall[level], plan.flat[level])
     to_partner, to_side, e1, e2 = call(
         coarse_kernel,
         plan,
-        [mixed_inner, *from_chips, push, y_table, z_table],
+        [mixed_inner, *from_chips, from_side, push, y_table, z_table],
         [array(24, 1024), array(24, 1024), window(1), window(2)],
-        [vmem(plan.planes * (chips - 1), plan.rows_mixed, LANES), ready(plan.flat[1], 3), ready(plan.flat[2], 3)],
+        [vmem(plan.planes * len(plan.near_chips), plan.rows_mixed, LANES), ready(plan.flat[1], 3), ready(plan.flat[2], 3)],
     )
     from_near = [partner_z(to_partner), across_z(to_side)]
 
-    chip_swap = lambda k: lambda i, j: ((i + 2 * k) % x.count ^ 1, j)
-    tops = [top] + [swap(top, ("gx", "gy"), chip_swap(k)) for k in range(1, chips)]
+    (top,) = call(top_chips_kernel, plan, [top, *from_chips], [array(*top.shape)])
+    tops = [top] + [shift(top, "gy", offset) for offset in range(1, y.count)]
     (e3,) = call(top_kernel, plan, tops, [window(3)])
 
     (potential,) = call(
         finish_kernel,
         plan,
-        [main_inner, main_halo, main_edge, e1, e2, *from_near, e3, *plan.finish()],
+        [main_inner, main_edge, e1, e2, *from_near, e3, *plan.finish()],
         [array(x.length * y.length, z.length)],
         [vmem(plan.tall[level], plan.flat[level]) for level in (1, 2)],
     )

time: 35.6 us -> 32.4 us (0.910)
  local copies, waits for them, and re-layouts: 4.1 us -> 2.37 us
  starting transfers between devices: 13.4 us -> 11.9 us
  waiting for transfers between devices: 7.36 us -> 8 us
    ppermute x9 -> x8, starting transfers between devices: 10.4 us -> 7.53 us  [swap(): return lax.ppermute(value, axes, pairs)]
    unnamed x14 -> x12, local copies, waits for them, and re-layouts: 4.1 us -> 2.37 us
    ppermute x1 -> x2, starting transfers between devices: 2.95 us -> 4.4 us  [shift(): lax.ppermute(value, axis, [(i, (i + offset) % count) for i in range(count)])]
    ppermute x9 -> x8, waiting for transfers between devices: 4.25 us -> 5.61 us  [swap(): return lax.ppermute(value, axes, pairs)]
    ppermute x1 -> x2, waiting for transfers between devices: 3.11 us -> 2.38 us  [shift(): lax.ppermute(value, axis, [(i, (i + offset) % count) for i in range(count)])]
    pallas_call x11 -> x12, Pallas kernels: 10.2 us -> 9.87 us  [call(): pl.pallas_call(functools.partial(kernel, plan), in_specs=[whole] * len(op...]
  transfers between devices with their start and end apart: 10 -> 10, of which waited for: 4 -> 5; matrix products, arithmetic and copies ran while one was open for 0% -> 0% of each run, Pallas kernels for 15% -> 15%
where the time goes in v4:
time: 32.4 us; the launch traced here: 32.3 us
  starting transfers between devices  11.9 us (37%)
  Pallas kernels  9.87 us (30%)
  waiting for transfers between devices  8 us (25%)
  local copies, waits for them, and re-layouts  2.37 us (7%)
    pallas_call x12, Pallas kernels, call(): pl.pallas_call(functools.partial(kernel, plan), in_specs=[whole] * len(op...  9.87 us
    ppermute x8, starting transfers between devices, swap(): return lax.ppermute(value, axes, pairs)  7.53 us
    ppermute x8, waiting for transfers between devices, swap(): return lax.ppermute(value, axes, pairs)  5.61 us
    ppermute x2, starting transfers between devices, shift(): lax.ppermute(value, axis, [(i, (i + offset) % count) for i in range(count)])  4.4 us
    ppermute x2, waiting for transfers between devices, shift(): lax.ppermute(value, axis, [(i, (i + offset) % count) for i in range(count)])  2.38 us
    unnamed x12, local copies, waits for them, and re-layouts  2.37 us
  transfers between devices with their start and end apart: 10, of which 5 were waited for; matrix products, arithmetic and copies ran while one was open for 0% of the time, Pallas kernels for 15%

profile of v4, /device:TPU:0, one launch (start us, length us, event | category | flops | bytes accessed | tf_op | source)
XLA Modules:
  0.0 32.3 jit_solution(6335957704335420790)
XLA Ops:
  0.0 1.3 %copy-done.2 = bf16[212,16,128]{2,1,0:T(8,128)(2,1)S(1)} copy-done((bf16[212,16,128]{2,1,0:T(8,128)(2,1)S(1)}, bf16[212,16,128]{2,1,0:T(8,128)(2,1)}, u32[]{:S(2)}) %copy-start.2) | copy-done | bytes 868376
  1.3 1.0 %copy-done.3 = f32[32,32,128]{2,1,0:T(8,128)S(1)} copy-done((f32[32,32,128]{2,1,0:T(8,128)S(1)}, f32[32,32,128]{2,1,0:T(8,128)}, u32[]{:S(2)}) %copy-start.3) | copy-done | bytes 524312
  2.4 0.8 %shard_map.64 = (f32[19,24,128]{2,1,0:T(8,128)S(1)}, f32[24,128]{1,0:T(8,128)S(1)}, f32[32,32,128]{2,1,0:T(8,128)S(1)}, bf16[272,256]{1,0:T(8,128)(2,1)S(1)}, bf...) custom-call(f32[32,32,128]{2,1,0:T(8,128)S(1)} %copy-done.3, bf16[212,16,128]{2,1,0:T(8,128)(2,1)S(1)} %copy-done.2), custom_call_target="tpu_custom_call" | custom-call | tf_op jit(solution)/shard_map/pallas_call | solution.py:918
  3.2 3.0 %collective-permute-start = (f32[70,8,128]{2,1,0:T(8,128)S(1)}, f32[70,8,128]{2,1,0:T(8,128)S(1)}, u32[]{:S(2)}, u32[]{:S(2)}) collective-permute-start(f32[70,8,128]{2,1,0:T(8,128)S(1)} %get-tuple-element.33), channel_id=1, source_target_pairs={{0,4},{4,0},{1,5},{5,1},{2,6},{6,2},{3,7},{7,3},{8,12},{12,8},{9,1... | collective-permute-start | bytes 860168 | tf_op jit(solution)/shard_map/ppermute | solution.py:930
  6.1 3.6 %collective-permute-start.3 = (f32[24,128]{1,0:T(8,128)S(1)}, f32[24,128]{1,0:T(8,128)S(1)}, u32[]{:S(2)}, u32[]{:S(2)}) collective-permute-start(f32[24,128]{1,0:T(8,128)S(1)} %get-tuple-element.38.own_ref), channel_id=1, source_target_pairs={{0,3},{1,2},{2,1},{3,0},{8,11},{9,10},{10,9},{11,8},{16,19},{17,18... | collective-permute-start | bytes 36872 | tf_op jit(solution)/shard_map/ppermute | solution.py:940
  9.7 0.8 %collective-permute-start.1 = (f32[24,128]{1,0:T(8,128)S(1)}, f32[24,128]{1,0:T(8,128)S(1)}, u32[]{:S(2)}, u32[]{:S(2)}) collective-permute-start(f32[24,128]{1,0:T(8,128)S(1)} %get-tuple-element.38.own_ref), channel_id=1, source_target_pairs={{0,1},{1,0},{2,3},{3,2},{8,9},{9,8},{10,11},{11,10},{16,17},{17,16... | collective-permute-start | bytes 36872 | tf_op jit(solution)/shard_map/ppermute | solution.py:940
  10.5 1.3 %shard_map.65 = (f32[3,512,128]{2,1,0:T(8,128)S(1)}, f32[16,96,128]{2,1,0:T(8,128)S(1)}) custom-call(f32[32,32,128]{2,1,0:T(8,128)S(1)} %get-tuple-element.29.q_ref, bf16[272,256]{1,0:T(8,128)(2,1)S(1)} %get-tuple-element.30.y_table.refs_3_), custom_call_target="tpu_custom_call" | custom-call | tf_op jit(solution)/shard_map/pallas_call | solution.py:918
  11.8 2.5 %collective-permute-done.2.refs_1_ = f32[24,128]{1,0:T(8,128)S(1)} collective-permute-done((f32[24,128]{1,0:T(8,128)S(1)}, f32[24,128]{1,0:T(8,128)S(1)}, u32[]{:S(2)}, u32[]{:S(2)}) %collective-permute-start.2) | collective-permute-done | bytes 12320 | tf_op jit(solution)/shard_map/ppermute | solution.py:940
  14.5 0.2 shard_map.68
  14.7 0.6 %collective-permute-start.5 = (f32[68,8,128]{2,1,0:T(8,128)S(1)}, f32[68,8,128]{2,1,0:T(8,128)S(1)}, u32[]{:S(2)}, u32[]{:S(2)}) collective-permute-start(f32[68,8,128]{2,1,0:T(8,128)S(1)} %get-tuple-element.41), channel_id=1, source_target_pairs={{0,4},{4,0},{8,16},{12,20},{16,8},{20,12},{24,28},{28,24},{1,5},{5... | collective-permute-start | bytes 835592 | tf_op jit(solution)/shard_map/ppermute | solution.py:940
  15.3 1.1 %collective-permute-done.4.partner_ref.pair_ref = f32[98,8,128]{2,1,0:T(8,128)S(1)} collective-permute-done((f32[98,8,128]{2,1,0:T(8,128)S(1)}, f32[98,8,128]{2,1,0:T(8,128)S(1)}, u32[]{:S(2)}, u32[]{:S(2)}) %collective-permute-start.4) | collective-permute-done | bytes 401440 | tf_op jit(solution)/shard_map/ppermute | solution.py:940
  16.6 1.3 %collective-permute-start.6 = (f32[26,8,128]{2,1,0:T(8,128)S(1)}, f32[26,8,128]{2,1,0:T(8,128)S(1)}, u32[]{:S(2)}, u32[]{:S(2)}) collective-permute-start(f32[26,8,128]{2,1,0:T(8,128)S(1)} %get-tuple-element.46), channel_id=1, source_target_pairs={{0,24},{4,28},{8,16},{12,20},{16,8},{20,12},{24,0},{28,4},{1,25},{... | collective-permute-start | bytes 319496 | tf_op jit(solution)/shard_map/ppermute | solution.py:940
  17.9 1.5 %shard_map.66 = (f32[512,128]{1,0:T(8,128)S(1)}, f32[16,512]{1,0:T(8,128)S(1)}, f32[16,96,128]{2,1,0:T(8,128)S(1)}) custom-call(f32[3,512,128]{2,1,0:T(8,128)S(1)} %get-tuple-element.31.inner_ref, f32[16,96,128]{2,1,0:T(8,128)S(1)} %get-tuple-element.34.edge_ref, bf16[272,256]{1,0:T(8,128)(2,1)S(1)} %get-tuple-element.30.y_table.refs_3_, ...), custom_call_target="tpu_custom_call" | custom-call | tf_op jit(solution)/shard_map/pallas_call | solution.py:918
  19.4 0.4 %shard_map.70.inner = f32[32,128,128]{2,1,0:T(8,128)S(1)} custom-call(f32[19,32,128]{2,1,0:T(8,128)S(1)} %get-tuple-element.45.ext_ref, f32[98,8,128]{2,1,0:T(8,128)S(1)} %collective-permute-done.4.partner_ref.pair_ref, bf16[272,256]{1,0:T(8,128)(2,1)S(1)} %get-tuple-element.30.y_table.refs_3_), custom_call_target="tpu_custom_call" | custom-call | tf_op jit(solution)/shard_map/pallas_call | solution.py:918
  19.9 1.5 %collective-permute-done.5.side_ref.refs_1_ = f32[68,8,128]{2,1,0:T(8,128)S(1)} collective-permute-done((f32[68,8,128]{2,1,0:T(8,128)S(1)}, f32[68,8,128]{2,1,0:T(8,128)S(1)}, u32[]{:S(2)}, u32[]{:S(2)}) %collective-permute-start.5) | collective-permute-done | bytes 278560 | tf_op jit(solution)/shard_map/ppermute | solution.py:940
  21.3 1.2 %shard_map.69 = (f32[512,128]{1,0:T(8,128)S(1)}, f32[16,1024]{1,0:T(8,128)S(1)}) custom-call(f32[98,8,128]{2,1,0:T(8,128)S(1)} %collective-permute-done.4.partner_ref.pair_ref, f32[68,8,128]{2,1,0:T(8,128)S(1)} %collective-permute-done.5.side_ref.refs_1_, f32[16,96,128]{2,1,0:T(8,128)S(1)} %get-tuple-element.42.edge_ref, ...), custom_call_target="tpu_custom_call" | custom-call | tf_op jit(solution)/shard_map/pallas_call | solution.py:918
  22.6 1.9 %shard_map.72 = (f32[24,1024]{1,0:T(8,128)S(1)}, f32[24,1024]{1,0:T(8,128)S(1)}, f32[72,456]{1,0:T(8,128)S(1)}, f32[40,208]{1,0:T(8,128)S(1)}) custom-call(f32[32,128,128]{2,1,0:T(8,128)S(1)} %shard_map.70.inner, f32[26,8,128]{2,1,0:T(8,128)S(1)} %collective-permute-done.6.refs_0_, f32[68,8,128]{2,1,0:T(8,128)S(1)} %collective-permute-done.5.side_ref.refs_1_, ...), custom_call_target="tpu_custom_call" | custom-call | tf_op jit(solution)/shard_map/pallas_call | solution.py:918
  24.5 0.4 %collective-permute-start.7 = (f32[24,1024]{1,0:T(8,128)S(1)}, f32[24,1024]{1,0:T(8,128)S(1)}, u32[]{:S(2)}, u32[]{:S(2)}) collective-permute-start(f32[24,1024]{1,0:T(8,128)S(1)} %get-tuple-element.50), channel_id=1, source_target_pairs={{0,1},{1,0},{2,3},{3,2},{8,9},{9,8},{10,11},{11,10},{16,17},{17,16... | collective-permute-start | bytes 294920 | tf_op jit(solution)/shard_map/ppermute | solution.py:940
  24.9 0.8 %collective-permute-start.8 = (f32[24,1024]{1,0:T(8,128)S(1)}, f32[24,1024]{1,0:T(8,128)S(1)}, u32[]{:S(2)}, u32[]{:S(2)}) collective-permute-start(f32[24,1024]{1,0:T(8,128)S(1)} %get-tuple-element.51), channel_id=1, source_target_pairs={{0,8},{1,2},{2,1},{3,11},{8,0},{9,10},{10,9},{11,3},{16,24},{17,18... | collective-permute-start | bytes 294920 | tf_op jit(solution)/shard_map/ppermute | solution.py:940
  25.7 1.4 %collective-permute-start.9 = (f32[48,128]{1,0:T(8,128)S(1)}, f32[48,128]{1,0:T(8,128)S(1)}, u32[]{:S(2)}, u32[]{:S(2)}) collective-permute-start(f32[48,128]{1,0:T(8,128)S(1)} %shard_map.73.refs_0_), channel_id=1, source_target_pairs={{0,4},{4,0},{1,5},{5,1},{2,6},{6,2},{3,7},{7,3},{8,12},{12,8},{9,1... | collective-permute-start | bytes 73736 | tf_op jit(solution)/shard_map/ppermute | solution.py:930
  27.1 2.4 %collective-permute-done.9.refs_1_ = f32[48,128]{1,0:T(8,128)S(1)} collective-permute-done((f32[48,128]{1,0:T(8,128)S(1)}, f32[48,128]{1,0:T(8,128)S(1)}, u32[]{:S(2)}, u32[]{:S(2)}) %collective-permute-start.9) | collective-permute-done | bytes 24608 | tf_op jit(solution)/shard_map/ppermute | solution.py:930
  29.5 0.2 shard_map.74.refs_2_
  29.7 0.5 %collective-permute-done.7.refs_0_ = f32[24,1024]{1,0:T(8,128)S(1)} collective-permute-done((f32[24,1024]{1,0:T(8,128)S(1)}, f32[24,1024]{1,0:T(8,128)S(1)}, u32[]{:S(2)}, u32[]{:S(2)}) %collective-permute-start.7) | collective-permute-done | bytes 98336 | tf_op jit(solution)/shard_map/ppermute | solution.py:940
  30.2 2.0 %shard_map.75 = f32[1024,128]{1,0:T(8,128)} custom-call(f32[512,128]{1,0:T(8,128)S(1)} %get-tuple-element.36.inner_ref, f32[512,128]{1,0:T(8,128)S(1)} %get-tuple-element.44.edge_ref, f32[72,456]{1,0:T(8,128)S(1)} %get-tuple-element.48.e1_ref, f32[40,208]{1,0:T(8,128)S(1)} %get-tuple-element.49.e2_ref, f32[24,1024]{1,0:T(8,128)S(1)} %collective-permute-done.7.refs_0_, ...), custom_call_target="tpu_custom_call" | custom-call | tf_op jit(solution)/shard_map/pallas_call | solution.py:918
  (20 shorter events, 0.4 us)
Async XLA Ops:
  0.0 17.9 %copy-start = (bf16[4,336,1152]{2,1,0:T(8,128)(2,1)S(1)}, bf16[4,336,1152]{2,1,0:T(8,128)(2,1)}, u32[]{:S(2)}) copy-start(bf16[4,336,1152]{2,1,0:T(8,128)(2,1)} %constant.11.clone.z_table.refs_4_) | copy-start | bytes 9289732
  0.0 1.3 %copy-start.2 = (bf16[212,16,128]{2,1,0:T(8,128)(2,1)S(1)}, bf16[212,16,128]{2,1,0:T(8,128)(2,1)}, u32[]{:S(2)}) copy-start(bf16[212,16,128]{2,1,0:T(8,128)(2,1)} %constant.10.clone.table_ref) | copy-start | bytes 2605060
  1.3 1.0 %copy-start.3 = (f32[32,32,128]{2,1,0:T(8,128)S(1)}, f32[32,32,128]{2,1,0:T(8,128)}, u32[]{:S(2)}) copy-start(f32[32,32,128]{2,1,0:T(8,128)} %q_ref.1) | copy-start | bytes 1572868
  3.2 11.3 %collective-permute-start = (f32[70,8,128]{2,1,0:T(8,128)S(1)}, f32[70,8,128]{2,1,0:T(8,128)S(1)}, u32[]{:S(2)}, u32[]{:S(2)}) collective-permute-start(f32[70,8,128]{2,1,0:T(8,128)S(1)} %get-tuple-element.33), channel_id=1, source_target_pairs={{0,4},{4,0},{1,5},{5,1},{2,6},{6,2},{3,7},{7,3},{8,12},{12,8},{9,1... | collective-permute-start | bytes 860168 | tf_op jit(solution)/shard_map/ppermute | solution.py:930
  6.1 5.7 %collective-permute-start.3 = (f32[24,128]{1,0:T(8,128)S(1)}, f32[24,128]{1,0:T(8,128)S(1)}, u32[]{:S(2)}, u32[]{:S(2)}) collective-permute-start(f32[24,128]{1,0:T(8,128)S(1)} %get-tuple-element.38.own_ref), channel_id=1, source_target_pairs={{0,3},{1,2},{2,1},{3,0},{8,11},{9,10},{10,9},{11,8},{16,19},{17,18... | collective-permute-start | bytes 36872 | tf_op jit(solution)/shard_map/ppermute | solution.py:940
  9.7 4.6 %collective-permute-start.2 = (f32[24,128]{1,0:T(8,128)S(1)}, f32[24,128]{1,0:T(8,128)S(1)}, u32[]{:S(2)}, u32[]{:S(2)}) collective-permute-start(f32[24,128]{1,0:T(8,128)S(1)} %get-tuple-element.38.own_ref), channel_id=1, source_target_pairs={{0,2},{1,3},{2,0},{3,1},{8,10},{9,11},{10,8},{11,9},{16,18},{17,19... | collective-permute-start | bytes 36872 | tf_op jit(solution)/shard_map/ppermute | solution.py:940
  9.7 4.6 %collective-permute-start.1 = (f32[24,128]{1,0:T(8,128)S(1)}, f32[24,128]{1,0:T(8,128)S(1)}, u32[]{:S(2)}, u32[]{:S(2)}) collective-permute-start(f32[24,128]{1,0:T(8,128)S(1)} %get-tuple-element.38.own_ref), channel_id=1, source_target_pairs={{0,1},{1,0},{2,3},{3,2},{8,9},{9,8},{10,11},{11,10},{16,17},{17,16... | collective-permute-start | bytes 36872 | tf_op jit(solution)/shard_map/ppermute | solution.py:940
  14.7 1.8 %collective-permute-start.4 = (f32[98,8,128]{2,1,0:T(8,128)S(1)}, f32[98,8,128]{2,1,0:T(8,128)S(1)}, u32[]{:S(2)}, u32[]{:S(2)}) collective-permute-start(f32[98,8,128]{2,1,0:T(8,128)S(1)} %get-tuple-element.40), channel_id=1, source_target_pairs={{0,8},{4,12},{8,0},{12,4},{16,24},{20,28},{24,16},{28,20},{1,9},{5... | collective-permute-start | bytes 1204232 | tf_op jit(solution)/shard_map/ppermute | solution.py:940
  14.7 6.6 %collective-permute-start.5 = (f32[68,8,128]{2,1,0:T(8,128)S(1)}, f32[68,8,128]{2,1,0:T(8,128)S(1)}, u32[]{:S(2)}, u32[]{:S(2)}) collective-permute-start(f32[68,8,128]{2,1,0:T(8,128)S(1)} %get-tuple-element.41), channel_id=1, source_target_pairs={{0,4},{4,0},{8,16},{12,20},{16,8},{20,12},{24,28},{28,24},{1,5},{5... | collective-permute-start | bytes 835592 | tf_op jit(solution)/shard_map/ppermute | solution.py:940
  16.6 6.0 %collective-permute-start.6 = (f32[26,8,128]{2,1,0:T(8,128)S(1)}, f32[26,8,128]{2,1,0:T(8,128)S(1)}, u32[]{:S(2)}, u32[]{:S(2)}) collective-permute-start(f32[26,8,128]{2,1,0:T(8,128)S(1)} %get-tuple-element.46), channel_id=1, source_target_pairs={{0,24},{4,28},{8,16},{12,20},{16,8},{20,12},{24,0},{28,4},{1,25},{... | collective-permute-start | bytes 319496 | tf_op jit(solution)/shard_map/ppermute | solution.py:940
  22.6 7.7 %copy-start.1 = (bf16[816,1024]{1,0:T(8,128)(2,1)S(1)}, bf16[816,1024]{1,0:T(8,128)(2,1)}, u32[]{:S(2)}) copy-start(bf16[816,1024]{1,0:T(8,128)(2,1)} %constant.12.clone.refs_3_) | copy-start | bytes 5013508
  22.6 7.7 %copy-start.4 = (bf16[4,224,128]{2,1,0:T(8,128)(2,1)S(1)}, bf16[4,224,128]{2,1,0:T(8,128)(2,1)}, u32[]{:S(2)}) copy-start(bf16[4,224,128]{2,1,0:T(8,128)(2,1)} %constant.14.clone.refs_5_) | copy-start | bytes 688132
  22.6 7.7 %copy-start.5 = (f32[8,8,512]{2,1,0:T(8,128)S(1)}, f32[8,8,512]{2,1,0:T(8,128)}, u32[]{:S(2)}) copy-start(f32[8,8,512]{2,1,0:T(8,128)} %constant.13.clone.refs_4_) | copy-start | bytes 393220
  24.5 5.7 %collective-permute-start.7 = (f32[24,1024]{1,0:T(8,128)S(1)}, f32[24,1024]{1,0:T(8,128)S(1)}, u32[]{:S(2)}, u32[]{:S(2)}) collective-permute-start(f32[24,1024]{1,0:T(8,128)S(1)} %get-tuple-element.50), channel_id=1, source_target_pairs={{0,1},{1,0},{2,3},{3,2},{8,9},{9,8},{10,11},{11,10},{16,17},{17,16... | collective-permute-start | bytes 294920 | tf_op jit(solution)/shard_map/ppermute | solution.py:940
  24.9 5.3 %collective-permute-start.8 = (f32[24,1024]{1,0:T(8,128)S(1)}, f32[24,1024]{1,0:T(8,128)S(1)}, u32[]{:S(2)}, u32[]{:S(2)}) collective-permute-start(f32[24,1024]{1,0:T(8,128)S(1)} %get-tuple-element.51), channel_id=1, source_target_pairs={{0,8},{1,2},{2,1},{3,11},{8,0},{9,10},{10,9},{11,3},{16,24},{17,18... | collective-permute-start | bytes 294920 | tf_op jit(solution)/shard_map/ppermute | solution.py:940
  25.7 3.8 %collective-permute-start.9 = (f32[48,128]{1,0:T(8,128)S(1)}, f32[48,128]{1,0:T(8,128)S(1)}, u32[]{:S(2)}, u32[]{:S(2)}) collective-permute-start(f32[48,128]{1,0:T(8,128)S(1)} %shard_map.73.refs_0_), channel_id=1, source_target_pairs={{0,4},{4,0},{1,5},{5,1},{2,6},{6,2},{3,7},{7,3},{8,12},{12,8},{9,1... | collective-permute-start | bytes 73736 | tf_op jit(solution)/shard_map/ppermute | solution.py:930

commit v5 on v4

--- a/solution.py
+++ b/solution.py
@@ -699,69 +699,93 @@
     push_ref[...] = dot(plan.z_matrix(z_table, 1), ready[...], ((1,), (1,)))
 
 
-def fine_edge_kernel(plan, partner_ref, side_ref, edge_ref, inner_ref, y_table, z_table, *refs):
-    main_ref, push_ref, mixed, ready = refs
+def fine_edge_kernel(plan, halo_ref, edge_ref, y_table, z_table, push_ref, ready_ref, mixed, *, partner):
     x, y = plan.x, plan.y
     gx = lax.axis_index("gx")
-    odd = gx % 2 == 1
-    from_partner = mask(odd), mask(~odd)
-    from_side = mask(~odd & (gx > 0)), mask(odd & (gx < x.count - 1))
+    odd = gx % 2
+    high = 1 - odd if partner else odd
+    keep = mask(True) if partner else mask(jnp.where(high == 1, gx < x.count - 1, gx > 0))
     padding = fine_padding(plan)
-
-    def get(i):
-        blocks = []
-        for k in range(plan.fine_rows // 8):
-            at = plan.fine_rows // 8 * (i % REACH) + k
-            blocks.append(partner_ref[at] * from_partner[i // REACH] + side_ref[at] * from_side[i // REACH])
-        return jnp.concatenate(blocks + padding, axis=0)
-
-    def put(i, value):
-        mixed[i] = value
-
-    mix_planes(get, put, 2 * REACH, plan.fine_matrix(y_table))
+    away = lambda k: jnp.where(high == 1, k, REACH - 1 - k)
+
+    def get(k):
+        return jnp.concatenate([plane(halo_ref, 0, plan.fine_rows, away(k)) * keep] + padding, axis=0)
+
+    def put(k, value):
+        mixed[k] = value
+
+    mix_planes(get, put, REACH, plan.fine_matrix(y_table))
     for s, sigma in enumerate(STENCIL_SIGMAS):
         for r in range(0, y.length, 16):
             row = s * y.length + r
-            at = lambda i: mixed[i, row : row + 16, :]
-            before = {k - REACH: at(k) for k in range(REACH)}
-            after = {x.length + k: at(REACH + k) for k in range(REACH)}
-            added = stencil(before, range(REACH), sigma)
-            added += stencil(after, range(x.length - REACH, x.length), sigma)
-            for i, value in enumerate(added):
-                put_ready(ready, 3, s, i * y.length + r, edge_ref[i, row : row + 16, :] + value)
-    main_ref[...] = dot(ready[...], plan.z_matrix(z_table, 0), ((1,), (1,)))
-    pushed = dot(plan.z_matrix(z_table, 1), ready[...], ((1,), (1,)))
-    push_ref[...] = jnp.concatenate([inner_ref[...], pushed], axis=1)
-
-
-def coarse_inner_kernel(plan, ext_ref, pair_ref, y_table, mixed):
+            after = {REACH + k: mixed[k, row : row + 16, :] for k in range(REACH)}
+            for i, added in enumerate(stencil(after, range(REACH), sigma)):
+                value = edge_ref[away(i) + REACH * high, row : row + 16, :] + added
+                top, low = split(value)
+                at = away(i) * (y.length // 16) + r // 16
+                for c, part in enumerate((top, low, top)):
+                    start = (3 * c + s) * LANES
+                    ready_ref[at, :, start : start + LANES] = part
+    whole = ready_ref[...].reshape(REACH * y.length, 9 * LANES)
+    push_ref[...] = dot(plan.z_matrix(z_table, 1), whole, ((1,), (1,)))
+
+
+def fine_main_kernel(plan, partner_ref, side_ref, z_table, out_ref):
+    odd = lax.axis_index("gx") % 2
+    for ref, at in ((partner_ref, 1 - odd), (side_ref, odd)):
+        whole = ref[...].reshape(REACH * plan.y.length, 9 * LANES)
+        out_ref[at] = dot(whole, plan.z_matrix(z_table, 0), ((1,), (1,)))
+
+
+def coarse_inner_kernel(plan, ext_ref, pair_ref, y_table, *refs):
+    *parts, mixed = refs
     own = plan.x.width[1]
 
     def put(i, value):
         mixed[i] = value
 
-    mix_planes(lambda i: ext_ref[i] if i < own else plan.pair_plane(pair_ref, i - own), put, own + plan.planes, plan.coarse_matrix(y_table))
-
-
-def collect(plan, level, inner, outer, row, rows):
-    x, gx = plan.x, lax.axis_index("gx")
-    odd, chip, chips = gx % 2, gx // 2, plan.x.count // 2
-    size, width = x.length >> level, x.width[level]
-    start = LOW[level]
-    reach = REACH
-    cells = {start + k: inner[k, row : row + rows, :] for k in range(width)}
+    get = lambda i: ext_ref[i] if i < own else plan.pair_plane(pair_ref, i - own)
+    mix_planes(get, put, own + plan.planes, plan.coarse_matrix(y_table))
+    for level, part in zip((1, 2), parts):
+        rows, width = (plan.rows1, plan.rows2)[level - 1], plan.x.width[level]
+        wanted = range(LOW[level], LOW[level] + width)
+        for s, sigma in enumerate(STENCIL_SIGMAS):
+            for r in range(0, rows, 8):
+                cells = collect_inner(plan, level, mixed, plan.group[level] + s * rows + r, 8)
+                for i, value in enumerate(stencil(cells, wanted, sigma)):
+                    part[s * width + i, r : r + 8, :] = value
+
+
+def adder(plan, level, cells):
+    start, width = LOW[level], plan.x.width[level]
 
     def add(cell, value, keep):
-        if start - reach <= cell < start + width + reach:
+        if start - REACH <= cell < start + width + REACH:
             value = value * keep
             cells[cell] = cells[cell] + value if cell in cells else value
 
-    own = x.width[1]
+    return add
+
+
+def collect_inner(plan, level, inner, row, rows):
+    x, odd = plan.x, lax.axis_index("gx") % 2
+    size, width, start, own = x.length >> level, x.width[level], LOW[level], x.width[1]
+    cells = {start + k: inner[k, row : row + rows, :] for k in range(width)}
+    add = adder(plan, level, cells)
     layers = FACE if level == 1 else width
     for k in range(layers):
         value = inner[own + k, row : row + rows, :]
         add(size + start + k, value, mask(odd == 0))
         add(-size + start + width - layers + k, value, mask(odd == 1))
+    return cells
+
+
+def collect_outer(plan, level, outer, row, rows):
+    x, gx = plan.x, lax.axis_index("gx")
+    odd, chip, chips = gx % 2, gx // 2, plan.x.count // 2
+    size, width, start = x.length >> level, x.width[level], LOW[level]
+    cells = {}
+    add = adder(plan, level, cells)
     if level == 1:
         for k in range(FACE):
             value = outer[k, row : row + rows, :]
@@ -780,10 +804,11 @@
     return cells
 
 
-def coarse_kernel(plan, inner, *refs):
+def coarse_kernel(plan, part1, part2, *refs):
     chips = plan.x.count // 2 - 1
     others, refs = refs[:chips], refs[chips:]
-    side_in, push_ref, y_table, z_table, partner_ref, side_ref, e1_ref, e2_ref, outer, *ready = refs
+    side_in, *pushes = refs[:4]
+    y_table, z_table, partner_ref, side_ref, e1_ref, e2_ref, outer, *ready = refs[4:]
 
     def put(i, value):
         outer[i] = value
@@ -807,15 +832,19 @@
         wanted = range(LOW[level], LOW[level] + x.width[level])
         for s, sigma in enumerate(STENCIL_SIGMAS):
             for r in range(0, rows, 8):
-                cells = collect(plan, level, inner, outer, plan.group[level] + s * rows + r, 8)
-                for i, value in enumerate(stencil(cells, wanted, sigma)):
-                    put_ready(ready[level - 1], 3, s, i * rows + r, value)
+                cells = collect_outer(plan, level, outer, plan.group[level] + s * rows + r, 8)
+                for i, added in enumerate(stencil(cells, wanted, sigma)):
+                    value = (part1, part2)[level - 1][s * x.width[level] + i, r : r + 8, :]
+                    put_ready(ready[level - 1], 3, s, i * rows + r, value if added is None else value + added)
         results.append(dot(plan.z_matrix(z_table, level + 1), ready[level - 1][...], ((1,), (1,))))
     one, two = results
     e1_ref[...] = one[: plan.tall[1]]
     e2_ref[...] = two[: plan.tall[2]]
+    inner, partner, side = (p[...] for p in pushes)
+    odd = lax.axis_index("gx") % 2 == 1
+    pushed = jnp.concatenate([inner, jnp.where(odd, partner, side), jnp.where(odd, side, partner)], axis=1)
     for n, ref in enumerate((partner_ref, side_ref)):
-        ref[:8, :] = push_ref[8 * n : 8 * n + 8, :]
+        ref[:8, :] = pushed[8 * n : 8 * n + 8, :]
         ref[8:, :] = jnp.zeros((16, ref.shape[1]), F32)
         start = plan.tall[1] + 16 * n
         ref[8:, : plan.flat[1]] = one[start : start + 16]
@@ -909,7 +938,8 @@
         if row < inner:
             value = value + inner_ref[row : row + 8]
         else:
-            value = value + edge_ref[row - inner : row - inner + 8]
+            end, row = divmod(row - inner, edge_ref.shape[1])
+            value = value + edge_ref[end, row : row + 8]
         out_ref[8 * (tiles * x + t) : 8 * (tiles * x + t) + 8] = value
 
 
@@ -982,7 +1012,6 @@
 
     z_table = plan.z_tables()
     inner_cells = (x.length - 2 * REACH) * y.length
-    edge_cells = 2 * REACH * y.length
     inner, edge = call(
         fine_inner_kernel,
         plan,
@@ -1024,23 +1053,32 @@
         swap(v, ("gx", "gy"), lambda i, j, k=k: ((i + 2 * k) % x.count ^ 1, j))
         for k, v in zip(range(1, chips), to_chips)
     ]
-    planes_inner = x.width[1] + plan.planes
-    (mixed_inner,) = call(
-        coarse_inner_kernel, plan, [ext, pair, y_table], [array(planes_inner, plan.rows_mixed, LANES)]
+    parts = call(
+        coarse_inner_kernel,
+        plan,
+        [ext, pair, y_table],
+        [array(3 * x.width[1], plan.rows1, LANES), array(3 * x.width[2], plan.rows2, LANES)],
+        [vmem(x.width[1] + plan.planes, plan.rows_mixed, LANES)],
     )
 
-    main_edge, push = call(
-        fine_edge_kernel,
-        plan,
-        [pair, from_side, edge, push_inner, y_table, z_table],
-        [array(edge_cells, z.length), array(16, x.length * y.length)],
-        [vmem(2 * REACH, 3 * y.length, LANES), ready(edge_cells, 3)],
-    )
+    def fine_end(halo, is_partner):
+        return call(
+            functools.partial(fine_edge_kernel, partner=is_partner),
+            plan,
+            [halo, edge, y_table, z_table],
+            [array(16, REACH * y.length), jax.ShapeDtypeStruct((REACH * y.length // 16, 16, 9 * LANES), BF)],
+            [vmem(REACH, 3 * y.length, LANES)],
+        )
+
+    push_partner, ready_partner = fine_end(pair, True)
+    from_side, push_partner, *parts = lax.optimization_barrier((from_side, push_partner, *parts))
+    push_side, ready_side = fine_end(from_side, False)
+    pushes = [push_inner, push_partner, push_side]
     window = lambda level: array(plan.tall[level], plan.flat[level])
     to_partner, to_side, e1, e2 = call(
         coarse_kernel,
         plan,
-        [mixed_inner, *from_chips, from_side, push, y_table, z_table],
+        [*parts, *from_chips, from_side, *pushes, y_table, z_table],
         [array(24, 1024), array(24, 1024), window(1), window(2)],
         [vmem(plan.planes * len(plan.near_chips), plan.rows_mixed, LANES), ready(plan.flat[1], 3), ready(plan.flat[2], 3)],
     )
@@ -1050,6 +1088,9 @@
     tops = [top] + [shift(top, "gy", offset) for offset in range(1, y.count)]
     (e3,) = call(top_kernel, plan, tops, [window(3)])
 
+    (main_edge,) = call(
+        fine_main_kernel, plan, [ready_partner, ready_side, z_table], [array(2, REACH * y.length, z.length)]
+    )
     (potential,) = call(
         finish_kernel,
         plan,

time: 32.4 us -> 31.6 us (0.975)
  waiting for transfers between devices: 8 us -> 5.78 us
  Pallas kernels: 9.87 us -> 10.7 us
  starting transfers between devices: 11.9 us -> 12.4 us
    ppermute x8, waiting for transfers between devices: 5.61 us -> 3.86 us  [swap(): return lax.ppermute(value, axes, pairs)]
    pallas_call x12 -> x14, Pallas kernels: 9.87 us -> 10.7 us  [call(): pl.pallas_call(functools.partial(kernel, plan), in_specs=[whole] * len(op...]
    ppermute x8, starting transfers between devices: 7.53 us -> 8.01 us  [swap(): return lax.ppermute(value, axes, pairs)]
    ppermute x2, waiting for transfers between devices: 2.38 us -> 1.91 us  [shift(): lax.ppermute(value, axis, [(i, (i + offset) % count) for i in range(count)])]
  transfers between devices with their start and end apart: 10 -> 10, of which waited for: 5 -> 4; matrix products, arithmetic and copies ran while one was open for 0% -> 0% of each run, Pallas kernels for 15% -> 19%
where the time goes in v5:
time: 31.6 us; the launch traced here: 31.4 us
  starting transfers between devices  12.4 us (39%)
  Pallas kernels  10.7 us (34%)
  waiting for transfers between devices  5.78 us (18%)
  local copies, waits for them, and re-layouts  2.38 us (8%)
    pallas_call x14, Pallas kernels, call(): pl.pallas_call(functools.partial(kernel, plan), in_specs=[whole] * len(op...  10.7 us
    ppermute x8, starting transfers between devices, swap(): return lax.ppermute(value, axes, pairs)  8.01 us
    ppermute x2, starting transfers between devices, shift(): lax.ppermute(value, axis, [(i, (i + offset) % count) for i in range(count)])  4.4 us
    ppermute x8, waiting for transfers between devices, swap(): return lax.ppermute(value, axes, pairs)  3.86 us
    unnamed x12, local copies, waits for them, and re-layouts  2.38 us
    ppermute x2, waiting for transfers between devices, shift(): lax.ppermute(value, axis, [(i, (i + offset) % count) for i in range(count)])  1.91 us
  transfers between devices with their start and end apart: 10, of which 4 were waited for; matrix products, arithmetic and copies ran while one was open for 0% of the time, Pallas kernels for 19%

profile of v5, /device:TPU:0, one launch (start us, length us, event | category | flops | bytes accessed | tf_op | source)
XLA Modules:
  0.0 31.4 jit_solution(8714894393383893073)
XLA Ops:
  0.0 1.3 %copy-done.2 = bf16[212,16,128]{2,1,0:T(8,128)(2,1)S(1)} copy-done((bf16[212,16,128]{2,1,0:T(8,128)(2,1)S(1)}, bf16[212,16,128]{2,1,0:T(8,128)(2,1)}, u32[]{:S(2)}) %copy-start.2) | copy-done | bytes 868376
  1.3 1.0 %copy-done.3 = f32[32,32,128]{2,1,0:T(8,128)S(1)} copy-done((f32[32,32,128]{2,1,0:T(8,128)S(1)}, f32[32,32,128]{2,1,0:T(8,128)}, u32[]{:S(2)}) %copy-start.3) | copy-done | bytes 524312
  2.4 0.8 %shard_map.64 = (f32[19,24,128]{2,1,0:T(8,128)S(1)}, f32[24,128]{1,0:T(8,128)S(1)}, f32[32,32,128]{2,1,0:T(8,128)S(1)}, bf16[272,256]{1,0:T(8,128)(2,1)S(1)}, bf...) custom-call(f32[32,32,128]{2,1,0:T(8,128)S(1)} %copy-done.3, bf16[212,16,128]{2,1,0:T(8,128)(2,1)S(1)} %copy-done.2), custom_call_target="tpu_custom_call" | custom-call | tf_op jit(solution)/shard_map/pallas_call | solution.py:948
  3.2 3.0 %collective-permute-start = (f32[70,8,128]{2,1,0:T(8,128)S(1)}, f32[70,8,128]{2,1,0:T(8,128)S(1)}, u32[]{:S(2)}, u32[]{:S(2)}) collective-permute-start(f32[70,8,128]{2,1,0:T(8,128)S(1)} %get-tuple-element.41), channel_id=1, source_target_pairs={{0,4},{4,0},{1,5},{5,1},{2,6},{6,2},{3,7},{7,3},{8,12},{12,8},{9,1... | collective-permute-start | bytes 860168 | tf_op jit(solution)/shard_map/ppermute | solution.py:960
  6.1 3.6 %collective-permute-start.3 = (f32[24,128]{1,0:T(8,128)S(1)}, f32[24,128]{1,0:T(8,128)S(1)}, u32[]{:S(2)}, u32[]{:S(2)}) collective-permute-start(f32[24,128]{1,0:T(8,128)S(1)} %get-tuple-element.46.own_ref), channel_id=1, source_target_pairs={{0,3},{1,2},{2,1},{3,0},{8,11},{9,10},{10,9},{11,8},{16,19},{17,18... | collective-permute-start | bytes 36872 | tf_op jit(solution)/shard_map/ppermute | solution.py:970
  9.7 0.8 %collective-permute-start.1 = (f32[24,128]{1,0:T(8,128)S(1)}, f32[24,128]{1,0:T(8,128)S(1)}, u32[]{:S(2)}, u32[]{:S(2)}) collective-permute-start(f32[24,128]{1,0:T(8,128)S(1)} %get-tuple-element.46.own_ref), channel_id=1, source_target_pairs={{0,1},{1,0},{2,3},{3,2},{8,9},{9,8},{10,11},{11,10},{16,17},{17,16... | collective-permute-start | bytes 36872 | tf_op jit(solution)/shard_map/ppermute | solution.py:970
  10.5 1.3 %shard_map.65 = (f32[3,512,128]{2,1,0:T(8,128)S(1)}, f32[16,96,128]{2,1,0:T(8,128)S(1)}) custom-call(f32[32,32,128]{2,1,0:T(8,128)S(1)} %get-tuple-element.37.q_ref, bf16[272,256]{1,0:T(8,128)(2,1)S(1)} %get-tuple-element.38.y_table.refs_5_), custom_call_target="tpu_custom_call" | custom-call | tf_op jit(solution)/shard_map/pallas_call | solution.py:948
  11.8 2.5 %collective-permute-done.2.refs_1_ = f32[24,128]{1,0:T(8,128)S(1)} collective-permute-done((f32[24,128]{1,0:T(8,128)S(1)}, f32[24,128]{1,0:T(8,128)S(1)}, u32[]{:S(2)}, u32[]{:S(2)}) %collective-permute-start.2) | collective-permute-done | bytes 12320 | tf_op jit(solution)/shard_map/ppermute | solution.py:970
  14.7 0.6 %collective-permute-start.5 = (f32[68,8,128]{2,1,0:T(8,128)S(1)}, f32[68,8,128]{2,1,0:T(8,128)S(1)}, u32[]{:S(2)}, u32[]{:S(2)}) collective-permute-start(f32[68,8,128]{2,1,0:T(8,128)S(1)} %get-tuple-element.51), channel_id=1, source_target_pairs={{0,4},{4,0},{8,16},{12,20},{16,8},{20,12},{24,28},{28,24},{1,5},{5... | collective-permute-start | bytes 835592 | tf_op jit(solution)/shard_map/ppermute | solution.py:970
  15.3 1.1 %collective-permute-done.4.halo_ref.pair_ref = f32[98,8,128]{2,1,0:T(8,128)S(1)} collective-permute-done((f32[98,8,128]{2,1,0:T(8,128)S(1)}, f32[98,8,128]{2,1,0:T(8,128)S(1)}, u32[]{:S(2)}, u32[]{:S(2)}) %collective-permute-start.4) | collective-permute-done | bytes 401440 | tf_op jit(solution)/shard_map/ppermute | solution.py:970
  16.6 1.3 %collective-permute-start.6 = (f32[26,8,128]{2,1,0:T(8,128)S(1)}, f32[26,8,128]{2,1,0:T(8,128)S(1)}, u32[]{:S(2)}, u32[]{:S(2)}) collective-permute-start(f32[26,8,128]{2,1,0:T(8,128)S(1)} %get-tuple-element.60), channel_id=1, source_target_pairs={{0,24},{4,28},{8,16},{12,20},{16,8},{20,12},{24,0},{28,4},{1,25},{... | collective-permute-start | bytes 319496 | tf_op jit(solution)/shard_map/ppermute | solution.py:970
  17.9 1.5 %shard_map.66 = (f32[512,128]{1,0:T(8,128)S(1)}, f32[16,512]{1,0:T(8,128)S(1)}, f32[16,96,128]{2,1,0:T(8,128)S(1)}) custom-call(f32[3,512,128]{2,1,0:T(8,128)S(1)} %get-tuple-element.39.inner_ref, f32[16,96,128]{2,1,0:T(8,128)S(1)} %get-tuple-element.42.edge_ref, bf16[272,256]{1,0:T(8,128)(2,1)S(1)} %get-tuple-element.38.y_table.refs_5_, ...), custom_call_target="tpu_custom_call" | custom-call | tf_op jit(solution)/shard_map/pallas_call | solution.py:948
  19.4 1.1 %shard_map.70 = (f32[57,24,128]{2,1,0:T(8,128)S(1)}, f32[39,16,128]{2,1,0:T(8,128)S(1)}) custom-call(f32[19,32,128]{2,1,0:T(8,128)S(1)} %get-tuple-element.53.ext_ref, f32[98,8,128]{2,1,0:T(8,128)S(1)} %collective-permute-done.4.halo_ref.pair_ref, bf16[272,256]{1,0:T(8,128)(2,1)S(1)} %get-tuple-element.38.y_table.refs_5_), custom_call_target="tpu_custom_call" | custom-call | tf_op jit(solution)/shard_map/pallas_call | solution.py:948
  20.5 0.6 %shard_map.69 = (f32[16,256]{1,0:T(8,128)S(1)}, bf16[16,16,1152]{2,1,0:T(8,128)(2,1)S(1)}) custom-call(f32[98,8,128]{2,1,0:T(8,128)S(1)} %collective-permute-done.4.halo_ref.pair_ref, f32[16,96,128]{2,1,0:T(8,128)S(1)} %get-tuple-element.49.edge_ref, bf16[272,256]{1,0:T(8,128)(2,1)S(1)} %get-tuple-element.38.y_table.refs_5_, bf16[4,336,1152]{2,1,0:T(8,128)(2,1)S(1)} %copy-done), custom_call_target="tpu_custom_call" | custom-call | tf_op jit(solution)/shard_map/pallas_call | solution.py:948
  21.1 0.2 collective-permute-done.5.halo_ref.refs_1_
  21.4 0.6 %shard_map.71 = (f32[16,256]{1,0:T(8,128)S(1)}, bf16[16,16,1152]{2,1,0:T(8,128)(2,1)S(1)}) custom-call(f32[68,8,128]{2,1,0:T(8,128)S(1)} %collective-permute-done.5.halo_ref.refs_1_, f32[16,96,128]{2,1,0:T(8,128)S(1)} %get-tuple-element.49.edge_ref, bf16[272,256]{1,0:T(8,128)(2,1)S(1)} %get-tuple-element.38.y_table.refs_5_, bf16[4,336,1152]{2,1,0:T(8,128)(2,1)S(1)} %copy-done), custom_call_target="tpu_custom_call" | custom-call | tf_op jit(solution)/shard_map/pallas_call | solution.py:948
  21.9 1.7 %shard_map.74 = (f32[24,1024]{1,0:T(8,128)S(1)}, f32[24,1024]{1,0:T(8,128)S(1)}, f32[72,456]{1,0:T(8,128)S(1)}, f32[40,208]{1,0:T(8,128)S(1)}) custom-call(f32[57,24,128]{2,1,0:T(8,128)S(1)} %get-tuple-element.58.part1, f32[39,16,128]{2,1,0:T(8,128)S(1)} %get-tuple-element.59.part2, f32[26,8,128]{2,1,0:T(8,128)S(1)} %collective-permute-done.6.refs_0_, ...), custom_call_target="tpu_custom_call" | custom-call | tf_op jit(solution)/shard_map/pallas_call | solution.py:948
  23.6 0.4 %collective-permute-start.7 = (f32[24,1024]{1,0:T(8,128)S(1)}, f32[24,1024]{1,0:T(8,128)S(1)}, u32[]{:S(2)}, u32[]{:S(2)}) collective-permute-start(f32[24,1024]{1,0:T(8,128)S(1)} %get-tuple-element.66), channel_id=1, source_target_pairs={{0,1},{1,0},{2,3},{3,2},{8,9},{9,8},{10,11},{11,10},{16,17},{17,16... | collective-permute-start | bytes 294920 | tf_op jit(solution)/shard_map/ppermute | solution.py:970
  24.0 1.2 %collective-permute-start.8 = (f32[24,1024]{1,0:T(8,128)S(1)}, f32[24,1024]{1,0:T(8,128)S(1)}, u32[]{:S(2)}, u32[]{:S(2)}) collective-permute-start(f32[24,1024]{1,0:T(8,128)S(1)} %get-tuple-element.67), channel_id=1, source_target_pairs={{0,8},{1,2},{2,1},{3,11},{8,0},{9,10},{10,9},{11,3},{16,24},{17,18... | collective-permute-start | bytes 294920 | tf_op jit(solution)/shard_map/ppermute | solution.py:970
  25.3 1.4 %collective-permute-start.9 = (f32[48,128]{1,0:T(8,128)S(1)}, f32[48,128]{1,0:T(8,128)S(1)}, u32[]{:S(2)}, u32[]{:S(2)}) collective-permute-start(f32[48,128]{1,0:T(8,128)S(1)} %shard_map.75.refs_0_), channel_id=1, source_target_pairs={{0,4},{4,0},{1,5},{5,1},{2,6},{6,2},{3,7},{7,3},{8,12},{12,8},{9,1... | collective-permute-start | bytes 73736 | tf_op jit(solution)/shard_map/ppermute | solution.py:960
  26.7 0.5 %shard_map.72.edge_ref = f32[2,256,128]{2,1,0:T(8,128)S(1)} custom-call(bf16[16,16,1152]{2,1,0:T(8,128)(2,1)S(1)} %get-tuple-element.50.partner_ref, bf16[16,16,1152]{2,1,0:T(8,128)(2,1)S(1)} %get-tuple-element.57.side_ref, bf16[4,336,1152]{2,1,0:T(8,128)(2,1)S(1)} %copy-done), custom_call_target="tpu_custom_call" | custom-call | tf_op jit(solution)/shard_map/pallas_call | solution.py:948
  27.2 1.9 %collective-permute-done.9.refs_1_ = f32[48,128]{1,0:T(8,128)S(1)} collective-permute-done((f32[48,128]{1,0:T(8,128)S(1)}, f32[48,128]{1,0:T(8,128)S(1)}, u32[]{:S(2)}, u32[]{:S(2)}) %collective-permute-start.9) | collective-permute-done | bytes 24608 | tf_op jit(solution)/shard_map/ppermute | solution.py:960
  29.1 0.2 shard_map.76.refs_2_
  29.4 2.0 %shard_map.77 = f32[1024,128]{1,0:T(8,128)} custom-call(f32[512,128]{1,0:T(8,128)S(1)} %get-tuple-element.44.inner_ref, f32[2,256,128]{2,1,0:T(8,128)S(1)} %shard_map.72.edge_ref, f32[72,456]{1,0:T(8,128)S(1)} %get-tuple-element.64.e1_ref, f32[40,208]{1,0:T(8,128)S(1)} %get-tuple-element.65.e2_ref, f32[24,1024]{1,0:T(8,128)S(1)} %collective-permute-done.7.refs_0_, ...), custom_call_target="tpu_custom_call" | custom-call | tf_op jit(solution)/shard_map/pallas_call | solution.py:948
  (22 shorter events, 0.6 us)
Async XLA Ops:
  0.0 17.9 %copy-start = (bf16[4,336,1152]{2,1,0:T(8,128)(2,1)S(1)}, bf16[4,336,1152]{2,1,0:T(8,128)(2,1)}, u32[]{:S(2)}) copy-start(bf16[4,336,1152]{2,1,0:T(8,128)(2,1)} %constant.11.clone.z_table.refs_6_) | copy-start | bytes 9289732
  0.0 1.3 %copy-start.2 = (bf16[212,16,128]{2,1,0:T(8,128)(2,1)S(1)}, bf16[212,16,128]{2,1,0:T(8,128)(2,1)}, u32[]{:S(2)}) copy-start(bf16[212,16,128]{2,1,0:T(8,128)(2,1)} %constant.10.clone.table_ref) | copy-start | bytes 2605060
  1.3 1.0 %copy-start.3 = (f32[32,32,128]{2,1,0:T(8,128)S(1)}, f32[32,32,128]{2,1,0:T(8,128)}, u32[]{:S(2)}) copy-start(f32[32,32,128]{2,1,0:T(8,128)} %q_ref.1) | copy-start | bytes 1572868
  3.2 11.3 %collective-permute-start = (f32[70,8,128]{2,1,0:T(8,128)S(1)}, f32[70,8,128]{2,1,0:T(8,128)S(1)}, u32[]{:S(2)}, u32[]{:S(2)}) collective-permute-start(f32[70,8,128]{2,1,0:T(8,128)S(1)} %get-tuple-element.41), channel_id=1, source_target_pairs={{0,4},{4,0},{1,5},{5,1},{2,6},{6,2},{3,7},{7,3},{8,12},{12,8},{9,1... | collective-permute-start | bytes 860168 | tf_op jit(solution)/shard_map/ppermute | solution.py:960
  6.1 5.7 %collective-permute-start.3 = (f32[24,128]{1,0:T(8,128)S(1)}, f32[24,128]{1,0:T(8,128)S(1)}, u32[]{:S(2)}, u32[]{:S(2)}) collective-permute-start(f32[24,128]{1,0:T(8,128)S(1)} %get-tuple-element.46.own_ref), channel_id=1, source_target_pairs={{0,3},{1,2},{2,1},{3,0},{8,11},{9,10},{10,9},{11,8},{16,19},{17,18... | collective-permute-start | bytes 36872 | tf_op jit(solution)/shard_map/ppermute | solution.py:970
  9.7 4.6 %collective-permute-start.2 = (f32[24,128]{1,0:T(8,128)S(1)}, f32[24,128]{1,0:T(8,128)S(1)}, u32[]{:S(2)}, u32[]{:S(2)}) collective-permute-start(f32[24,128]{1,0:T(8,128)S(1)} %get-tuple-element.46.own_ref), channel_id=1, source_target_pairs={{0,2},{1,3},{2,0},{3,1},{8,10},{9,11},{10,8},{11,9},{16,18},{17,19... | collective-permute-start | bytes 36872 | tf_op jit(solution)/shard_map/ppermute | solution.py:970
  9.7 4.6 %collective-permute-start.1 = (f32[24,128]{1,0:T(8,128)S(1)}, f32[24,128]{1,0:T(8,128)S(1)}, u32[]{:S(2)}, u32[]{:S(2)}) collective-permute-start(f32[24,128]{1,0:T(8,128)S(1)} %get-tuple-element.46.own_ref), channel_id=1, source_target_pairs={{0,1},{1,0},{2,3},{3,2},{8,9},{9,8},{10,11},{11,10},{16,17},{17,16... | collective-permute-start | bytes 36872 | tf_op jit(solution)/shard_map/ppermute | solution.py:970
  14.7 1.8 %collective-permute-start.4 = (f32[98,8,128]{2,1,0:T(8,128)S(1)}, f32[98,8,128]{2,1,0:T(8,128)S(1)}, u32[]{:S(2)}, u32[]{:S(2)}) collective-permute-start(f32[98,8,128]{2,1,0:T(8,128)S(1)} %get-tuple-element.48), channel_id=1, source_target_pairs={{0,8},{4,12},{8,0},{12,4},{16,24},{20,28},{24,16},{28,20},{1,9},{5... | collective-permute-start | bytes 1204232 | tf_op jit(solution)/shard_map/ppermute | solution.py:970
  14.7 6.6 %collective-permute-start.5 = (f32[68,8,128]{2,1,0:T(8,128)S(1)}, f32[68,8,128]{2,1,0:T(8,128)S(1)}, u32[]{:S(2)}, u32[]{:S(2)}) collective-permute-start(f32[68,8,128]{2,1,0:T(8,128)S(1)} %get-tuple-element.51), channel_id=1, source_target_pairs={{0,4},{4,0},{8,16},{12,20},{16,8},{20,12},{24,28},{28,24},{1,5},{5... | collective-permute-start | bytes 835592 | tf_op jit(solution)/shard_map/ppermute | solution.py:970
  16.6 5.3 %collective-permute-start.6 = (f32[26,8,128]{2,1,0:T(8,128)S(1)}, f32[26,8,128]{2,1,0:T(8,128)S(1)}, u32[]{:S(2)}, u32[]{:S(2)}) collective-permute-start(f32[26,8,128]{2,1,0:T(8,128)S(1)} %get-tuple-element.60), channel_id=1, source_target_pairs={{0,24},{4,28},{8,16},{12,20},{16,8},{20,12},{24,0},{28,4},{1,25},{... | collective-permute-start | bytes 319496 | tf_op jit(solution)/shard_map/ppermute | solution.py:970
  23.6 5.8 %copy-start.1 = (bf16[816,1024]{1,0:T(8,128)(2,1)S(1)}, bf16[816,1024]{1,0:T(8,128)(2,1)}, u32[]{:S(2)}) copy-start(bf16[816,1024]{1,0:T(8,128)(2,1)} %constant.12.clone.refs_3_) | copy-start | bytes 5013508
  23.6 5.8 %copy-start.4 = (bf16[4,224,128]{2,1,0:T(8,128)(2,1)S(1)}, bf16[4,224,128]{2,1,0:T(8,128)(2,1)}, u32[]{:S(2)}) copy-start(bf16[4,224,128]{2,1,0:T(8,128)(2,1)} %constant.14.clone.refs_5_) | copy-start | bytes 688132
  23.6 5.8 %copy-start.5 = (f32[8,8,512]{2,1,0:T(8,128)S(1)}, f32[8,8,512]{2,1,0:T(8,128)}, u32[]{:S(2)}) copy-start(f32[8,8,512]{2,1,0:T(8,128)} %constant.13.clone.refs_4_) | copy-start | bytes 393220
  23.6 5.7 %collective-permute-start.7 = (f32[24,1024]{1,0:T(8,128)S(1)}, f32[24,1024]{1,0:T(8,128)S(1)}, u32[]{:S(2)}, u32[]{:S(2)}) collective-permute-start(f32[24,1024]{1,0:T(8,128)S(1)} %get-tuple-element.66), channel_id=1, source_target_pairs={{0,1},{1,0},{2,3},{3,2},{8,9},{9,8},{10,11},{11,10},{16,17},{17,16... | collective-permute-start | bytes 294920 | tf_op jit(solution)/shard_map/ppermute | solution.py:970
  24.0 5.3 %collective-permute-start.8 = (f32[24,1024]{1,0:T(8,128)S(1)}, f32[24,1024]{1,0:T(8,128)S(1)}, u32[]{:S(2)}, u32[]{:S(2)}) collective-permute-start(f32[24,1024]{1,0:T(8,128)S(1)} %get-tuple-element.67), channel_id=1, source_target_pairs={{0,8},{1,2},{2,1},{3,11},{8,0},{9,10},{10,9},{11,3},{16,24},{17,18... | collective-permute-start | bytes 294920 | tf_op jit(solution)/shard_map/ppermute | solution.py:970
  25.3 3.8 %collective-permute-start.9 = (f32[48,128]{1,0:T(8,128)S(1)}, f32[48,128]{1,0:T(8,128)S(1)}, u32[]{:S(2)}, u32[]{:S(2)}) collective-permute-start(f32[48,128]{1,0:T(8,128)S(1)} %shard_map.75.refs_0_), channel_id=1, source_target_pairs={{0,4},{4,0},{1,5},{5,1},{2,6},{6,2},{3,7},{7,3},{8,12},{12,8},{9,1... | collective-permute-start | bytes 73736 | tf_op jit(solution)/shard_map/ppermute | solution.py:960

commit v6 on v5

--- a/solution.py
+++ b/solution.py
@@ -181,6 +181,7 @@
             columns = [p[:, :, c : c + LANES] for c in range(0, p.shape[2], LANES)]
             blocks.append(np.concatenate(columns, axis=1).reshape(len(p), -1, 16, LANES))
         self.blocks = [b.shape[1] for b in blocks]
+        self.blocks.append(2 * up(self.tall[3], 16) // 16)
         table = np.concatenate([b.reshape(-1, 16, LANES) for b in blocks] + [self.top_select().reshape(-1, 2, LANES)
             .transpose(1, 0, 2).reshape(-1, 16, LANES).astype(np.float32)])
         return table.astype(jnp.bfloat16)
@@ -348,37 +349,29 @@
         x, y, z = self.x, self.y, self.z
         rows = (y.length, self.rows1, self.rows2, self.rows3)
         exact = lambda m: np.asarray(m, dtype=jnp.bfloat16)
-
-        def free(axis, level):
-            inner = Axis(5, axis.length)
-            return inner.prolong(level, 2)
-
-        flat = []
-        for level in (3, 2, 1):
-            q = place((rows[level], rows[level - 1]), (0, 0, free(y, level).T))
-            matrix = np.kron(free(x, level).T, q)
-            if level == 1:
-                cells = [x_ * y.length + 8 * t + k for x_, t in self.tiles() for k in range(8)]
-                matrix = matrix[:, cells]
-            flat.append(exact(matrix))
-        joined = np.concatenate([np.pad(m, ((0, -len(m) % 16), (0, 1024 - m.shape[1]))) for m in flat])
-        self.flat_rows = np.cumsum([0] + [up(len(m), 16) for m in flat])
-        masks = np.zeros((x.count * y.count, 8, 512), np.float32)
-        for level in (3, 2, 1):
-            for bx in range(x.count):
-                for by in range(y.count):
-                    inside = np.zeros(rows[level])
-                    inside[: y.width[level]] = y.window(level, by)[1]
-                    line = np.kron(x.window(level, bx)[1], inside)
-                    masks[bx * y.count + by, level, : len(line)] = line
         tall = []
         for b in range(z.count):
             ends = (0, z.length - 8) if b % 2 else (z.length - 8, 0)
-            pieces = [(0, 0, free(z, 1).T)] + [(self.tall[1] + 8 * k, end, np.eye(8)) for k, end in enumerate(ends)]
-            last = place((up(self.tall[1] + 16, 16), LANES), *pieces)
-            parts = [place((up(self.tall[l - 1], 16), LANES), (0, 0, z.prolong(l, b))) for l in (3, 2)]
-            tall.append(np.concatenate([last, *parts]))
-        return joined, masks, exact(np.stack(tall))
+            one = z.prolong(1, b)
+            two = one @ z.prolong(2, b)
+            three = two @ z.prolong(3, b)
+            deep = [place((up(self.tall[l], 16), LANES), (0, 0, m.T)) for l, m in ((1, one), (2, two), (3, three))]
+            ends = place((16, LANES), *[(8 * k, 0, np.eye(8, LANES, end)) for k, end in enumerate(ends)])
+            parts = [exact(deep[0]), exact(deep[0]), exact(ends), exact(ends), right3(deep[1]), right3(deep[2])]
+            tall.append(np.concatenate(parts))
+        self.tall_rows = np.cumsum([0] + [2 * up(self.tall[1], 16), 32, 3 * up(self.tall[2], 16), 3 * up(self.tall[3], 16)])
+
+        flat = []
+        for level in (3, 2, 1):
+            p, q = (Axis(5, axis.length).prolong(level, 2) for axis in (x, y))
+            matrix = np.kron(p, place((rows[level - 1], rows[level]), (0, 0, q)))
+            if level == 1:
+                matrix = matrix[[x_ * y.length + 8 * t + k for x_, t in self.tiles() for k in range(8)]]
+            flat.append(matrix)
+        self.flat_rows = np.cumsum([0] + [up(len(m), 16) for m in flat])
+        cols = up(max(self.flat), LANES)
+        joined = np.concatenate([np.pad(m, ((0, -len(m) % 16), (0, cols - m.shape[1]))) for m in flat])
+        return exact(joined), np.stack(tall)
 
 
 def plane(ref, base, rows, index):
@@ -399,24 +392,31 @@
     return jnp.concatenate(parts, axis=1)
 
 
-def restrict_kernel(plan, q_ref, table_ref, own_ref, top_ref, q_out, y_table_ref, z_table_ref, *rest):
-    targets, (mixed, top) = rest[: plan.kinds], rest[plan.kinds :]
+def restrict_kernel(plan, q_hbm, table_hbm, own_ref, top_ref, y_table_ref, z_table_ref, *rest):
+    targets, (mixed, top, q_ref, table_ref, sems) = rest[: plan.kinds], rest[plan.kinds :]
     nx, ny, nz = plan.x.length, plan.y.length, plan.z.length
     by, bz = lax.axis_index("gy"), lax.axis_index("gz")
-    blocks_z, blocks_y, blocks_table, blocks_top = plan.blocks
-    at_y = plan.z.count * blocks_z
-    at_table = at_y + plan.y.count * blocks_y
-    at_top = at_table + plan.y.count * blocks_table
-    at_select = at_top + plan.z.count * blocks_top
-    matrix_z = table_ref[pl.ds(blocks_z * bz, blocks_z)].reshape(3 * nz, LANES)
-    matrix_y = table_ref[pl.ds(at_y + blocks_y * by, blocks_y)].reshape(16 * blocks_y, LANES)
+    copies, starts, source, at = [pltpu.make_async_copy(q_hbm, q_ref, sems.at[0])], [], 0, 0
+    bricks = ((plan.z.count, bz), (plan.y.count, by), (plan.y.count, by), (plan.z.count, bz), (1, 0))
+    for n, (blocks, (count, brick)) in enumerate(zip(plan.blocks, bricks)):
+        part = table_hbm.at[pl.ds(source + blocks * brick, blocks)]
+        copies.append(pltpu.make_async_copy(part, table_ref.at[pl.ds(at, blocks)], sems.at[n + 1]))
+        starts.append(at)
+        source, at = source + count * blocks, at + blocks
+    for copy in copies:
+        copy.start()
+    for copy in copies:
+        copy.wait()
+    blocks_z, blocks_y = plan.blocks[:2]
+    matrix_z = table_ref[:blocks_z].reshape(3 * nz, LANES)
+    matrix_y = table_ref[blocks_z : blocks_z + blocks_y].reshape(16 * blocks_y, LANES)
     matrix_y = matrix_y[:, : 3 * ny]
-    q_out[...] = q_ref[...]
-    for ref, at in ((y_table_ref, at_table + blocks_table * by), (z_table_ref, at_top + blocks_top * bz)):
+    at_select = starts[4]
+    for ref, at in ((y_table_ref, starts[2]), (z_table_ref, starts[3])):
         rows = ref.shape[0]
         for c in range(ref.shape[1] // LANES):
-            part = table_ref[pl.ds(at + rows // 16 * c, rows // 16)]
-            ref[:, c * LANES : (c + 1) * LANES] = part.reshape(rows, LANES)
+            first = at + rows // 16 * c
+            ref[:, c * LANES : (c + 1) * LANES] = table_ref[first : first + rows // 16].reshape(rows, LANES)
     for i in range(nx):
         faces = [q_ref[i, ny - REACH :, :], q_ref[i, :REACH, :]]
         if plan.kinds == 1:
@@ -639,8 +639,9 @@
     return [jnp.zeros((pad, LANES), F32)] if pad else []
 
 
-def fine_inner_kernel(plan, q_ref, y_table, inner_ref, edge_ref, mixed):
+def fine_inner_kernel(plan, q_ref, y_table, inner_ref, edge_ref, q_out, mixed):
     x, y = plan.x, plan.y
+    q_out[...] = q_ref[...]
     halo = jnp.zeros((up(plan.fine_rows, 16) - y.length, LANES), F32)
 
     def put(i, value):
@@ -881,58 +882,56 @@
     out_ref[...] = result
 
 
-def finish_kernel(plan, inner_ref, edge_ref, e1_ref, e2_ref, *refs):
-    z = plan.z
-    refs = list(refs)
-    partner_ref, side_ref, e3_ref, flat, masks, tall, out_ref, e1, e2 = refs
-    bz = lax.axis_index("gz")
-    column = lax.axis_index("gx") * plan.y.count + lax.axis_index("gy")
-    odd = bz % 2
-    spread_cols = plan.x.length * plan.y.length
-    keep = lambda level: masks[column, level : level + 1, : plan.flat[level]]
-    bounds = [int(r) for r in plan.flat_rows]
-    flat3, flat2, flat1 = (
-        flat[bounds[k] : bounds[k + 1], :][: plan.flat[3 - k], :cols]
-        for k, cols in enumerate((plan.flat[2], plan.flat[1], spread_cols))
-    )
-    e1[...], e2[...] = e1_ref[...], e2_ref[...]
+def finish_kernel(plan, inner_ref, edge_ref, e1_ref, e2_ref, partner_ref, side_ref, e3_ref, flat, tall, out_ref, e1, e2):
+    x, y, z = plan.x, plan.y, plan.z
+    gx, gy, gz = (lax.axis_index(name) for name in ("gx", "gy", "gz"))
+    odd = gz % 2
+    for window, own, tall_ in ((e1, e1_ref, plan.tall[1]), (e2, e2_ref, plan.tall[2])):
+        window[:tall_, :] = own[...]
+        if window.shape[0] > tall_:
+            window[tall_:, :] = jnp.zeros((window.shape[0] - tall_, window.shape[1]), F32)
     kept = lax.broadcasted_iota(jnp.int32, (16, 1), 0) < FACE
     for ref, high in ((partner_ref, odd == 0), (side_ref, odd == 1)):
         one = jnp.where(kept, ref[8:, : plan.flat[1]], 0.0)
         two = ref[8:, 512 : 512 + plan.flat[2]]
         for window, value, tall_ in ((e1, one, plan.tall[1]), (e2, two, plan.tall[2])):
             window[:16, :] += value * mask(~high)
-            window[tall_ - 16 :, :] += value * mask(high)
-
-    def across(value, matrix):
+            window[tall_ - 16 : tall_, :] += value * mask(high)
+
+    bounds = [int(r) for r in plan.tall_rows]
+
+    def along_z(value, number, parts):
         high, low = split(value)
-        both = dot(jnp.concatenate([high, low], axis=0), matrix)
-        return both[: value.shape[0]] + both[value.shape[0] :]
-
-    def along(matrix, value):
+        stacked = jnp.concatenate([high, low, high][:parts], axis=0)
+        return dot(stacked, tall[gz, bounds[number] : bounds[number + 1], :], ((0,), (0,)))
+
+    def inside(level):
+        rows = (0, plan.rows1, plan.rows2, plan.rows3)[level]
+        index = lax.broadcasted_iota(jnp.int32, (plan.flat[level], LANES), 0)
+        cell_x = index // rows + ((x.length >> level) * gx + LOW[level])
+        cell_y = index % rows + ((y.length >> level) * gy + LOW[level])
+        in_x = (cell_x >= 0) & (cell_x < (x.count * x.length) >> level)
+        return in_x & (cell_y >= 0) & (cell_y < (y.count * y.length) >> level)
+
+    flat_bounds = [int(r) for r in plan.flat_rows]
+
+    def finer(value, number):
         high, low = split(value)
-        return dot(matrix, high) + dot(matrix, low)
-
-    start = up(plan.tall[1] + 16, 16)
-    middle = start + up(plan.tall[2], 16)
-    tall3 = tall[bz, start:middle, :][: plan.tall[2], : plan.tall[3]]
-    tall2 = tall[bz, middle:, :][: plan.tall[1], : plan.tall[2]]
-    last = tall[bz, :start, :]
-    three = e3_ref[...] * keep(3)
-    two = (e2[...] + along(tall3, across(three, flat3))) * keep(2)
-    one = (e1[...] + along(tall2, across(two, flat2))) * keep(1)
-    spread = across(one, flat1)
-    rows = jnp.concatenate([spread, partner_ref[:8], side_ref[:8]], axis=0)
-    pad = last.shape[0] - rows.shape[0]
-    if pad:
-        rows = jnp.concatenate([rows, jnp.zeros((pad, rows.shape[1]), F32)], axis=0)
-    high, low = split(rows)
-    stacked = jnp.concatenate([high, low], axis=0)
-    matrix = jnp.concatenate([last, last], axis=0)
-    coarse = dot(stacked, matrix, ((0,), (0,)))
+        matrix = flat[flat_bounds[number] : flat_bounds[number + 1], :][:, : value.shape[0]]
+        both = dot(matrix, jnp.concatenate([high, low], axis=1))
+        return both[:, :LANES] + both[:, LANES:]
+
+    pad = up(plan.tall[3], 16) - plan.tall[3]
+    e3 = jnp.concatenate([e3_ref[...]] + ([jnp.zeros((pad, e3_ref.shape[1]), F32)] if pad else []), axis=0)
+    ends = along_z(jnp.concatenate([partner_ref[:8], side_ref[:8]], axis=0), 1, 2)
+    one, two, three = along_z(e1[...], 0, 2), along_z(e2[...], 2, 3), along_z(e3, 3, 3)
+    three = jnp.where(inside(3), three, 0.0)
+    two = jnp.where(inside(2), two + finer(three, 0)[: plan.flat[2]], 0.0)
+    one = jnp.where(inside(1), one + finer(two, 1)[: plan.flat[1]], 0.0)
+    coarse = finer(one, 2) + ends
     inner = inner_ref.shape[0]
-    tiles = plan.y.length // 8
-    for k, (x, t) in enumerate(plan.tiles()):
+    tiles = y.length // 8
+    for k, (x_, t) in enumerate(plan.tiles()):
         row = 8 * k
         value = coarse[row : row + 8]
         if row < inner:
@@ -940,18 +939,18 @@
         else:
             end, row = divmod(row - inner, edge_ref.shape[1])
             value = value + edge_ref[end, row : row + 8]
-        out_ref[8 * (tiles * x + t) : 8 * (tiles * x + t) + 8] = value
-
-
-def call(kernel, plan, operands, outs, scratch=()):
-    whole = pl.BlockSpec(memory_space=pltpu.VMEM)
+        out_ref[8 * (tiles * x_ + t) : 8 * (tiles * x_ + t) + 8] = value
+
+
+def call(kernel, plan, operands, outs, scratch=(), hbm=(), vmem=32):
+    whole, left = pl.BlockSpec(memory_space=pltpu.VMEM), pl.BlockSpec(memory_space=pl.ANY)
     return pl.pallas_call(
         functools.partial(kernel, plan),
-        in_specs=[whole] * len(operands),
+        in_specs=[left if i in hbm else whole for i in range(len(operands))],
         out_specs=[whole] * len(outs),
         scratch_shapes=list(scratch),
         out_shape=list(outs),
-        compiler_params=pltpu.CompilerParams(vmem_limit_bytes=32 * 2**20),
+        compiler_params=pltpu.CompilerParams(vmem_limit_bytes=int(vmem * 2**20)),
     )(*[jnp.asarray(o) for o in operands])
 
 
@@ -987,19 +986,26 @@
 
     rows_y = 8 * x.length + 16 * x.width[1]
     table = plan.restrict_tables()
-    own, top, charges, y_table, top_table, *to_y = call(
+    own, top, y_table, top_table, *to_y = call(
         restrict_kernel,
         plan,
         [charges, table],
         [
             array(x.width[1], plan.rows1, LANES),
             array(plan.tall[3], plan.flat_top),
-            array(*charges.shape),
             jax.ShapeDtypeStruct((3 * y.length + plan.rows_mixed + plan.halo_rows, plan.y_cols), BF),
             jax.ShapeDtypeStruct((2 * plan.tall[3], up(plan.top_cols, LANES)), BF),
         ]
         + [array(rows_y // 8, 8, LANES)] * plan.kinds,
-        [vmem(x.length, plan.rows_restricted, LANES), vmem(x.width[3], plan.whole3, LANES)],
+        [
+            vmem(x.length, plan.rows_restricted, LANES),
+            vmem(x.width[3], plan.whole3, LANES),
+            vmem(*charges.shape),
+            pltpu.VMEM((sum(plan.blocks), 16, LANES), BF),
+            pltpu.SemaphoreType.DMA((6,)),
+        ],
+        hbm=(0, 1),
+        vmem=53,
     )
     from_y = []
     for offset in range(1, y.count):
@@ -1012,11 +1018,11 @@
 
     z_table = plan.z_tables()
     inner_cells = (x.length - 2 * REACH) * y.length
-    inner, edge = call(
+    inner, edge, held = call(
         fine_inner_kernel,
         plan,
         [charges, y_table],
-        [array(3, inner_cells, LANES), array(2 * REACH, 3 * y.length, LANES)],
+        [array(3, inner_cells, LANES), array(2 * REACH, 3 * y.length, LANES), array(*charges.shape)],
         [vmem(x.length, 3 * y.length, LANES)],
     )
     edge, *from_y = lax.optimization_barrier((edge, *from_y))
@@ -1024,7 +1030,7 @@
     ext, to_partner, to_side = call(
         extend_kernel,
         plan,
-        [charges, own, top, *from_y],
+        [held, own, top, *from_y],
         [
             array(x.width[1], plan.coarse_rows, LANES),
             array((plan.top_row + plan.top_rows) // 8, 8, LANES),
@@ -1096,7 +1102,7 @@
         plan,
         [main_inner, main_edge, e1, e2, *from_near, e3, *plan.finish()],
         [array(x.length * y.length, z.length)],
-        [vmem(plan.tall[level], plan.flat[level]) for level in (1, 2)],
+        [vmem(up(plan.tall[level], 16), plan.flat[level]) for level in (1, 2)],
     )
     return potential.reshape(charges.shape)
 

time: 31.6 us -> 30.5 us (0.965)
  local copies, waits for them, and re-layouts: 2.38 us -> 1.06 us
  Pallas kernels: 10.7 us -> 12 us
  waiting for transfers between devices: 5.78 us -> 4.7 us
    pallas_call x14, Pallas kernels: 10.7 us -> 12 us  [call(): pl.pallas_call(functools.partial(kernel, plan), in_specs=[left if i in hb...]
    unnamed x12 -> x8, local copies, waits for them, and re-layouts: 2.38 us -> 1.06 us
    ppermute x8, waiting for transfers between devices: 3.86 us -> 2.79 us  [swap(): return lax.ppermute(value, axes, pairs)]
  transfers between devices with their start and end apart: 10 -> 10, of which waited for: 4 -> 4; matrix products, arithmetic and copies ran while one was open for 0% -> 0% of each run, Pallas kernels for 19% -> 20%
where the time goes in v6:
time: 30.5 us; the launch traced here: 30.4 us
  starting transfers between devices  12.4 us (41%)
  Pallas kernels  12 us (39%)
  waiting for transfers between devices  4.7 us (15%)
  local copies, waits for them, and re-layouts  1.06 us (3%)
    pallas_call x14, Pallas kernels, call(): pl.pallas_call(functools.partial(kernel, plan), in_specs=[left if i in hb...  12 us
    ppermute x8, starting transfers between devices, swap(): return lax.ppermute(value, axes, pairs)  8 us
    ppermute x2, starting transfers between devices, shift(): lax.ppermute(value, axis, [(i, (i + offset) % count) for i in range(count)])  4.44 us
    ppermute x8, waiting for transfers between devices, swap(): return lax.ppermute(value, axes, pairs)  2.79 us
    ppermute x2, waiting for transfers between devices, shift(): lax.ppermute(value, axis, [(i, (i + offset) % count) for i in range(count)])  1.92 us
    unnamed x8, local copies, waits for them, and re-layouts  1.06 us
  transfers between devices with their start and end apart: 10, of which 4 were waited for; matrix products, arithmetic and copies ran while one was open for 0% of the time, Pallas kernels for 20%

profile of v6, /device:TPU:0, one launch (start us, length us, event | category | flops | bytes accessed | tf_op | source)
XLA Modules:
  0.0 30.4 jit_solution(850374297628625797)
XLA Ops:
  0.0 2.2 %shard_map.55 = (f32[19,24,128]{2,1,0:T(8,128)S(1)}, f32[24,128]{1,0:T(8,128)S(1)}, bf16[272,256]{1,0:T(8,128)(2,1)S(1)}, bf16[48,384]{1,0:T(8,128)(2,1)S(1)}, f32[70,8,128]{2,1,0:T(8,128)S(1)}) custom-call(f32[32,32,128]{2,1,0:T(8,128)} %q_ref.1, bf16[212,16,128]{2,1,0:T(8,128)(2,1)} %constant.8.clone.table_hbm), custom_call_target="tpu_custom_call" | custom-call | tf_op jit(solution)/shard_map/pallas_call | solution.py:947
  2.2 3.0 %collective-permute-start = (f32[70,8,128]{2,1,0:T(8,128)S(1)}, f32[70,8,128]{2,1,0:T(8,128)S(1)}, u32[]{:S(2)}, u32[]{:S(2)}) collective-permute-start(f32[70,8,128]{2,1,0:T(8,128)S(1)} %get-tuple-element.40), channel_id=1, source_target_pairs={{0,4},{4,0},{1,5},{5,1},{2,6},{6,2},{3,7},{7,3},{8,12},{12,8},{9,1... | collective-permute-start | bytes 860168 | tf_op jit(solution)/shard_map/ppermute | solution.py:959
  5.2 3.6 %collective-permute-start.3 = (f32[24,128]{1,0:T(8,128)S(1)}, f32[24,128]{1,0:T(8,128)S(1)}, u32[]{:S(2)}, u32[]{:S(2)}) collective-permute-start(f32[24,128]{1,0:T(8,128)S(1)} %get-tuple-element.46.own_ref), channel_id=1, source_target_pairs={{0,3},{1,2},{2,1},{3,0},{8,11},{9,10},{10,9},{11,8},{16,19},{17,18... | collective-permute-start | bytes 36872 | tf_op jit(solution)/shard_map/ppermute | solution.py:969
  8.8 0.8 %collective-permute-start.1 = (f32[24,128]{1,0:T(8,128)S(1)}, f32[24,128]{1,0:T(8,128)S(1)}, u32[]{:S(2)}, u32[]{:S(2)}) collective-permute-start(f32[24,128]{1,0:T(8,128)S(1)} %get-tuple-element.46.own_ref), channel_id=1, source_target_pairs={{0,1},{1,0},{2,3},{3,2},{8,9},{9,8},{10,11},{11,10},{16,17},{17,16... | collective-permute-start | bytes 36872 | tf_op jit(solution)/shard_map/ppermute | solution.py:969
  9.6 1.0 %copy-done.1 = f32[32,32,128]{2,1,0:T(8,128)S(1)} copy-done((f32[32,32,128]{2,1,0:T(8,128)S(1)}, f32[32,32,128]{2,1,0:T(8,128)}, u32[]{:S(2)}) %copy-start.1) | copy-done | bytes 524312
  10.6 1.3 %shard_map.56 = (f32[3,512,128]{2,1,0:T(8,128)S(1)}, f32[16,96,128]{2,1,0:T(8,128)S(1)}, f32[32,32,128]{2,1,0:T(8,128)S(1)}) custom-call(f32[32,32,128]{2,1,0:T(8,128)S(1)} %copy-done.1, bf16[272,256]{1,0:T(8,128)(2,1)S(1)} %get-tuple-element.37.y_table.refs_5_), custom_call_target="tpu_custom_call" | custom-call | tf_op jit(solution)/shard_map/pallas_call | solution.py:947
  11.9 1.4 %collective-permute-done.2.refs_1_ = f32[24,128]{1,0:T(8,128)S(1)} collective-permute-done((f32[24,128]{1,0:T(8,128)S(1)}, f32[24,128]{1,0:T(8,128)S(1)}, u32[]{:S(2)}, u32[]{:S(2)}) %collective-permute-start.2) | collective-permute-done | bytes 12320 | tf_op jit(solution)/shard_map/ppermute | solution.py:969
  13.5 0.2 shard_map.59
  13.8 0.6 %collective-permute-start.5 = (f32[68,8,128]{2,1,0:T(8,128)S(1)}, f32[68,8,128]{2,1,0:T(8,128)S(1)}, u32[]{:S(2)}, u32[]{:S(2)}) collective-permute-start(f32[68,8,128]{2,1,0:T(8,128)S(1)} %get-tuple-element.51), channel_id=1, source_target_pairs={{0,4},{4,0},{8,16},{12,20},{16,8},{20,12},{24,28},{28,24},{1,5},{5... | collective-permute-start | bytes 835592 | tf_op jit(solution)/shard_map/ppermute | solution.py:969
  14.4 1.1 %collective-permute-done.4.halo_ref.pair_ref = f32[98,8,128]{2,1,0:T(8,128)S(1)} collective-permute-done((f32[98,8,128]{2,1,0:T(8,128)S(1)}, f32[98,8,128]{2,1,0:T(8,128)S(1)}, u32[]{:S(2)}, u32[]{:S(2)}) %collective-permute-start.4) | collective-permute-done | bytes 401440 | tf_op jit(solution)/shard_map/ppermute | solution.py:969
  15.7 1.3 %collective-permute-start.6 = (f32[26,8,128]{2,1,0:T(8,128)S(1)}, f32[26,8,128]{2,1,0:T(8,128)S(1)}, u32[]{:S(2)}, u32[]{:S(2)}) collective-permute-start(f32[26,8,128]{2,1,0:T(8,128)S(1)} %get-tuple-element.60), channel_id=1, source_target_pairs={{0,24},{4,28},{8,16},{12,20},{16,8},{20,12},{24,0},{28,4},{1,25},{... | collective-permute-start | bytes 319496 | tf_op jit(solution)/shard_map/ppermute | solution.py:969
  17.0 1.5 %shard_map.57 = (f32[512,128]{1,0:T(8,128)S(1)}, f32[16,512]{1,0:T(8,128)S(1)}, f32[16,96,128]{2,1,0:T(8,128)S(1)}) custom-call(f32[3,512,128]{2,1,0:T(8,128)S(1)} %get-tuple-element.38.inner_ref, f32[16,96,128]{2,1,0:T(8,128)S(1)} %get-tuple-element.41.edge_ref, bf16[272,256]{1,0:T(8,128)(2,1)S(1)} %get-tuple-element.37.y_table.refs_5_, ...), custom_call_target="tpu_custom_call" | custom-call | tf_op jit(solution)/shard_map/pallas_call | solution.py:947
  18.5 1.1 %shard_map.61 = (f32[57,24,128]{2,1,0:T(8,128)S(1)}, f32[39,16,128]{2,1,0:T(8,128)S(1)}) custom-call(f32[19,32,128]{2,1,0:T(8,128)S(1)} %get-tuple-element.53.ext_ref, f32[98,8,128]{2,1,0:T(8,128)S(1)} %collective-permute-done.4.halo_ref.pair_ref, bf16[272,256]{1,0:T(8,128)(2,1)S(1)} %get-tuple-element.37.y_table.refs_5_), custom_call_target="tpu_custom_call" | custom-call | tf_op jit(solution)/shard_map/pallas_call | solution.py:947
  19.6 0.6 %shard_map.60 = (f32[16,256]{1,0:T(8,128)S(1)}, bf16[16,16,1152]{2,1,0:T(8,128)(2,1)S(1)}) custom-call(f32[98,8,128]{2,1,0:T(8,128)S(1)} %collective-permute-done.4.halo_ref.pair_ref, f32[16,96,128]{2,1,0:T(8,128)S(1)} %get-tuple-element.49.edge_ref, bf16[272,256]{1,0:T(8,128)(2,1)S(1)} %get-tuple-element.37.y_table.refs_5_, bf16[4,336,1152]{2,1,0:T(8,128)(2,1)S(1)} %copy-done), custom_call_target="tpu_custom_call" | custom-call | tf_op jit(solution)/shard_map/pallas_call | solution.py:947
  20.2 0.2 collective-permute-done.5.halo_ref.refs_1_
  20.4 0.6 %shard_map.62 = (f32[16,256]{1,0:T(8,128)S(1)}, bf16[16,16,1152]{2,1,0:T(8,128)(2,1)S(1)}) custom-call(f32[68,8,128]{2,1,0:T(8,128)S(1)} %collective-permute-done.5.halo_ref.refs_1_, f32[16,96,128]{2,1,0:T(8,128)S(1)} %get-tuple-element.49.edge_ref, bf16[272,256]{1,0:T(8,128)(2,1)S(1)} %get-tuple-element.37.y_table.refs_5_, bf16[4,336,1152]{2,1,0:T(8,128)(2,1)S(1)} %copy-done), custom_call_target="tpu_custom_call" | custom-call | tf_op jit(solution)/shard_map/pallas_call | solution.py:947
  21.0 1.7 %shard_map.65 = (f32[24,1024]{1,0:T(8,128)S(1)}, f32[24,1024]{1,0:T(8,128)S(1)}, f32[72,456]{1,0:T(8,128)S(1)}, f32[40,208]{1,0:T(8,128)S(1)}) custom-call(f32[57,24,128]{2,1,0:T(8,128)S(1)} %get-tuple-element.58.part1, f32[39,16,128]{2,1,0:T(8,128)S(1)} %get-tuple-element.59.part2, f32[26,8,128]{2,1,0:T(8,128)S(1)} %collective-permute-done.6.refs_0_, ...), custom_call_target="tpu_custom_call" | custom-call | tf_op jit(solution)/shard_map/pallas_call | solution.py:947
  22.7 0.4 %collective-permute-start.7 = (f32[24,1024]{1,0:T(8,128)S(1)}, f32[24,1024]{1,0:T(8,128)S(1)}, u32[]{:S(2)}, u32[]{:S(2)}) collective-permute-start(f32[24,1024]{1,0:T(8,128)S(1)} %get-tuple-element.66), channel_id=1, source_target_pairs={{0,1},{1,0},{2,3},{3,2},{8,9},{9,8},{10,11},{11,10},{16,17},{17,16... | collective-permute-start | bytes 294920 | tf_op jit(solution)/shard_map/ppermute | solution.py:969
  23.1 1.3 %collective-permute-start.8 = (f32[24,1024]{1,0:T(8,128)S(1)}, f32[24,1024]{1,0:T(8,128)S(1)}, u32[]{:S(2)}, u32[]{:S(2)}) collective-permute-start(f32[24,1024]{1,0:T(8,128)S(1)} %get-tuple-element.67), channel_id=1, source_target_pairs={{0,8},{1,2},{2,1},{3,11},{8,0},{9,10},{10,9},{11,3},{16,24},{17,18... | collective-permute-start | bytes 294920 | tf_op jit(solution)/shard_map/ppermute | solution.py:969
  24.3 1.4 %collective-permute-start.9 = (f32[48,128]{1,0:T(8,128)S(1)}, f32[48,128]{1,0:T(8,128)S(1)}, u32[]{:S(2)}, u32[]{:S(2)}) collective-permute-start(f32[48,128]{1,0:T(8,128)S(1)} %shard_map.66.refs_0_), channel_id=1, source_target_pairs={{0,4},{4,0},{1,5},{5,1},{2,6},{6,2},{3,7},{7,3},{8,12},{12,8},{9,1... | collective-permute-start | bytes 73736 | tf_op jit(solution)/shard_map/ppermute | solution.py:959
  25.8 0.5 %shard_map.63.edge_ref = f32[2,256,128]{2,1,0:T(8,128)S(1)} custom-call(bf16[16,16,1152]{2,1,0:T(8,128)(2,1)S(1)} %get-tuple-element.50.partner_ref, bf16[16,16,1152]{2,1,0:T(8,128)(2,1)S(1)} %get-tuple-element.57.side_ref, bf16[4,336,1152]{2,1,0:T(8,128)(2,1)S(1)} %copy-done), custom_call_target="tpu_custom_call" | custom-call | tf_op jit(solution)/shard_map/pallas_call | solution.py:947
  26.2 1.9 %collective-permute-done.9.refs_1_ = f32[48,128]{1,0:T(8,128)S(1)} collective-permute-done((f32[48,128]{1,0:T(8,128)S(1)}, f32[48,128]{1,0:T(8,128)S(1)}, u32[]{:S(2)}, u32[]{:S(2)}) %collective-permute-start.9) | collective-permute-done | bytes 24608 | tf_op jit(solution)/shard_map/ppermute | solution.py:959
  28.1 0.2 shard_map.67.e3_ref
  28.4 2.0 %shard_map.68 = f32[1024,128]{1,0:T(8,128)} custom-call(f32[512,128]{1,0:T(8,128)S(1)} %get-tuple-element.43.inner_ref, f32[2,256,128]{2,1,0:T(8,128)S(1)} %shard_map.63.edge_ref, f32[72,456]{1,0:T(8,128)S(1)} %get-tuple-element.64.e1_ref, f32[40,208]{1,0:T(8,128)S(1)} %get-tuple-element.65.e2_ref, f32[24,1024]{1,0:T(8,128)S(1)} %collective-permute-done.7.partner_ref, ...), custom_call_target="tpu_custom_call" | custom-call | tf_op jit(solution)/shard_map/pallas_call | solution.py:947
  (18 shorter events, 0.4 us)
Async XLA Ops:
  0.0 17.0 %copy-start = (bf16[4,336,1152]{2,1,0:T(8,128)(2,1)S(1)}, bf16[4,336,1152]{2,1,0:T(8,128)(2,1)}, u32[]{:S(2)}) copy-start(bf16[4,336,1152]{2,1,0:T(8,128)(2,1)} %constant.9.clone.z_table.refs_6_) | copy-start | bytes 9289732
  2.2 11.4 %collective-permute-start = (f32[70,8,128]{2,1,0:T(8,128)S(1)}, f32[70,8,128]{2,1,0:T(8,128)S(1)}, u32[]{:S(2)}, u32[]{:S(2)}) collective-permute-start(f32[70,8,128]{2,1,0:T(8,128)S(1)} %get-tuple-element.40), channel_id=1, source_target_pairs={{0,4},{4,0},{1,5},{5,1},{2,6},{6,2},{3,7},{7,3},{8,12},{12,8},{9,1... | collective-permute-start | bytes 860168 | tf_op jit(solution)/shard_map/ppermute | solution.py:959
  5.2 6.8 %collective-permute-start.3 = (f32[24,128]{1,0:T(8,128)S(1)}, f32[24,128]{1,0:T(8,128)S(1)}, u32[]{:S(2)}, u32[]{:S(2)}) collective-permute-start(f32[24,128]{1,0:T(8,128)S(1)} %get-tuple-element.46.own_ref), channel_id=1, source_target_pairs={{0,3},{1,2},{2,1},{3,0},{8,11},{9,10},{10,9},{11,8},{16,19},{17,18... | collective-permute-start | bytes 36872 | tf_op jit(solution)/shard_map/ppermute | solution.py:969
  8.8 4.6 %collective-permute-start.2 = (f32[24,128]{1,0:T(8,128)S(1)}, f32[24,128]{1,0:T(8,128)S(1)}, u32[]{:S(2)}, u32[]{:S(2)}) collective-permute-start(f32[24,128]{1,0:T(8,128)S(1)} %get-tuple-element.46.own_ref), channel_id=1, source_target_pairs={{0,2},{1,3},{2,0},{3,1},{8,10},{9,11},{10,8},{11,9},{16,18},{17,19... | collective-permute-start | bytes 36872 | tf_op jit(solution)/shard_map/ppermute | solution.py:969
  8.8 4.6 %collective-permute-start.1 = (f32[24,128]{1,0:T(8,128)S(1)}, f32[24,128]{1,0:T(8,128)S(1)}, u32[]{:S(2)}, u32[]{:S(2)}) collective-permute-start(f32[24,128]{1,0:T(8,128)S(1)} %get-tuple-element.46.own_ref), channel_id=1, source_target_pairs={{0,1},{1,0},{2,3},{3,2},{8,9},{9,8},{10,11},{11,10},{16,17},{17,16... | collective-permute-start | bytes 36872 | tf_op jit(solution)/shard_map/ppermute | solution.py:969
  9.6 1.0 %copy-start.1 = (f32[32,32,128]{2,1,0:T(8,128)S(1)}, f32[32,32,128]{2,1,0:T(8,128)}, u32[]{:S(2)}) copy-start(f32[32,32,128]{2,1,0:T(8,128)} %q_ref.1) | copy-start | bytes 1572868
  13.7 1.8 %collective-permute-start.4 = (f32[98,8,128]{2,1,0:T(8,128)S(1)}, f32[98,8,128]{2,1,0:T(8,128)S(1)}, u32[]{:S(2)}, u32[]{:S(2)}) collective-permute-start(f32[98,8,128]{2,1,0:T(8,128)S(1)} %get-tuple-element.48), channel_id=1, source_target_pairs={{0,8},{4,12},{8,0},{12,4},{16,24},{20,28},{24,16},{28,20},{1,9},{5... | collective-permute-start | bytes 1204232 | tf_op jit(solution)/shard_map/ppermute | solution.py:969
  13.8 6.6 %collective-permute-start.5 = (f32[68,8,128]{2,1,0:T(8,128)S(1)}, f32[68,8,128]{2,1,0:T(8,128)S(1)}, u32[]{:S(2)}, u32[]{:S(2)}) collective-permute-start(f32[68,8,128]{2,1,0:T(8,128)S(1)} %get-tuple-element.51), channel_id=1, source_target_pairs={{0,4},{4,0},{8,16},{12,20},{16,8},{20,12},{24,28},{28,24},{1,5},{5... | collective-permute-start | bytes 835592 | tf_op jit(solution)/shard_map/ppermute | solution.py:969
  15.7 5.3 %collective-permute-start.6 = (f32[26,8,128]{2,1,0:T(8,128)S(1)}, f32[26,8,128]{2,1,0:T(8,128)S(1)}, u32[]{:S(2)}, u32[]{:S(2)}) collective-permute-start(f32[26,8,128]{2,1,0:T(8,128)S(1)} %get-tuple-element.60), channel_id=1, source_target_pairs={{0,24},{4,28},{8,16},{12,20},{16,8},{20,12},{24,0},{28,4},{1,25},{... | collective-permute-start | bytes 319496 | tf_op jit(solution)/shard_map/ppermute | solution.py:969
  22.7 5.7 %copy-start.2 = (bf16[1696,512]{1,0:T(8,128)(2,1)S(1)}, bf16[1696,512]{1,0:T(8,128)(2,1)}, u32[]{:S(2)}) copy-start(bf16[1696,512]{1,0:T(8,128)(2,1)} %constant.10.clone.flat) | copy-start | bytes 5210116
  22.7 5.7 %copy-start.3 = (bf16[4,432,128]{2,1,0:T(8,128)(2,1)S(1)}, bf16[4,432,128]{2,1,0:T(8,128)(2,1)}, u32[]{:S(2)}) copy-start(bf16[4,432,128]{2,1,0:T(8,128)(2,1)} %constant.11.clone.tall) | copy-start | bytes 1327108
  22.7 5.7 %collective-permute-start.7 = (f32[24,1024]{1,0:T(8,128)S(1)}, f32[24,1024]{1,0:T(8,128)S(1)}, u32[]{:S(2)}, u32[]{:S(2)}) collective-permute-start(f32[24,1024]{1,0:T(8,128)S(1)} %get-tuple-element.66), channel_id=1, source_target_pairs={{0,1},{1,0},{2,3},{3,2},{8,9},{9,8},{10,11},{11,10},{16,17},{17,16... | collective-permute-start | bytes 294920 | tf_op jit(solution)/shard_map/ppermute | solution.py:969
  23.1 5.3 %collective-permute-start.8 = (f32[24,1024]{1,0:T(8,128)S(1)}, f32[24,1024]{1,0:T(8,128)S(1)}, u32[]{:S(2)}, u32[]{:S(2)}) collective-permute-start(f32[24,1024]{1,0:T(8,128)S(1)} %get-tuple-element.67), channel_id=1, source_target_pairs={{0,8},{1,2},{2,1},{3,11},{8,0},{9,10},{10,9},{11,3},{16,24},{17,18... | collective-permute-start | bytes 294920 | tf_op jit(solution)/shard_map/ppermute | solution.py:969
  24.3 3.8 %collective-permute-start.9 = (f32[48,128]{1,0:T(8,128)S(1)}, f32[48,128]{1,0:T(8,128)S(1)}, u32[]{:S(2)}, u32[]{:S(2)}) collective-permute-start(f32[48,128]{1,0:T(8,128)S(1)} %shard_map.66.refs_0_), channel_id=1, source_target_pairs={{0,4},{4,0},{1,5},{5,1},{2,6},{6,2},{3,7},{7,3},{8,12},{12,8},{9,1... | collective-permute-start | bytes 73736 | tf_op jit(solution)/shard_map/ppermute | solution.py:959

commit v7 on v6

--- a/solution.py
+++ b/solution.py
@@ -882,7 +882,7 @@
     out_ref[...] = result
 
 
-def finish_kernel(plan, inner_ref, edge_ref, e1_ref, e2_ref, partner_ref, side_ref, e3_ref, flat, tall, out_ref, e1, e2):
+def finish_kernel(plan, inner_ref, edge_ref, e1_ref, e2_ref, partner_ref, side_ref, e3_ref, flat, tall, out_hbm, e1, e2, out_ref, sems):
     x, y, z = plan.x, plan.y, plan.z
     gx, gy, gz = (lax.axis_index(name) for name in ("gx", "gy", "gz"))
     odd = gz % 2
@@ -928,26 +928,37 @@
     three = jnp.where(inside(3), three, 0.0)
     two = jnp.where(inside(2), two + finer(three, 0)[: plan.flat[2]], 0.0)
     one = jnp.where(inside(1), one + finer(two, 1)[: plan.flat[1]], 0.0)
-    coarse = finer(one, 2) + ends
+    high, low = split(one)
+    stacked = jnp.concatenate([high, low], axis=1)
     inner = inner_ref.shape[0]
-    tiles = y.length // 8
-    for k, (x_, t) in enumerate(plan.tiles()):
-        row = 8 * k
-        value = coarse[row : row + 8]
-        if row < inner:
-            value = value + inner_ref[row : row + 8]
-        else:
-            end, row = divmod(row - inner, edge_ref.shape[1])
-            value = value + edge_ref[end, row : row + 8]
-        out_ref[8 * (tiles * x_ + t) : 8 * (tiles * x_ + t) + 8] = value
-
-
-def call(kernel, plan, operands, outs, scratch=(), hbm=(), vmem=32):
+    edge, tiles, order = edge_ref.shape[1], y.length // 8, plan.tiles()
+    copies = []
+    for first, last, to in ((inner, inner + edge, 0), (inner + edge, inner + 2 * edge, inner + edge), (0, inner, edge)):
+        matrix = flat[flat_bounds[2] + first : flat_bounds[2] + last, :][:, : plan.flat[1]]
+        both = dot(matrix, stacked)
+        coarse = both[:, :LANES] + both[:, LANES:] + ends[first:last]
+        for row in range(first, last, 8):
+            x_, t = order[row // 8]
+            value = coarse[row - first : row - first + 8]
+            if row < inner:
+                value = value + inner_ref[row : row + 8]
+            else:
+                end, at = divmod(row - inner, edge)
+                value = value + edge_ref[end, at : at + 8]
+            out_ref[8 * (tiles * x_ + t) : 8 * (tiles * x_ + t) + 8] = value
+        rows = pl.ds(to, last - first)
+        copies.append(pltpu.make_async_copy(out_ref.at[rows], out_hbm.at[rows], sems.at[len(copies)]))
+        copies[-1].start()
+    for copy in copies:
+        copy.wait()
+
+
+def call(kernel, plan, operands, outs, scratch=(), hbm=(), vmem=32, out=None):
     whole, left = pl.BlockSpec(memory_space=pltpu.VMEM), pl.BlockSpec(memory_space=pl.ANY)
     return pl.pallas_call(
         functools.partial(kernel, plan),
         in_specs=[left if i in hbm else whole for i in range(len(operands))],
-        out_specs=[whole] * len(outs),
+        out_specs=[out or whole] * len(outs),
         scratch_shapes=list(scratch),
         out_shape=list(outs),
         compiler_params=pltpu.CompilerParams(vmem_limit_bytes=int(vmem * 2**20)),
@@ -1102,7 +1113,9 @@
         plan,
         [main_inner, main_edge, e1, e2, *from_near, e3, *plan.finish()],
         [array(x.length * y.length, z.length)],
-        [vmem(up(plan.tall[level], 16), plan.flat[level]) for level in (1, 2)],
+        [vmem(up(plan.tall[level], 16), plan.flat[level]) for level in (1, 2)]
+        + [vmem(x.length * y.length, z.length), pltpu.SemaphoreType.DMA((3,))],
+        out=pl.BlockSpec(memory_space=pl.ANY),
     )
     return potential.reshape(charges.shape)
 

time: 30.5 us -> 30.7 us (level)
  no operation moved by 1% of the time
where the time goes in v7:
time: 30.7 us; the launch traced here: 30.5 us
  starting transfers between devices  12.4 us (40%)
  Pallas kernels  12.2 us (40%)
  waiting for transfers between devices  4.7 us (15%)
  local copies, waits for them, and re-layouts  1.06 us (3%)
    pallas_call x14, Pallas kernels, call(): pl.pallas_call(functools.partial(kernel, plan), in_specs=[left if i in hb...  12.2 us
    ppermute x8, starting transfers between devices, swap(): return lax.ppermute(value, axes, pairs)  8 us
    ppermute x2, starting transfers between devices, shift(): lax.ppermute(value, axis, [(i, (i + offset) % count) for i in range(count)])  4.44 us
    ppermute x8, waiting for transfers between devices, swap(): return lax.ppermute(value, axes, pairs)  2.79 us
    ppermute x2, waiting for transfers between devices, shift(): lax.ppermute(value, axis, [(i, (i + offset) % count) for i in range(count)])  1.92 us
    unnamed x8, local copies, waits for them, and re-layouts  1.06 us
  transfers between devices with their start and end apart: 10, of which 4 were waited for; matrix products, arithmetic and copies ran while one was open for 0% of the time, Pallas kernels for 20%

profile of v7, /device:TPU:0, one launch (start us, length us, event | category | flops | bytes accessed | tf_op | source)
XLA Modules:
  0.0 30.5 jit_solution(6124724249626203315)
XLA Ops:
  0.0 2.2 %shard_map.55 = (f32[19,24,128]{2,1,0:T(8,128)S(1)}, f32[24,128]{1,0:T(8,128)S(1)}, bf16[272,256]{1,0:T(8,128)(2,1)S(1)}, bf16[48,384]{1,0:T(8,128)(2,1)S(1)}, f32[70,8,128]{2,1,0:T(8,128)S(1)}) custom-call(f32[32,32,128]{2,1,0:T(8,128)} %q_ref.1, bf16[212,16,128]{2,1,0:T(8,128)(2,1)} %constant.8.clone.table_hbm), custom_call_target="tpu_custom_call" | custom-call | tf_op jit(solution)/shard_map/pallas_call | solution.py:958
  2.2 3.0 %collective-permute-start = (f32[70,8,128]{2,1,0:T(8,128)S(1)}, f32[70,8,128]{2,1,0:T(8,128)S(1)}, u32[]{:S(2)}, u32[]{:S(2)}) collective-permute-start(f32[70,8,128]{2,1,0:T(8,128)S(1)} %get-tuple-element.40), channel_id=1, source_target_pairs={{0,4},{4,0},{1,5},{5,1},{2,6},{6,2},{3,7},{7,3},{8,12},{12,8},{9,1... | collective-permute-start | bytes 860168 | tf_op jit(solution)/shard_map/ppermute | solution.py:970
  5.2 3.6 %collective-permute-start.3 = (f32[24,128]{1,0:T(8,128)S(1)}, f32[24,128]{1,0:T(8,128)S(1)}, u32[]{:S(2)}, u32[]{:S(2)}) collective-permute-start(f32[24,128]{1,0:T(8,128)S(1)} %get-tuple-element.46.own_ref), channel_id=1, source_target_pairs={{0,3},{1,2},{2,1},{3,0},{8,11},{9,10},{10,9},{11,8},{16,19},{17,18... | collective-permute-start | bytes 36872 | tf_op jit(solution)/shard_map/ppermute | solution.py:980
  8.8 0.8 %collective-permute-start.1 = (f32[24,128]{1,0:T(8,128)S(1)}, f32[24,128]{1,0:T(8,128)S(1)}, u32[]{:S(2)}, u32[]{:S(2)}) collective-permute-start(f32[24,128]{1,0:T(8,128)S(1)} %get-tuple-element.46.own_ref), channel_id=1, source_target_pairs={{0,1},{1,0},{2,3},{3,2},{8,9},{9,8},{10,11},{11,10},{16,17},{17,16... | collective-permute-start | bytes 36872 | tf_op jit(solution)/shard_map/ppermute | solution.py:980
  9.6 1.0 %copy-done.1 = f32[32,32,128]{2,1,0:T(8,128)S(1)} copy-done((f32[32,32,128]{2,1,0:T(8,128)S(1)}, f32[32,32,128]{2,1,0:T(8,128)}, u32[]{:S(2)}) %copy-start.1) | copy-done | bytes 524312
  10.6 1.3 %shard_map.56 = (f32[3,512,128]{2,1,0:T(8,128)S(1)}, f32[16,96,128]{2,1,0:T(8,128)S(1)}, f32[32,32,128]{2,1,0:T(8,128)S(1)}) custom-call(f32[32,32,128]{2,1,0:T(8,128)S(1)} %copy-done.1, bf16[272,256]{1,0:T(8,128)(2,1)S(1)} %get-tuple-element.37.y_table.refs_5_), custom_call_target="tpu_custom_call" | custom-call | tf_op jit(solution)/shard_map/pallas_call | solution.py:958
  11.9 1.4 %collective-permute-done.2.refs_1_ = f32[24,128]{1,0:T(8,128)S(1)} collective-permute-done((f32[24,128]{1,0:T(8,128)S(1)}, f32[24,128]{1,0:T(8,128)S(1)}, u32[]{:S(2)}, u32[]{:S(2)}) %collective-permute-start.2) | collective-permute-done | bytes 12320 | tf_op jit(solution)/shard_map/ppermute | solution.py:980
  13.5 0.2 shard_map.59
  13.8 0.6 %collective-permute-start.5 = (f32[68,8,128]{2,1,0:T(8,128)S(1)}, f32[68,8,128]{2,1,0:T(8,128)S(1)}, u32[]{:S(2)}, u32[]{:S(2)}) collective-permute-start(f32[68,8,128]{2,1,0:T(8,128)S(1)} %get-tuple-element.51), channel_id=1, source_target_pairs={{0,4},{4,0},{8,16},{12,20},{16,8},{20,12},{24,28},{28,24},{1,5},{5... | collective-permute-start | bytes 835592 | tf_op jit(solution)/shard_map/ppermute | solution.py:980
  14.4 1.1 %collective-permute-done.4.halo_ref.pair_ref = f32[98,8,128]{2,1,0:T(8,128)S(1)} collective-permute-done((f32[98,8,128]{2,1,0:T(8,128)S(1)}, f32[98,8,128]{2,1,0:T(8,128)S(1)}, u32[]{:S(2)}, u32[]{:S(2)}) %collective-permute-start.4) | collective-permute-done | bytes 401440 | tf_op jit(solution)/shard_map/ppermute | solution.py:980
  15.7 1.3 %collective-permute-start.6 = (f32[26,8,128]{2,1,0:T(8,128)S(1)}, f32[26,8,128]{2,1,0:T(8,128)S(1)}, u32[]{:S(2)}, u32[]{:S(2)}) collective-permute-start(f32[26,8,128]{2,1,0:T(8,128)S(1)} %get-tuple-element.60), channel_id=1, source_target_pairs={{0,24},{4,28},{8,16},{12,20},{16,8},{20,12},{24,0},{28,4},{1,25},{... | collective-permute-start | bytes 319496 | tf_op jit(solution)/shard_map/ppermute | solution.py:980
  17.0 1.5 %shard_map.57 = (f32[512,128]{1,0:T(8,128)S(1)}, f32[16,512]{1,0:T(8,128)S(1)}, f32[16,96,128]{2,1,0:T(8,128)S(1)}) custom-call(f32[3,512,128]{2,1,0:T(8,128)S(1)} %get-tuple-element.38.inner_ref, f32[16,96,128]{2,1,0:T(8,128)S(1)} %get-tuple-element.41.edge_ref, bf16[272,256]{1,0:T(8,128)(2,1)S(1)} %get-tuple-element.37.y_table.refs_5_, ...), custom_call_target="tpu_custom_call" | custom-call | tf_op jit(solution)/shard_map/pallas_call | solution.py:958
  18.5 1.1 %shard_map.61 = (f32[57,24,128]{2,1,0:T(8,128)S(1)}, f32[39,16,128]{2,1,0:T(8,128)S(1)}) custom-call(f32[19,32,128]{2,1,0:T(8,128)S(1)} %get-tuple-element.53.ext_ref, f32[98,8,128]{2,1,0:T(8,128)S(1)} %collective-permute-done.4.halo_ref.pair_ref, bf16[272,256]{1,0:T(8,128)(2,1)S(1)} %get-tuple-element.37.y_table.refs_5_), custom_call_target="tpu_custom_call" | custom-call | tf_op jit(solution)/shard_map/pallas_call | solution.py:958
  19.6 0.6 %shard_map.60 = (f32[16,256]{1,0:T(8,128)S(1)}, bf16[16,16,1152]{2,1,0:T(8,128)(2,1)S(1)}) custom-call(f32[98,8,128]{2,1,0:T(8,128)S(1)} %collective-permute-done.4.halo_ref.pair_ref, f32[16,96,128]{2,1,0:T(8,128)S(1)} %get-tuple-element.49.edge_ref, bf16[272,256]{1,0:T(8,128)(2,1)S(1)} %get-tuple-element.37.y_table.refs_5_, bf16[4,336,1152]{2,1,0:T(8,128)(2,1)S(1)} %copy-done), custom_call_target="tpu_custom_call" | custom-call | tf_op jit(solution)/shard_map/pallas_call | solution.py:958
  20.2 0.2 collective-permute-done.5.halo_ref.refs_1_
  20.4 0.6 %shard_map.62 = (f32[16,256]{1,0:T(8,128)S(1)}, bf16[16,16,1152]{2,1,0:T(8,128)(2,1)S(1)}) custom-call(f32[68,8,128]{2,1,0:T(8,128)S(1)} %collective-permute-done.5.halo_ref.refs_1_, f32[16,96,128]{2,1,0:T(8,128)S(1)} %get-tuple-element.49.edge_ref, bf16[272,256]{1,0:T(8,128)(2,1)S(1)} %get-tuple-element.37.y_table.refs_5_, bf16[4,336,1152]{2,1,0:T(8,128)(2,1)S(1)} %copy-done), custom_call_target="tpu_custom_call" | custom-call | tf_op jit(solution)/shard_map/pallas_call | solution.py:958
  21.0 1.7 %shard_map.65 = (f32[24,1024]{1,0:T(8,128)S(1)}, f32[24,1024]{1,0:T(8,128)S(1)}, f32[72,456]{1,0:T(8,128)S(1)}, f32[40,208]{1,0:T(8,128)S(1)}) custom-call(f32[57,24,128]{2,1,0:T(8,128)S(1)} %get-tuple-element.58.part1, f32[39,16,128]{2,1,0:T(8,128)S(1)} %get-tuple-element.59.part2, f32[26,8,128]{2,1,0:T(8,128)S(1)} %collective-permute-done.6.refs_0_, ...), custom_call_target="tpu_custom_call" | custom-call | tf_op jit(solution)/shard_map/pallas_call | solution.py:958
  22.7 0.4 %collective-permute-start.7 = (f32[24,1024]{1,0:T(8,128)S(1)}, f32[24,1024]{1,0:T(8,128)S(1)}, u32[]{:S(2)}, u32[]{:S(2)}) collective-permute-start(f32[24,1024]{1,0:T(8,128)S(1)} %get-tuple-element.66), channel_id=1, source_target_pairs={{0,1},{1,0},{2,3},{3,2},{8,9},{9,8},{10,11},{11,10},{16,17},{17,16... | collective-permute-start | bytes 294920 | tf_op jit(solution)/shard_map/ppermute | solution.py:980
  23.1 1.3 %collective-permute-start.8 = (f32[24,1024]{1,0:T(8,128)S(1)}, f32[24,1024]{1,0:T(8,128)S(1)}, u32[]{:S(2)}, u32[]{:S(2)}) collective-permute-start(f32[24,1024]{1,0:T(8,128)S(1)} %get-tuple-element.67), channel_id=1, source_target_pairs={{0,8},{1,2},{2,1},{3,11},{8,0},{9,10},{10,9},{11,3},{16,24},{17,18... | collective-permute-start | bytes 294920 | tf_op jit(solution)/shard_map/ppermute | solution.py:980
  24.3 1.4 %collective-permute-start.9 = (f32[48,128]{1,0:T(8,128)S(1)}, f32[48,128]{1,0:T(8,128)S(1)}, u32[]{:S(2)}, u32[]{:S(2)}) collective-permute-start(f32[48,128]{1,0:T(8,128)S(1)} %shard_map.66.refs_0_), channel_id=1, source_target_pairs={{0,4},{4,0},{1,5},{5,1},{2,6},{6,2},{3,7},{7,3},{8,12},{12,8},{9,1... | collective-permute-start | bytes 73736 | tf_op jit(solution)/shard_map/ppermute | solution.py:970
  25.8 0.5 %shard_map.63.edge_ref = f32[2,256,128]{2,1,0:T(8,128)S(1)} custom-call(bf16[16,16,1152]{2,1,0:T(8,128)(2,1)S(1)} %get-tuple-element.50.partner_ref, bf16[16,16,1152]{2,1,0:T(8,128)(2,1)S(1)} %get-tuple-element.57.side_ref, bf16[4,336,1152]{2,1,0:T(8,128)(2,1)S(1)} %copy-done), custom_call_target="tpu_custom_call" | custom-call | tf_op jit(solution)/shard_map/pallas_call | solution.py:958
  26.2 1.9 %collective-permute-done.9.refs_1_ = f32[48,128]{1,0:T(8,128)S(1)} collective-permute-done((f32[48,128]{1,0:T(8,128)S(1)}, f32[48,128]{1,0:T(8,128)S(1)}, u32[]{:S(2)}, u32[]{:S(2)}) %collective-permute-start.9) | collective-permute-done | bytes 24608 | tf_op jit(solution)/shard_map/ppermute | solution.py:970
  28.1 0.2 shard_map.67.e3_ref
  28.4 2.1 %shard_map.68 = f32[1024,128]{1,0:T(8,128)} custom-call(f32[512,128]{1,0:T(8,128)S(1)} %get-tuple-element.43.inner_ref, f32[2,256,128]{2,1,0:T(8,128)S(1)} %shard_map.63.edge_ref, f32[72,456]{1,0:T(8,128)S(1)} %get-tuple-element.64.e1_ref, f32[40,208]{1,0:T(8,128)S(1)} %get-tuple-element.65.e2_ref, f32[24,1024]{1,0:T(8,128)S(1)} %collective-permute-done.7.partner_ref, ...), custom_call_target="tpu_custom_call" | custom-call | tf_op jit(solution)/shard_map/pallas_call | solution.py:958
  (18 shorter events, 0.4 us)
Async XLA Ops:
  0.0 17.0 %copy-start = (bf16[4,336,1152]{2,1,0:T(8,128)(2,1)S(1)}, bf16[4,336,1152]{2,1,0:T(8,128)(2,1)}, u32[]{:S(2)}) copy-start(bf16[4,336,1152]{2,1,0:T(8,128)(2,1)} %constant.9.clone.z_table.refs_6_) | copy-start | bytes 9289732
  2.2 11.4 %collective-permute-start = (f32[70,8,128]{2,1,0:T(8,128)S(1)}, f32[70,8,128]{2,1,0:T(8,128)S(1)}, u32[]{:S(2)}, u32[]{:S(2)}) collective-permute-start(f32[70,8,128]{2,1,0:T(8,128)S(1)} %get-tuple-element.40), channel_id=1, source_target_pairs={{0,4},{4,0},{1,5},{5,1},{2,6},{6,2},{3,7},{7,3},{8,12},{12,8},{9,1... | collective-permute-start | bytes 860168 | tf_op jit(solution)/shard_map/ppermute | solution.py:970
  5.2 6.8 %collective-permute-start.3 = (f32[24,128]{1,0:T(8,128)S(1)}, f32[24,128]{1,0:T(8,128)S(1)}, u32[]{:S(2)}, u32[]{:S(2)}) collective-permute-start(f32[24,128]{1,0:T(8,128)S(1)} %get-tuple-element.46.own_ref), channel_id=1, source_target_pairs={{0,3},{1,2},{2,1},{3,0},{8,11},{9,10},{10,9},{11,8},{16,19},{17,18... | collective-permute-start | bytes 36872 | tf_op jit(solution)/shard_map/ppermute | solution.py:980
  8.8 4.6 %collective-permute-start.2 = (f32[24,128]{1,0:T(8,128)S(1)}, f32[24,128]{1,0:T(8,128)S(1)}, u32[]{:S(2)}, u32[]{:S(2)}) collective-permute-start(f32[24,128]{1,0:T(8,128)S(1)} %get-tuple-element.46.own_ref), channel_id=1, source_target_pairs={{0,2},{1,3},{2,0},{3,1},{8,10},{9,11},{10,8},{11,9},{16,18},{17,19... | collective-permute-start | bytes 36872 | tf_op jit(solution)/shard_map/ppermute | solution.py:980
  8.8 4.6 %collective-permute-start.1 = (f32[24,128]{1,0:T(8,128)S(1)}, f32[24,128]{1,0:T(8,128)S(1)}, u32[]{:S(2)}, u32[]{:S(2)}) collective-permute-start(f32[24,128]{1,0:T(8,128)S(1)} %get-tuple-element.46.own_ref), channel_id=1, source_target_pairs={{0,1},{1,0},{2,3},{3,2},{8,9},{9,8},{10,11},{11,10},{16,17},{17,16... | collective-permute-start | bytes 36872 | tf_op jit(solution)/shard_map/ppermute | solution.py:980
  9.6 1.0 %copy-start.1 = (f32[32,32,128]{2,1,0:T(8,128)S(1)}, f32[32,32,128]{2,1,0:T(8,128)}, u32[]{:S(2)}) copy-start(f32[32,32,128]{2,1,0:T(8,128)} %q_ref.1) | copy-start | bytes 1572868
  13.7 1.8 %collective-permute-start.4 = (f32[98,8,128]{2,1,0:T(8,128)S(1)}, f32[98,8,128]{2,1,0:T(8,128)S(1)}, u32[]{:S(2)}, u32[]{:S(2)}) collective-permute-start(f32[98,8,128]{2,1,0:T(8,128)S(1)} %get-tuple-element.48), channel_id=1, source_target_pairs={{0,8},{4,12},{8,0},{12,4},{16,24},{20,28},{24,16},{28,20},{1,9},{5... | collective-permute-start | bytes 1204232 | tf_op jit(solution)/shard_map/ppermute | solution.py:980
  13.8 6.6 %collective-permute-start.5 = (f32[68,8,128]{2,1,0:T(8,128)S(1)}, f32[68,8,128]{2,1,0:T(8,128)S(1)}, u32[]{:S(2)}, u32[]{:S(2)}) collective-permute-start(f32[68,8,128]{2,1,0:T(8,128)S(1)} %get-tuple-element.51), channel_id=1, source_target_pairs={{0,4},{4,0},{8,16},{12,20},{16,8},{20,12},{24,28},{28,24},{1,5},{5... | collective-permute-start | bytes 835592 | tf_op jit(solution)/shard_map/ppermute | solution.py:980
  15.7 5.3 %collective-permute-start.6 = (f32[26,8,128]{2,1,0:T(8,128)S(1)}, f32[26,8,128]{2,1,0:T(8,128)S(1)}, u32[]{:S(2)}, u32[]{:S(2)}) collective-permute-start(f32[26,8,128]{2,1,0:T(8,128)S(1)} %get-tuple-element.60), channel_id=1, source_target_pairs={{0,24},{4,28},{8,16},{12,20},{16,8},{20,12},{24,0},{28,4},{1,25},{... | collective-permute-start | bytes 319496 | tf_op jit(solution)/shard_map/ppermute | solution.py:980
  22.7 5.7 %copy-start.2 = (bf16[1696,512]{1,0:T(8,128)(2,1)S(1)}, bf16[1696,512]{1,0:T(8,128)(2,1)}, u32[]{:S(2)}) copy-start(bf16[1696,512]{1,0:T(8,128)(2,1)} %constant.10.clone.flat) | copy-start | bytes 5210116
  22.7 5.7 %copy-start.3 = (bf16[4,432,128]{2,1,0:T(8,128)(2,1)S(1)}, bf16[4,432,128]{2,1,0:T(8,128)(2,1)}, u32[]{:S(2)}) copy-start(bf16[4,432,128]{2,1,0:T(8,128)(2,1)} %constant.11.clone.tall) | copy-start | bytes 1327108
  22.7 5.7 %collective-permute-start.7 = (f32[24,1024]{1,0:T(8,128)S(1)}, f32[24,1024]{1,0:T(8,128)S(1)}, u32[]{:S(2)}, u32[]{:S(2)}) collective-permute-start(f32[24,1024]{1,0:T(8,128)S(1)} %get-tuple-element.66), channel_id=1, source_target_pairs={{0,1},{1,0},{2,3},{3,2},{8,9},{9,8},{10,11},{11,10},{16,17},{17,16... | collective-permute-start | bytes 294920 | tf_op jit(solution)/shard_map/ppermute | solution.py:980
  23.1 5.3 %collective-permute-start.8 = (f32[24,1024]{1,0:T(8,128)S(1)}, f32[24,1024]{1,0:T(8,128)S(1)}, u32[]{:S(2)}, u32[]{:S(2)}) collective-permute-start(f32[24,1024]{1,0:T(8,128)S(1)} %get-tuple-element.67), channel_id=1, source_target_pairs={{0,8},{1,2},{2,1},{3,11},{8,0},{9,10},{10,9},{11,3},{16,24},{17,18... | collective-permute-start | bytes 294920 | tf_op jit(solution)/shard_map/ppermute | solution.py:980
  24.3 3.8 %collective-permute-start.9 = (f32[48,128]{1,0:T(8,128)S(1)}, f32[48,128]{1,0:T(8,128)S(1)}, u32[]{:S(2)}, u32[]{:S(2)}) collective-permute-start(f32[48,128]{1,0:T(8,128)S(1)} %shard_map.66.refs_0_), channel_id=1, source_target_pairs={{0,4},{4,0},{1,5},{5,1},{2,6},{6,2},{3,7},{7,3},{8,12},{12,8},{9,1... | collective-permute-start | bytes 73736 | tf_op jit(solution)/shard_map/ppermute | solution.py:970

commit v8 on v6

--- a/solution.py
+++ b/solution.py
@@ -1013,7 +1013,8 @@
         value = value if offset in (1, y.count - 1) else value[x.length :]
         from_y.append(shift(value, "gy", offset))
 
-    tops = [swap(top, ("gx", "gz"), lambda i, j, m=m: (i, j ^ m)) for m in range(1, z.count)]
+    tops = {m: swap(top, ("gx", "gz"), lambda i, j, m=m: (i, j ^ m)) for m in sorted(range(1, z.count), key=lambda m: (m == 2, m))}
+    tops = [tops[m] for m in range(1, z.count)]
     (top,) = call(top_z_kernel, plan, [top, *tops, top_table], [array(*plan.top_shape)])
 
     z_table = plan.z_tables()

time: 30.5 us -> 30.5 us (level)
  no operation moved by 1% of the time
where the time goes in v8:
time: 30.5 us; the launch traced here: 30.4 us
  starting transfers between devices  12.4 us (41%)
  Pallas kernels  12 us (39%)
  waiting for transfers between devices  4.7 us (15%)
  local copies, waits for them, and re-layouts  1.06 us (3%)
    pallas_call x14, Pallas kernels, call(): pl.pallas_call(functools.partial(kernel, plan), in_specs=[left if i in hb...  12 us
    ppermute x8, starting transfers between devices, swap(): return lax.ppermute(value, axes, pairs)  8 us
    ppermute x2, starting transfers between devices, shift(): lax.ppermute(value, axis, [(i, (i + offset) % count) for i in range(count)])  4.44 us
    ppermute x8, waiting for transfers between devices, swap(): return lax.ppermute(value, axes, pairs)  2.79 us
    ppermute x2, waiting for transfers between devices, shift(): lax.ppermute(value, axis, [(i, (i + offset) % count) for i in range(count)])  1.92 us
    unnamed x8, local copies, waits for them, and re-layouts  1.06 us
  transfers between devices with their start and end apart: 10, of which 4 were waited for; matrix products, arithmetic and copies ran while one was open for 0% of the time, Pallas kernels for 20%

profile of v8, /device:TPU:0, one launch (start us, length us, event | category | flops | bytes accessed | tf_op | source)
XLA Modules:
  0.0 30.4 jit_solution(850374297628625797)
XLA Ops:
  0.0 2.2 %shard_map.55 = (f32[19,24,128]{2,1,0:T(8,128)S(1)}, f32[24,128]{1,0:T(8,128)S(1)}, bf16[272,256]{1,0:T(8,128)(2,1)S(1)}, bf16[48,384]{1,0:T(8,128)(2,1)S(1)}, f32[70,8,128]{2,1,0:T(8,128)S(1)}) custom-call(f32[32,32,128]{2,1,0:T(8,128)} %q_ref.1, bf16[212,16,128]{2,1,0:T(8,128)(2,1)} %constant.8.clone.table_hbm), custom_call_target="tpu_custom_call" | custom-call | tf_op jit(solution)/shard_map/pallas_call | solution.py:947
  2.2 3.0 %collective-permute-start = (f32[70,8,128]{2,1,0:T(8,128)S(1)}, f32[70,8,128]{2,1,0:T(8,128)S(1)}, u32[]{:S(2)}, u32[]{:S(2)}) collective-permute-start(f32[70,8,128]{2,1,0:T(8,128)S(1)} %get-tuple-element.40), channel_id=1, source_target_pairs={{0,4},{4,0},{1,5},{5,1},{2,6},{6,2},{3,7},{7,3},{8,12},{12,8},{9,1... | collective-permute-start | bytes 860168 | tf_op jit(solution)/shard_map/ppermute | solution.py:959
  5.2 3.6 %collective-permute-start.3 = (f32[24,128]{1,0:T(8,128)S(1)}, f32[24,128]{1,0:T(8,128)S(1)}, u32[]{:S(2)}, u32[]{:S(2)}) collective-permute-start(f32[24,128]{1,0:T(8,128)S(1)} %get-tuple-element.46.own_ref), channel_id=1, source_target_pairs={{0,3},{1,2},{2,1},{3,0},{8,11},{9,10},{10,9},{11,8},{16,19},{17,18... | collective-permute-start | bytes 36872 | tf_op jit(solution)/shard_map/ppermute | solution.py:969
  8.8 0.8 %collective-permute-start.1 = (f32[24,128]{1,0:T(8,128)S(1)}, f32[24,128]{1,0:T(8,128)S(1)}, u32[]{:S(2)}, u32[]{:S(2)}) collective-permute-start(f32[24,128]{1,0:T(8,128)S(1)} %get-tuple-element.46.own_ref), channel_id=1, source_target_pairs={{0,1},{1,0},{2,3},{3,2},{8,9},{9,8},{10,11},{11,10},{16,17},{17,16... | collective-permute-start | bytes 36872 | tf_op jit(solution)/shard_map/ppermute | solution.py:969
  9.6 1.0 %copy-done.1 = f32[32,32,128]{2,1,0:T(8,128)S(1)} copy-done((f32[32,32,128]{2,1,0:T(8,128)S(1)}, f32[32,32,128]{2,1,0:T(8,128)}, u32[]{:S(2)}) %copy-start.1) | copy-done | bytes 524312
  10.6 1.3 %shard_map.56 = (f32[3,512,128]{2,1,0:T(8,128)S(1)}, f32[16,96,128]{2,1,0:T(8,128)S(1)}, f32[32,32,128]{2,1,0:T(8,128)S(1)}) custom-call(f32[32,32,128]{2,1,0:T(8,128)S(1)} %copy-done.1, bf16[272,256]{1,0:T(8,128)(2,1)S(1)} %get-tuple-element.37.y_table.refs_5_), custom_call_target="tpu_custom_call" | custom-call | tf_op jit(solution)/shard_map/pallas_call | solution.py:947
  11.9 1.4 %collective-permute-done.2.refs_1_ = f32[24,128]{1,0:T(8,128)S(1)} collective-permute-done((f32[24,128]{1,0:T(8,128)S(1)}, f32[24,128]{1,0:T(8,128)S(1)}, u32[]{:S(2)}, u32[]{:S(2)}) %collective-permute-start.2) | collective-permute-done | bytes 12320 | tf_op jit(solution)/shard_map/ppermute | solution.py:969
  13.5 0.2 shard_map.59
  13.8 0.6 %collective-permute-start.5 = (f32[68,8,128]{2,1,0:T(8,128)S(1)}, f32[68,8,128]{2,1,0:T(8,128)S(1)}, u32[]{:S(2)}, u32[]{:S(2)}) collective-permute-start(f32[68,8,128]{2,1,0:T(8,128)S(1)} %get-tuple-element.51), channel_id=1, source_target_pairs={{0,4},{4,0},{8,16},{12,20},{16,8},{20,12},{24,28},{28,24},{1,5},{5... | collective-permute-start | bytes 835592 | tf_op jit(solution)/shard_map/ppermute | solution.py:969
  14.4 1.1 %collective-permute-done.4.halo_ref.pair_ref = f32[98,8,128]{2,1,0:T(8,128)S(1)} collective-permute-done((f32[98,8,128]{2,1,0:T(8,128)S(1)}, f32[98,8,128]{2,1,0:T(8,128)S(1)}, u32[]{:S(2)}, u32[]{:S(2)}) %collective-permute-start.4) | collective-permute-done | bytes 401440 | tf_op jit(solution)/shard_map/ppermute | solution.py:969
  15.7 1.3 %collective-permute-start.6 = (f32[26,8,128]{2,1,0:T(8,128)S(1)}, f32[26,8,128]{2,1,0:T(8,128)S(1)}, u32[]{:S(2)}, u32[]{:S(2)}) collective-permute-start(f32[26,8,128]{2,1,0:T(8,128)S(1)} %get-tuple-element.60), channel_id=1, source_target_pairs={{0,24},{4,28},{8,16},{12,20},{16,8},{20,12},{24,0},{28,4},{1,25},{... | collective-permute-start | bytes 319496 | tf_op jit(solution)/shard_map/ppermute | solution.py:969
  17.0 1.5 %shard_map.57 = (f32[512,128]{1,0:T(8,128)S(1)}, f32[16,512]{1,0:T(8,128)S(1)}, f32[16,96,128]{2,1,0:T(8,128)S(1)}) custom-call(f32[3,512,128]{2,1,0:T(8,128)S(1)} %get-tuple-element.38.inner_ref, f32[16,96,128]{2,1,0:T(8,128)S(1)} %get-tuple-element.41.edge_ref, bf16[272,256]{1,0:T(8,128)(2,1)S(1)} %get-tuple-element.37.y_table.refs_5_, ...), custom_call_target="tpu_custom_call" | custom-call | tf_op jit(solution)/shard_map/pallas_call | solution.py:947
  18.5 1.1 %shard_map.61 = (f32[57,24,128]{2,1,0:T(8,128)S(1)}, f32[39,16,128]{2,1,0:T(8,128)S(1)}) custom-call(f32[19,32,128]{2,1,0:T(8,128)S(1)} %get-tuple-element.53.ext_ref, f32[98,8,128]{2,1,0:T(8,128)S(1)} %collective-permute-done.4.halo_ref.pair_ref, bf16[272,256]{1,0:T(8,128)(2,1)S(1)} %get-tuple-element.37.y_table.refs_5_), custom_call_target="tpu_custom_call" | custom-call | tf_op jit(solution)/shard_map/pallas_call | solution.py:947
  19.6 0.6 %shard_map.60 = (f32[16,256]{1,0:T(8,128)S(1)}, bf16[16,16,1152]{2,1,0:T(8,128)(2,1)S(1)}) custom-call(f32[98,8,128]{2,1,0:T(8,128)S(1)} %collective-permute-done.4.halo_ref.pair_ref, f32[16,96,128]{2,1,0:T(8,128)S(1)} %get-tuple-element.49.edge_ref, bf16[272,256]{1,0:T(8,128)(2,1)S(1)} %get-tuple-element.37.y_table.refs_5_, bf16[4,336,1152]{2,1,0:T(8,128)(2,1)S(1)} %copy-done), custom_call_target="tpu_custom_call" | custom-call | tf_op jit(solution)/shard_map/pallas_call | solution.py:947
  20.2 0.2 collective-permute-done.5.halo_ref.refs_1_
  20.4 0.6 %shard_map.62 = (f32[16,256]{1,0:T(8,128)S(1)}, bf16[16,16,1152]{2,1,0:T(8,128)(2,1)S(1)}) custom-call(f32[68,8,128]{2,1,0:T(8,128)S(1)} %collective-permute-done.5.halo_ref.refs_1_, f32[16,96,128]{2,1,0:T(8,128)S(1)} %get-tuple-element.49.edge_ref, bf16[272,256]{1,0:T(8,128)(2,1)S(1)} %get-tuple-element.37.y_table.refs_5_, bf16[4,336,1152]{2,1,0:T(8,128)(2,1)S(1)} %copy-done), custom_call_target="tpu_custom_call" | custom-call | tf_op jit(solution)/shard_map/pallas_call | solution.py:947
  21.0 1.7 %shard_map.65 = (f32[24,1024]{1,0:T(8,128)S(1)}, f32[24,1024]{1,0:T(8,128)S(1)}, f32[72,456]{1,0:T(8,128)S(1)}, f32[40,208]{1,0:T(8,128)S(1)}) custom-call(f32[57,24,128]{2,1,0:T(8,128)S(1)} %get-tuple-element.58.part1, f32[39,16,128]{2,1,0:T(8,128)S(1)} %get-tuple-element.59.part2, f32[26,8,128]{2,1,0:T(8,128)S(1)} %collective-permute-done.6.refs_0_, ...), custom_call_target="tpu_custom_call" | custom-call | tf_op jit(solution)/shard_map/pallas_call | solution.py:947
  22.7 0.4 %collective-permute-start.7 = (f32[24,1024]{1,0:T(8,128)S(1)}, f32[24,1024]{1,0:T(8,128)S(1)}, u32[]{:S(2)}, u32[]{:S(2)}) collective-permute-start(f32[24,1024]{1,0:T(8,128)S(1)} %get-tuple-element.66), channel_id=1, source_target_pairs={{0,1},{1,0},{2,3},{3,2},{8,9},{9,8},{10,11},{11,10},{16,17},{17,16... | collective-permute-start | bytes 294920 | tf_op jit(solution)/shard_map/ppermute | solution.py:969
  23.1 1.3 %collective-permute-start.8 = (f32[24,1024]{1,0:T(8,128)S(1)}, f32[24,1024]{1,0:T(8,128)S(1)}, u32[]{:S(2)}, u32[]{:S(2)}) collective-permute-start(f32[24,1024]{1,0:T(8,128)S(1)} %get-tuple-element.67), channel_id=1, source_target_pairs={{0,8},{1,2},{2,1},{3,11},{8,0},{9,10},{10,9},{11,3},{16,24},{17,18... | collective-permute-start | bytes 294920 | tf_op jit(solution)/shard_map/ppermute | solution.py:969
  24.3 1.4 %collective-permute-start.9 = (f32[48,128]{1,0:T(8,128)S(1)}, f32[48,128]{1,0:T(8,128)S(1)}, u32[]{:S(2)}, u32[]{:S(2)}) collective-permute-start(f32[48,128]{1,0:T(8,128)S(1)} %shard_map.66.refs_0_), channel_id=1, source_target_pairs={{0,4},{4,0},{1,5},{5,1},{2,6},{6,2},{3,7},{7,3},{8,12},{12,8},{9,1... | collective-permute-start | bytes 73736 | tf_op jit(solution)/shard_map/ppermute | solution.py:959
  25.8 0.5 %shard_map.63.edge_ref = f32[2,256,128]{2,1,0:T(8,128)S(1)} custom-call(bf16[16,16,1152]{2,1,0:T(8,128)(2,1)S(1)} %get-tuple-element.50.partner_ref, bf16[16,16,1152]{2,1,0:T(8,128)(2,1)S(1)} %get-tuple-element.57.side_ref, bf16[4,336,1152]{2,1,0:T(8,128)(2,1)S(1)} %copy-done), custom_call_target="tpu_custom_call" | custom-call | tf_op jit(solution)/shard_map/pallas_call | solution.py:947
  26.2 1.9 %collective-permute-done.9.refs_1_ = f32[48,128]{1,0:T(8,128)S(1)} collective-permute-done((f32[48,128]{1,0:T(8,128)S(1)}, f32[48,128]{1,0:T(8,128)S(1)}, u32[]{:S(2)}, u32[]{:S(2)}) %collective-permute-start.9) | collective-permute-done | bytes 24608 | tf_op jit(solution)/shard_map/ppermute | solution.py:959
  28.1 0.2 shard_map.67.e3_ref
  28.4 2.0 %shard_map.68 = f32[1024,128]{1,0:T(8,128)} custom-call(f32[512,128]{1,0:T(8,128)S(1)} %get-tuple-element.43.inner_ref, f32[2,256,128]{2,1,0:T(8,128)S(1)} %shard_map.63.edge_ref, f32[72,456]{1,0:T(8,128)S(1)} %get-tuple-element.64.e1_ref, f32[40,208]{1,0:T(8,128)S(1)} %get-tuple-element.65.e2_ref, f32[24,1024]{1,0:T(8,128)S(1)} %collective-permute-done.7.partner_ref, ...), custom_call_target="tpu_custom_call" | custom-call | tf_op jit(solution)/shard_map/pallas_call | solution.py:947
  (18 shorter events, 0.4 us)
Async XLA Ops:
  0.0 17.0 %copy-start = (bf16[4,336,1152]{2,1,0:T(8,128)(2,1)S(1)}, bf16[4,336,1152]{2,1,0:T(8,128)(2,1)}, u32[]{:S(2)}) copy-start(bf16[4,336,1152]{2,1,0:T(8,128)(2,1)} %constant.9.clone.z_table.refs_6_) | copy-start | bytes 9289732
  2.2 11.4 %collective-permute-start = (f32[70,8,128]{2,1,0:T(8,128)S(1)}, f32[70,8,128]{2,1,0:T(8,128)S(1)}, u32[]{:S(2)}, u32[]{:S(2)}) collective-permute-start(f32[70,8,128]{2,1,0:T(8,128)S(1)} %get-tuple-element.40), channel_id=1, source_target_pairs={{0,4},{4,0},{1,5},{5,1},{2,6},{6,2},{3,7},{7,3},{8,12},{12,8},{9,1... | collective-permute-start | bytes 860168 | tf_op jit(solution)/shard_map/ppermute | solution.py:959
  5.2 6.8 %collective-permute-start.3 = (f32[24,128]{1,0:T(8,128)S(1)}, f32[24,128]{1,0:T(8,128)S(1)}, u32[]{:S(2)}, u32[]{:S(2)}) collective-permute-start(f32[24,128]{1,0:T(8,128)S(1)} %get-tuple-element.46.own_ref), channel_id=1, source_target_pairs={{0,3},{1,2},{2,1},{3,0},{8,11},{9,10},{10,9},{11,8},{16,19},{17,18... | collective-permute-start | bytes 36872 | tf_op jit(solution)/shard_map/ppermute | solution.py:969
  8.8 4.6 %collective-permute-start.2 = (f32[24,128]{1,0:T(8,128)S(1)}, f32[24,128]{1,0:T(8,128)S(1)}, u32[]{:S(2)}, u32[]{:S(2)}) collective-permute-start(f32[24,128]{1,0:T(8,128)S(1)} %get-tuple-element.46.own_ref), channel_id=1, source_target_pairs={{0,2},{1,3},{2,0},{3,1},{8,10},{9,11},{10,8},{11,9},{16,18},{17,19... | collective-permute-start | bytes 36872 | tf_op jit(solution)/shard_map/ppermute | solution.py:969
  8.8 4.6 %collective-permute-start.1 = (f32[24,128]{1,0:T(8,128)S(1)}, f32[24,128]{1,0:T(8,128)S(1)}, u32[]{:S(2)}, u32[]{:S(2)}) collective-permute-start(f32[24,128]{1,0:T(8,128)S(1)} %get-tuple-element.46.own_ref), channel_id=1, source_target_pairs={{0,1},{1,0},{2,3},{3,2},{8,9},{9,8},{10,11},{11,10},{16,17},{17,16... | collective-permute-start | bytes 36872 | tf_op jit(solution)/shard_map/ppermute | solution.py:969
  9.6 1.0 %copy-start.1 = (f32[32,32,128]{2,1,0:T(8,128)S(1)}, f32[32,32,128]{2,1,0:T(8,128)}, u32[]{:S(2)}) copy-start(f32[32,32,128]{2,1,0:T(8,128)} %q_ref.1) | copy-start | bytes 1572868
  13.7 1.8 %collective-permute-start.4 = (f32[98,8,128]{2,1,0:T(8,128)S(1)}, f32[98,8,128]{2,1,0:T(8,128)S(1)}, u32[]{:S(2)}, u32[]{:S(2)}) collective-permute-start(f32[98,8,128]{2,1,0:T(8,128)S(1)} %get-tuple-element.48), channel_id=1, source_target_pairs={{0,8},{4,12},{8,0},{12,4},{16,24},{20,28},{24,16},{28,20},{1,9},{5... | collective-permute-start | bytes 1204232 | tf_op jit(solution)/shard_map/ppermute | solution.py:969
  13.8 6.6 %collective-permute-start.5 = (f32[68,8,128]{2,1,0:T(8,128)S(1)}, f32[68,8,128]{2,1,0:T(8,128)S(1)}, u32[]{:S(2)}, u32[]{:S(2)}) collective-permute-start(f32[68,8,128]{2,1,0:T(8,128)S(1)} %get-tuple-element.51), channel_id=1, source_target_pairs={{0,4},{4,0},{8,16},{12,20},{16,8},{20,12},{24,28},{28,24},{1,5},{5... | collective-permute-start | bytes 835592 | tf_op jit(solution)/shard_map/ppermute | solution.py:969
  15.7 5.3 %collective-permute-start.6 = (f32[26,8,128]{2,1,0:T(8,128)S(1)}, f32[26,8,128]{2,1,0:T(8,128)S(1)}, u32[]{:S(2)}, u32[]{:S(2)}) collective-permute-start(f32[26,8,128]{2,1,0:T(8,128)S(1)} %get-tuple-element.60), channel_id=1, source_target_pairs={{0,24},{4,28},{8,16},{12,20},{16,8},{20,12},{24,0},{28,4},{1,25},{... | collective-permute-start | bytes 319496 | tf_op jit(solution)/shard_map/ppermute | solution.py:969
  22.7 5.7 %copy-start.2 = (bf16[1696,512]{1,0:T(8,128)(2,1)S(1)}, bf16[1696,512]{1,0:T(8,128)(2,1)}, u32[]{:S(2)}) copy-start(bf16[1696,512]{1,0:T(8,128)(2,1)} %constant.10.clone.flat) | copy-start | bytes 5210116
  22.7 5.7 %copy-start.3 = (bf16[4,432,128]{2,1,0:T(8,128)(2,1)S(1)}, bf16[4,432,128]{2,1,0:T(8,128)(2,1)}, u32[]{:S(2)}) copy-start(bf16[4,432,128]{2,1,0:T(8,128)(2,1)} %constant.11.clone.tall) | copy-start | bytes 1327108
  22.7 5.7 %collective-permute-start.7 = (f32[24,1024]{1,0:T(8,128)S(1)}, f32[24,1024]{1,0:T(8,128)S(1)}, u32[]{:S(2)}, u32[]{:S(2)}) collective-permute-start(f32[24,1024]{1,0:T(8,128)S(1)} %get-tuple-element.66), channel_id=1, source_target_pairs={{0,1},{1,0},{2,3},{3,2},{8,9},{9,8},{10,11},{11,10},{16,17},{17,16... | collective-permute-start | bytes 294920 | tf_op jit(solution)/shard_map/ppermute | solution.py:969
  23.1 5.3 %collective-permute-start.8 = (f32[24,1024]{1,0:T(8,128)S(1)}, f32[24,1024]{1,0:T(8,128)S(1)}, u32[]{:S(2)}, u32[]{:S(2)}) collective-permute-start(f32[24,1024]{1,0:T(8,128)S(1)} %get-tuple-element.67), channel_id=1, source_target_pairs={{0,8},{1,2},{2,1},{3,11},{8,0},{9,10},{10,9},{11,3},{16,24},{17,18... | collective-permute-start | bytes 294920 | tf_op jit(solution)/shard_map/ppermute | solution.py:969
  24.3 3.8 %collective-permute-start.9 = (f32[48,128]{1,0:T(8,128)S(1)}, f32[48,128]{1,0:T(8,128)S(1)}, u32[]{:S(2)}, u32[]{:S(2)}) collective-permute-start(f32[48,128]{1,0:T(8,128)S(1)} %shard_map.66.refs_0_), channel_id=1, source_target_pairs={{0,4},{4,0},{1,5},{5,1},{2,6},{6,2},{3,7},{7,3},{8,12},{12,8},{9,1... | collective-permute-start | bytes 73736 | tf_op jit(solution)/shard_map/ppermute | solution.py:959
